TPU v7x, 32 devices: a whole 2x2x4 slice. The times are simulated.
32 devices in a mesh: group: 2 (over y), wide: 4 (over z), sub: 2 (over x), pol: 2 (over core).
Axes of the slice: x: 2, y: 2, z: 4, core: 2. Of those that a mesh axis runs over, the one named last changes fastest.
Arguments:
- voltages: bfloat16 [2, 2048, 4, 2048], P('pol', ('group', 'wide'), 'sub'), parts along dimension 1, may hold values from -6 to 6
- real_weight: bfloat16 [512, 1024, 256], P(('wide', 'sub', 'pol')), may hold values from -0.125 to 0.125
- imaginary_weight: bfloat16 [512, 1024, 256], P(('wide', 'sub', 'pol')), may hold values from -0.125 to 0.125
- delays: int32 [128, 512], P('pol'), may hold values from 0 to 3
Outputs:
- dedispersed: float32 [512, 4, 128], P(('group', 'wide', 'sub'), None, 'pol'), parts along dimension 0
There are 2 independent parts, one for each index of `group`. A program takes and returns all parts, laid end to end along the dimension named above; an argument that names none is the same for every part. Nothing has to cross between parts.
Inputs may be any that keep to these rules, and one draw needn't show every extreme that they name: `delays`: integer sample shifts of each delay trial and channel.
All inputs are finite; a program needn't handle non-finite values.
Results may differ from a plain program's by a relative error of at most 0.012.
Values may be sent and summed in bfloat16 or wider, within the bound.
No kernel may reach another device: no remote copies, remote signals or barrier semaphores. Data moves between devices by JAX's collectives and lax.ppermute only.
A program may use at most 256 MiB of HBM per device.

v0:
```python
import math

import jax
import jax.numpy as jnp
from jax import lax
from jax.sharding import PartitionSpec as P


def dft_table(sample_total, channel_total):
    first_bin = sample_total // 2 - channel_total
    freq_bins = first_bin + jnp.arange(channel_total, dtype=jnp.int32)
    sample_ids = jnp.arange(sample_total, dtype=jnp.int32)
    turns = freq_bins[:, None] * sample_ids[None, :] % sample_total
    angles = turns.astype(jnp.float32) * (2.0 * math.pi / sample_total)
    factor = 1.0 / math.sqrt(sample_total)
    exact = jnp.stack([jnp.cos(angles) * factor, -jnp.sin(angles) * factor], axis=1)
    upper = exact.astype(jnp.bfloat16)
    lower = (exact - upper.astype(jnp.float32)).astype(jnp.bfloat16)
    return jnp.stack([upper, lower], axis=2).reshape(4 * channel_total, sample_total)


def voltage_turn(blocks_in):
    result = lax.all_to_all(blocks_in, ("wide", "sub"), split_axis=0, concat_axis=0, tiled=True)
    return result


def pol_turn(blocks_in):
    return lax.all_to_all(blocks_in, "pol", split_axis=1, concat_axis=1, tiled=True)


def power_turn(blocks_in):
    result = lax.all_to_all(blocks_in, ("wide", "sub"), split_axis=0, concat_axis=0, tiled=True)
    return result


def dedisperse(power_all, delay_rows, frames, channel_total):
    frame_ids = jnp.arange(frames, dtype=jnp.int32)
    scale_step = 2.0 * math.pi / frames
    fwd_angle = (frame_ids[:, None] * frame_ids[None, :] % frames).astype(jnp.float32) * scale_step
    keeper = (frame_ids != 0).astype(jnp.float32)[:, None]
    fwd_cos = jnp.cos(fwd_angle) * keeper
    fwd_sin = jnp.sin(fwd_angle) * keeper
    spec_re = jnp.einsum("kn,cnb->kcb", fwd_cos, power_all, precision=lax.Precision.HIGHEST)
    spec_im = -jnp.einsum("kn,cnb->kcb", fwd_sin, power_all, precision=lax.Precision.HIGHEST)
    block = 8 if frames % 8 == 0 else frames
    beam_local = power_all.shape[2]
    trial_local = delay_rows.shape[0]

    def add_block(step_index, total):
        start = step_index * block
        freq_vals = start + jnp.arange(block, dtype=jnp.int32)
        turns = freq_vals[:, None, None] * delay_rows[None, :, :] % frames
        angles = turns.astype(jnp.float32) * scale_step
        rot_cos = jnp.cos(angles)
        rot_sin = jnp.sin(angles)
        part_re = lax.dynamic_slice_in_dim(spec_re, start, block, 0)
        part_im = lax.dynamic_slice_in_dim(spec_im, start, block, 0)
        sum_re = jnp.einsum(
            "ktc,kcb->ktb", rot_cos, part_re, precision=lax.Precision.HIGHEST
        ) - jnp.einsum("ktc,kcb->ktb", rot_sin, part_im, precision=lax.Precision.HIGHEST)
        sum_im = jnp.einsum(
            "ktc,kcb->ktb", rot_sin, part_re, precision=lax.Precision.HIGHEST
        ) + jnp.einsum("ktc,kcb->ktb", rot_cos, part_im, precision=lax.Precision.HIGHEST)
        back_angle = (freq_vals[:, None] * frame_ids[None, :] % frames).astype(
            jnp.float32
        ) * scale_step
        total = total + jnp.einsum(
            "ktb,kn->bnt", sum_re, jnp.cos(back_angle), precision=lax.Precision.HIGHEST
        )
        return total - jnp.einsum(
            "ktb,kn->bnt", sum_im, jnp.sin(back_angle), precision=lax.Precision.HIGHEST
        )

    initial = jnp.zeros((beam_local, frames, trial_local), jnp.float32)
    total = lax.fori_loop(0, frames // block, add_block, initial)
    return total * (1.0 / (frames * math.sqrt(channel_total)))


def local(voltages, real_weight, imaginary_weight, delays):
    widening_count = lax.axis_size("wide")
    subband_count = lax.axis_size("sub")
    polar_count = lax.axis_size("pol")
    group_list = widening_count * subband_count
    antenna_slice = voltages.shape[1]
    frame_slice = voltages.shape[2]
    sample_total = voltages.shape[3]
    channel_pairs = real_weight.shape[0]
    beam_total = real_weight.shape[2]
    channel_total = channel_pairs * group_list * polar_count
    frames = subband_count * frame_slice
    sample_matrix = voltages[0].reshape(antenna_slice * frame_slice, sample_total)
    dft_weights = dft_table(sample_total, channel_total)
    weighted_product = lax.dot_general(
        dft_weights, sample_matrix, (((1,), (1,)), ((), ())), preferred_element_type=jnp.float32
    )
    spectrum_rows = (
        weighted_product.reshape(channel_total, 2, 2, antenna_slice * frame_slice)
        .sum(axis=2)
        .astype(jnp.bfloat16)
    )
    current_blocks = spectrum_rows.reshape(
        group_list, polar_count, channel_pairs * 2, antenna_slice * frame_slice
    )
    current_blocks = pol_turn(voltage_turn(current_blocks))
    voltage_collection = current_blocks.reshape(
        widening_count, subband_count, polar_count, channel_pairs, 2, antenna_slice, frame_slice
    )
    real_section = real_weight.reshape(channel_pairs, widening_count, antenna_slice, beam_total)
    imaginary_split = imaginary_weight.reshape(
        channel_pairs, widening_count, antenna_slice, beam_total
    )
    form_re = jnp.stack([real_section, -imaginary_split], axis=1)
    form_im = jnp.stack([imaginary_split, real_section], axis=1)
    real_form = jnp.stack([form_re, form_im], axis=4)
    beam_field = jnp.einsum(
        "wsqckaf,ckwaob->cqsfob", voltage_collection, real_form, preferred_element_type=jnp.float32
    )
    power_field = jnp.sum(beam_field * beam_field, axis=(1, 4)).reshape(
        channel_pairs, frames, beam_total
    )
    beam_local = beam_total // group_list
    outgoing = power_field.reshape(channel_pairs, frames, group_list, beam_local)
    outgoing = jnp.transpose(outgoing, (2, 0, 1, 3)).reshape(
        group_list, channel_pairs * frames * beam_local
    )
    arrived = power_turn(outgoing)
    both_pols = lax.all_gather(
        arrived.reshape(group_list, 1, channel_pairs * frames * beam_local),
        "pol",
        axis=1,
        tiled=True,
    )
    power_all = both_pols.reshape(channel_total, frames, beam_local)
    return dedisperse(power_all, delays, frames, channel_total)


def solution(mesh):
    placed = (
        P("pol", ("group", "wide"), "sub", None),
        P(("wide", "sub", "pol"), None, None),
        P(("wide", "sub", "pol"), None, None),
        P("pol", None),
    )
    return jax.shard_map(
        local,
        mesh=mesh,
        in_specs=placed,
        out_specs=P(("group", "wide", "sub"), None, "pol"),
        check_vma=False,
    )
```

profile of v0, /device:TPU:0, one launch (start us, length us, event | category | flops | bytes accessed | tf_op | source)
XLA Modules:
  0.0 323.3 jit_solution(8248861408916826605)
XLA Ops:
  0.0 16.9 %multiply_bitcast_fusion.1 = (f32[512,1,1,2048]{3,0,2,1:T(8,128)S(1)}, f32[512,1,1,2048]{3,0,2,1:T(8,128)S(1)}) fusion(s32[512]{0:T(512)S(1)} %iota_add_fusion), kind=kLoop, calls=%fused_computation.21 | loop fusion | flops 17825792 | bytes 8390656 | tf_op jit(solution)/shard_map/stack | solution.py:16
  16.9 2.4 subtract_convert_fusion
  19.3 0.0 copy-start
  19.3 2.7 fusion.8
  22.0 0.0 copy-done
  22.0 2.2 reshape.211
  24.2 8.7 %fusion.16 = bf16[512,2,512]{2,0,1:T(8,128)(2,1)S(1)} fusion(bf16[512,2048,1,1]{1,0,2,3:T(8,128)(2,1)} %reshape.211, bf16[512,2,1,2048]{3,0,2,1:T(8,128)(2,1)} %subtract_convert_fusion, bf16[512,2,1,2048]{3,0,2,1:T(8,128)(2,1)} %fusion.8), kind=kOutput, calls=%fused_computation.26 | convolution fusion | flops 4299685888 | bytes 11534336 | tf_op jit(solution)/shard_map/dot_general | solution.py:93
  32.9 1.1 copy.55
  34.0 1.2 convert_element_type.107
  35.2 7.3 %all-to-all-start = ((bf16[8,2,64,512]{3,2,1,0:T(8,128)(2,1)}), bf16[8,2,64,512]{3,2,1,0:T(8,128)(2,1)S(1)}, u32[]{:S(2)}, u32[]{:S(2)}) async-start(bf16[8,2,64,512]{3,2,1,0:T(8,128)(2,1)} %convert_element_type.107), calls=%async_computation | async-start | bytes 2097152 | tf_op jit(solution)/shard_map/all_to_all | solution.py:23
  42.5 14.7 %neg.32 = bf16[32,1,4,256,256]{4,3,2,1,0:T(8,128)(2,1)} negate(bf16[32,1,4,256,256]{4,3,2,1,0:T(8,128)(2,1)} %bitcast.74) | non-fusion elementwise | flops 8388608 | bytes 33554432 | tf_op jit(solution)/shard_map/neg | solution.py:112
  57.2 44.1 %maximum_bitcast_fusion.2 = (bf16[32,2,4,256,1,256]{5,3,2,1,4,0:T(8,128)(2,1)}, bf16[32,2,4,256,1,256]{5,3,2,1,4,0:T(8,128)(2,1)}) fusion(bf16[32,1,4,256,256]{4,3,2,1,0:T(8,128)(2,1)} %neg.32, bf16[32,1,4,256,256]{4,3,2,1,0:T(8,128)(2,1)} %bitcast.76, bf16[32,1,4,256,256]{4,3,2,1,0:T(8,128)(2,1)} %bitcast.75), kind=kLoop, calls=%fused_computation.5 | loop fusion | flops 33554432 | bytes 117440512 | tf_op jit(solution)/shard_map/stack | solution.py:114
  101.3 0.0 all-to-all-done
  101.3 0.1 copy.56
  101.4 4.6 %all_to_all.20 = bf16[8,2,64,512]{3,2,0,1:T(8,128)(2,1)S(1)} all-to-all(bf16[8,2,64,512]{3,2,0,1:T(8,128)(2,1)S(1)} %copy.56), channel_id=1, replica_groups=mesh['group'=2,'wide'=4,'sub'=2,'pol'=2] {'pol'}, dimensions={1} | all-to-all | bytes 2097152 | tf_op jit(solution)/shard_map/all_to_all | solution.py:28
  106.0 145.5 %reshape.220 = bf16[4,2,2,32,2,256,2]{6,5,4,3,1,0,2:T(8,128)(2,1)} reshape(bf16[8,2,64,512]{3,2,0,1:T(8,128)(2,1)S(1)} %all_to_all.20) | data formatting | bytes 2097152 | tf_op jit(solution)/shard_map/reshape | solution.py:105
  251.5 42.6 %fusion.27 = f32[32,256,2,2]{1,3,2,0:T(2,128)S(1)} fusion(bf16[32,2,4,256,1,256]{5,3,2,1,4,0:T(8,128)(2,1)} %get-tuple-element.18, bf16[32,2,4,256,1,256]{5,3,2,1,4,0:T(8,128)(2,1)} %get-tuple-element.17, bf16[4,2,2,32,2,256,2]{6,5,4,3,1,0,2:T(8,128)(2,1)} %reshape.220), kind=kOutput, calls=%fused_computation.29 | convolution fusion | flops 671318016 | bytes 68288512 | tf_op jit(solution)/shard_map/wsqckaf,ckwaob->cqsfob/dot_general | solution.py:115
  294.1 0.0 copy-start.1
  294.2 0.2 reshape_reshape.3
  294.3 0.3 copy.60
  294.7 1.0 all_to_all.16
  295.7 6.0 %all-to-all-start.2 = ((f32[8,1,4096]{2,1,0:T(1,128)}), f32[8,1,4096]{2,1,0:T(1,128)S(1)}, u32[]{:S(2)}, u32[]{:S(2)}) async-start(f32[8,1,4096]{2,1,0:T(1,128)} %all_to_all.16), calls=%async_computation.2 | async-start | bytes 262144 | tf_op jit(solution)/shard_map/all_to_all | solution.py:32
  301.7 7.3 %all-to-all-done.2 = f32[8,1,4096]{2,1,0:T(1,128)S(1)} async-done(((f32[8,1,4096]{2,1,0:T(1,128)}), f32[8,1,4096]{2,1,0:T(1,128)S(1)}, u32[]{:S(2)}, u32[]{:S(2)}) %all-to-all-start.2) | async-done | bytes 131104 | tf_op jit(solution)/shard_map/all_to_all | solution.py:32
  309.0 0.1 copy.62
  309.1 2.2 all_gather.3
  311.3 0.2 copy.63
  311.5 0.6 reshape.210
  312.1 0.4 copy.65
  312.5 0.7 fusion.57
  313.2 0.7 fusion.55
  314.0 0.0 copy-done.1
  314.0 2.0 fusion.41
  316.0 2.0 fusion.43
  318.0 2.0 convolution_subtract_fusion.1
  320.0 0.3 fusion.49
  320.3 2.0 convolution_add_fusion
  322.3 0.9 fusion.31
  (3 shorter events, 0.0 us)
Async XLA Ops:
  19.3 2.7 copy-start
  35.2 66.1 %all-to-all-start = ((bf16[8,2,64,512]{3,2,1,0:T(8,128)(2,1)}), bf16[8,2,64,512]{3,2,1,0:T(8,128)(2,1)S(1)}, u32[]{:S(2)}, u32[]{:S(2)}) async-start(bf16[8,2,64,512]{3,2,1,0:T(8,128)(2,1)} %convert_element_type.107), calls=%async_computation | async-start | bytes 2097152 | tf_op jit(solution)/shard_map/all_to_all | solution.py:23
  294.1 19.9 %copy-start.1 = (s32[64,512]{1,0:T(8,128)S(1)}, s32[64,512]{1,0:T(8,128)}, u32[]{:S(2)}) copy-start(s32[64,512]{1,0:T(8,128)} %param.7) | copy-start | bytes 393220
  295.7 13.3 %all-to-all-start.2 = ((f32[8,1,4096]{2,1,0:T(1,128)}), f32[8,1,4096]{2,1,0:T(1,128)S(1)}, u32[]{:S(2)}, u32[]{:S(2)}) async-start(f32[8,1,4096]{2,1,0:T(1,128)} %all_to_all.16), calls=%async_computation.2 | async-start | bytes 262144 | tf_op jit(solution)/shard_map/all_to_all | solution.py:32
where the time goes:
time: 324 us; the launch traced here: 323 us
  local copies, waits for them, and re-layouts  153 us (47%)
  other arithmetic  80.8 us (25%)
  matrix products  62 us (19%)
  starting transfers between devices  13.2 us (4%)
  waiting for transfers between devices  7.34 us (2%)
  blocking collectives  6.79 us (2%)
    reshape x1, local copies, waits for them, and re-layouts, local(): current_blocks.reshape(widening_count, subband_count, polar_count, channe...  146 us
    another operation x1, other arithmetic, local(): real_form = jnp.stack([form_re, form_im], axis=4)  44.1 us
    dot_general x1, matrix products, local(): jnp.einsum('wsqckaf,ckwaob->cqsfob', voltage_collection, real_form, prefe...  42.6 us
    another operation x1, other arithmetic, dft_table(): jnp.stack([jnp.cos(angles) * factor, -jnp.sin(angles) * factor], axis=1)  16.9 us
    neg x1, other arithmetic, local(): form_re = jnp.stack([real_section, -imaginary_split], axis=1)  14.7 us
    dot_general x1, matrix products, local(): lax.dot_general(dft_weights, sample_matrix, (((1,), (1,)), ((), ())), pre...  8.67 us
    all_to_all x1, waiting for transfers between devices, power_turn(): lax.all_to_all(blocks_in, ('wide', 'sub'), split_axis=0, concat_axis=0, t...  7.34 us
    all_to_all x1, starting transfers between devices, voltage_turn(): lax.all_to_all(blocks_in, ('wide', 'sub'), split_axis=0, concat_axis=0, t...  7.25 us
  transfers between devices with their start and end apart: 2, of which 1 were waited for; matrix products, arithmetic and copies ran while one was open for 18% of the time, Pallas kernels for 0%

commit v1 on v0

v1 whole, which is shorter than its diff:
```python
import functools
import math

import jax
import jax.numpy as jnp
import ml_dtypes
import numpy as np
from jax import lax
from jax.experimental import pallas as pl
from jax.experimental.pallas import tpu as pltpu
from jax.sharding import PartitionSpec as P

OWNERS = ("wide", "sub", "pol")
ROWS = 16


def dft_parts(samples, channels):
    first = samples // 2 - channels
    bins = first + np.arange(channels, dtype=np.int64)
    turns = bins[:, None] * np.arange(samples, dtype=np.int64)[None, :] % samples
    angles = turns * (2.0 * math.pi / samples)
    exact = np.stack([np.cos(angles), -np.sin(angles)], axis=1) / math.sqrt(samples)
    upper = exact.astype(ml_dtypes.bfloat16)
    lower = (exact - upper.astype(np.float64)).astype(ml_dtypes.bfloat16)
    return upper, lower


def dft_kernel(table_ref, volt_ref, out_ref):
    rows = out_ref.shape[0] * out_ref.shape[2]
    for frame in range(volt_ref.shape[0]):
        both = lax.dot_general(
            table_ref[0],
            volt_ref[frame],
            (((1,), (1,)), ((), ())),
            preferred_element_type=jnp.float32,
        )
        spectrum = (both[:rows] + both[rows:]).astype(jnp.bfloat16)
        out_ref[:, frame] = spectrum.reshape(out_ref.shape[0], out_ref.shape[2], -1)


def spectra(volts, owners, channels):
    frames, antennas, samples = volts.shape
    own = channels // owners
    upper, lower = dft_parts(samples, channels)
    group = ROWS // 2

    def order(part):
        part = part.reshape(owners, own // group, group, 2, samples)
        return part.transpose(0, 1, 3, 2, 4).reshape(owners, 2 * own, samples)

    upper, lower = order(upper), order(lower)
    step = max(1, min(owners, 256 // (2 * own)))
    while owners % step:
        step -= 1
    steps = owners // step
    table = np.concatenate(
        [
            upper.reshape(steps, step * 2 * own, samples),
            lower.reshape(steps, step * 2 * own, samples),
        ],
        axis=1,
    )
    return pl.pallas_call(
        dft_kernel,
        grid=(steps,),
        in_specs=[
            pl.BlockSpec((1,) + table.shape[1:], lambda i: (i, 0, 0)),
            pl.BlockSpec(volts.shape, lambda i: (0, 0, 0)),
        ],
        out_specs=pl.BlockSpec((step, frames, 2 * own, antennas), lambda i: (i, 0, 0, 0)),
        out_shape=jax.ShapeDtypeStruct((owners, frames, 2 * own, antennas), jnp.bfloat16),
        compiler_params=pltpu.CompilerParams(vmem_limit_bytes=48 * 2**20),
        name="spectra",
    )(jnp.asarray(table), volts)


def beam_kernel(sources, wides, order_ref, x_ref, re_ref, im_ref, out_ref, sorted_ref, power_ref):
    group = re_ref.shape[0]
    per_wide = sources // wides
    frames = x_ref.shape[1]
    for wide in range(wides):
        block = x_ref[pl.ds(wide * per_wide, per_wide)]
        block = block.reshape(per_wide * frames * ROWS, block.shape[-1])
        ordered = jnp.dot(order_ref[...], block, preferred_element_type=jnp.float32)
        sorted_ref[:, wide * block.shape[-1] : (wide + 1) * block.shape[-1]] = ordered.astype(
            jnp.bfloat16
        )
    half = per_wide * frames
    total = half // 2
    for channel in range(group):
        rows = sorted_ref[channel * 2 * half : (channel + 1) * 2 * half, :]
        by_re = jnp.dot(rows, re_ref[channel], preferred_element_type=jnp.float32)
        by_im = jnp.dot(rows, im_ref[channel], preferred_element_type=jnp.float32)
        beam_re = by_re[:half] - by_im[half:]
        beam_im = by_im[:half] + by_re[half:]
        power = beam_re * beam_re + beam_im * beam_im
        power = power[:total] + power[total:]
        power = power - jnp.mean(power, axis=0, keepdims=True)
        power_ref[:, channel, :] = power
    targets = out_ref.shape[0]
    beams = power_ref.shape[2] // targets
    for target in range(targets):
        block = jnp.concatenate(
            [power_ref[f, :, target * beams : (target + 1) * beams] for f in range(total)], axis=1
        )
        out_ref[target] = block.astype(jnp.bfloat16)


def beam_power(x, real_weight, imaginary_weight, wides, subs, pols):
    sources, frames, _, antennas = x.shape
    channels, antenna_total, beams = real_weight.shape
    group = ROWS // 2
    per_wide = sources // wides
    count = per_wide * frames * ROWS
    place = np.arange(count).reshape(subs, pols, frames, 2, group).transpose(4, 3, 1, 0, 2).reshape(-1)
    order = np.zeros((count, count), np.float32)
    order[np.arange(count), place] = 1.0
    targets = wides * subs
    width = subs * frames * (beams // targets)
    return pl.pallas_call(
        functools.partial(beam_kernel, sources, wides),
        grid=(channels // group,),
        in_specs=[
            pl.BlockSpec((count, count), lambda i: (0, 0)),
            pl.BlockSpec((sources, frames, ROWS, antennas), lambda i: (0, 0, i, 0)),
            pl.BlockSpec((group, antenna_total, beams), lambda i: (i, 0, 0)),
            pl.BlockSpec((group, antenna_total, beams), lambda i: (i, 0, 0)),
        ],
        out_specs=pl.BlockSpec((targets, group, width), lambda i: (0, i, 0)),
        out_shape=jax.ShapeDtypeStruct((targets, channels, width), jnp.bfloat16),
        scratch_shapes=[
            pltpu.VMEM((count, antenna_total), jnp.bfloat16),
            pltpu.VMEM((subs * frames, group, beams), jnp.float32),
        ],
        compiler_params=pltpu.CompilerParams(vmem_limit_bytes=48 * 2**20),
        name="beam_power",
    )(jnp.asarray(order, jnp.bfloat16), x, real_weight, imaginary_weight)


def shift_kernel(scale, power_ref, delay_ref, out_ref):
    beams, frames, _ = out_ref.shape
    delays = delay_ref[...]
    power = power_ref[...]
    sums = [None] * frames
    for delay in range(frames):
        chosen = (delays == delay).astype(jnp.float32).astype(jnp.bfloat16)
        picked = lax.dot_general(
            power, chosen, (((0,), (1,)), ((), ())), preferred_element_type=jnp.float32
        )
        for frame in range(frames):
            row = (frame + delay) % frames * beams
            term = picked[row : row + beams]
            sums[frame] = term if sums[frame] is None else sums[frame] + term
    for frame in range(frames):
        out_ref[:, frame, :] = sums[frame] * scale


def shift_and_add(power, delays, frames):
    channels, width = power.shape
    beams = width // frames
    return pl.pallas_call(
        functools.partial(shift_kernel, 1.0 / math.sqrt(channels)),
        out_shape=jax.ShapeDtypeStruct((beams, frames, delays.shape[0]), jnp.float32),
        name="shift_and_add",
    )(power, delays % frames)


def plain_spectra(volts, owners, channels):
    frames, antennas, samples = volts.shape
    upper, lower = (jnp.asarray(part) for part in dft_parts(samples, channels))
    x = sum(
        jnp.einsum("krn,fan->kfra", part, volts, preferred_element_type=jnp.float32)
        for part in (upper, lower)
    )
    x = x.astype(jnp.bfloat16).reshape(owners, channels // owners, frames, 2, antennas)
    return x


def plain_beam_power(x, real_weight, imaginary_weight, wides, subs, pols):
    _, own, frames, _, antennas = x.shape
    beams = real_weight.shape[2]
    x = x.reshape(wides, subs, pols, own, frames, 2, antennas)
    x = x.transpose(3, 5, 2, 1, 4, 0, 6).reshape(own, 2, pols * subs * frames, wides * antennas)
    by_re, by_im = (
        jnp.einsum("crfa,cab->rcfb", x, weight, preferred_element_type=jnp.float32)
        for weight in (real_weight, imaginary_weight)
    )
    power = (by_re[0] - by_im[1]) ** 2 + (by_im[0] + by_re[1]) ** 2
    power = power.reshape(own, pols, subs * frames, beams).sum(axis=1)
    power = power - jnp.mean(power, axis=1, keepdims=True)
    targets = wides * subs
    power = power.reshape(own, subs * frames, targets, beams // targets)
    return power.transpose(2, 0, 1, 3).reshape(targets, own, -1).astype(jnp.bfloat16)


def plain_shift_and_add(power, delays, frames):
    channels = power.shape[0]
    power = power.reshape(channels, frames, -1)
    chosen = (delays[None] % frames == jnp.arange(frames)[:, None, None]).astype(jnp.bfloat16)
    picked = jnp.einsum("dtc,cfb->dbft", chosen, power, preferred_element_type=jnp.float32)
    moved = sum(jnp.roll(picked[delay], -delay, axis=1) for delay in range(frames))
    return moved * (1.0 / math.sqrt(channels))


def local(voltages, real_weight, imaginary_weight, delays):
    wides, subs, pols = (lax.axis_size(name) for name in OWNERS)
    owners = wides * subs * pols
    own, _, beams = real_weight.shape
    frames = subs * voltages.shape[2]
    volts = jnp.transpose(voltages[0], (1, 0, 2))
    tiled = (
        own % ROWS == 0
        and voltages.shape[1] % 128 == 0
        and (beams // (wides * subs)) % 32 == 0
        and frames == 4
        and pols == 2
    )
    form = spectra if tiled else plain_spectra
    beamform = beam_power if tiled else plain_beam_power
    finish = shift_and_add if tiled else plain_shift_and_add
    x = form(volts, owners, own * owners)
    x = lax.all_to_all(x, OWNERS, split_axis=0, concat_axis=0, tiled=True)
    power = beamform(x, real_weight, imaginary_weight, wides, subs, pols)
    width = power.shape[2]
    power = jnp.broadcast_to(power[:, None], (wides * subs, pols, own, width))
    power = power.reshape(owners, own, width)
    power = lax.all_to_all(power, OWNERS, split_axis=0, concat_axis=0, tiled=True)
    return finish(power.reshape(owners * own, width), delays, frames)


def solution(mesh):
    placed = (
        P("pol", ("group", "wide"), "sub", None),
        P(OWNERS, None, None),
        P(OWNERS, None, None),
        P("pol", None),
    )
    return jax.shard_map(
        local,
        mesh=mesh,
        in_specs=placed,
        out_specs=P(("group", "wide", "sub"), None, "pol"),
        check_vma=False,
    )
```

time: 324 us -> 70.6 us (0.22)
  local copies, waits for them, and re-layouts: 153 us -> 3.8 us
  other arithmetic: 80.8 us -> 0.7 us
  matrix products: 62 us -> 0 us
  blocking collectives: 6.79 us -> 32 us
  Pallas kernels: 0 us -> 21.5 us
  starting transfers between devices: 13.2 us -> 4.99 us
    reshape x3 -> x0, local copies, waits for them, and re-layouts: 146 us -> none  [the longest x1 146 us: local(): current_blocks.reshape(widening_count, subband_count, polar_count, channe...]
    dot_general x10 -> x0, matrix products: 62 us -> none  [the longest x1 42.6 us: local(): jnp.einsum('wsqckaf,ckwaob->cqsfob', voltage_collection, real_form, prefe...]
    another operation x2 -> x0, other arithmetic: 61 us -> none  [the longest x1 44.1 us: local(): real_form = jnp.stack([form_re, form_im], axis=4)]
    all_to_all x1, blocking collectives: 4.58 us -> 32 us  [local(): x = lax.all_to_all(x, OWNERS, split_axis=0, concat_axis=0, tiled=True)]
    pallas_call x0 -> x3, Pallas kernels: none -> 21.5 us  [the longest x1 12.5 us: beam_power(): pl.pallas_call(functools.partial(beam_kernel, sources, wides), grid=(chan...]
    neg x1 -> x0, other arithmetic: 14.7 us -> none  [local(): form_re = jnp.stack([real_section, -imaginary_split], axis=1)]
    all_to_all x2 -> x1, starting transfers between devices: 13.2 us -> 4.99 us  [local(): lax.all_to_all(power, OWNERS, split_axis=0, concat_axis=0, tiled=True)]
    convert_element_type x3 -> x0, other arithmetic: 5.16 us -> none  [the longest x1 2.71 us: dft_table(): upper = exact.astype(jnp.bfloat16)]
  transfers between devices with their start and end apart: 2 -> 1, of which waited for: 1 -> 1; matrix products, arithmetic and copies ran while one was open for 18% -> 1% of each run, Pallas kernels for 0% -> 0%
where the time goes in v1:
time: 70.6 us; the launch traced here: 70.3 us
  blocking collectives  32 us (45%)
  Pallas kernels  21.5 us (30%)
  waiting for transfers between devices  7.22 us (10%)
  starting transfers between devices  4.99 us (7%)
  local copies, waits for them, and re-layouts  3.8 us (5%)
    all_to_all x1, blocking collectives, local(): x = lax.all_to_all(x, OWNERS, split_axis=0, concat_axis=0, tiled=True)  32 us
    pallas_call x1, Pallas kernels, beam_power(): pl.pallas_call(functools.partial(beam_kernel, sources, wides), grid=(chan...  12.5 us
    all_to_all x1, waiting for transfers between devices, local(): lax.all_to_all(power, OWNERS, split_axis=0, concat_axis=0, tiled=True)  7.22 us
    pallas_call x1, Pallas kernels, spectra(): pl.pallas_call(dft_kernel, grid=(steps,), in_specs=[pl.BlockSpec((1,) + t...  7.14 us
    all_to_all x1, starting transfers between devices, local(): lax.all_to_all(power, OWNERS, split_axis=0, concat_axis=0, tiled=True)  4.99 us
    unnamed x7, local copies, waits for them, and re-layouts  3.13 us
    pallas_call x1, Pallas kernels, shift_and_add(): pl.pallas_call(functools.partial(shift_kernel, 1.0 / math.sqrt(channels))...  1.94 us
  transfers between devices with their start and end apart: 1, of which 1 were waited for; matrix products, arithmetic and copies ran while one was open for 1% of the time, Pallas kernels for 0%

profile of v1, /device:TPU:0, one launch (start us, length us, event | category | flops | bytes accessed | tf_op | source)
XLA Modules:
  0.0 70.3 jit_solution(10708036825603043305)
XLA Ops:
  0.0 0.0 copy-start
  0.0 2.5 %copy.9 = bf16[1,256,2,2048]{3,1,2,0:T(8,128)(2,1)S(1)} copy(bf16[1,256,2,2048]{3,2,1,0:T(2,128)(2,1)} %param.6) | data formatting | bytes 4194304 | tf_op args[0]
  2.5 7.1 %spectra.1 = bf16[16,2,64,256]{3,2,1,0:T(8,128)(2,1)S(1)} custom-call(bf16[4,512,2048]{2,1,0:T(8,128)(2,1)} %constant.19.clone.table_ref, bf16[2,256,2048]{2,1,0:T(8,128)(2,1)S(1)} %bitcast.7), custom_call_target="tpu_custom_call" | custom-call | tf_op jit(solution)/shard_map/spectra/pallas_call | solution.py:63
  9.6 32.0 %all_to_all.10.x_ref = bf16[16,2,64,256]{3,2,1,0:T(8,128)(2,1)S(1)} all-to-all(bf16[16,2,64,256]{3,2,1,0:T(8,128)(2,1)S(1)} %spectra.1), channel_id=1, replica_groups=mesh['group'=2,'wide'=4,'sub'=2,'pol'=2] {'wide','sub','pol'}, dimensions={0} | all-to-all | bytes 2097152 | tf_op jit(solution)/shard_map/all_to_all | solution.py:222
  41.6 0.0 copy-done
  41.6 0.0 copy-start.2
  41.6 12.5 %beam_power.1 = bf16[8,32,128]{2,1,0:T(8,128)(2,1)S(1)} custom-call(bf16[128,128]{1,0:T(8,128)(2,1)S(1)} %copy-done, bf16[16,2,64,256]{3,2,1,0:T(8,128)(2,1)S(1)} %all_to_all.10.x_ref, bf16[32,1024,256]{2,1,0:T(8,128)(2,1)} %re_ref.1, bf16[32,1024,256]{2,1,0:T(8,128)(2,1)} %im_ref.1), custom_call_target="tpu_custom_call" | custom-call | tf_op jit(solution)/shard_map/beam_power/pallas_call | solution.py:120
  54.1 0.7 broadcast_in_dim.2
  54.8 5.0 %all-to-all-start.1 = ((bf16[16,32,128]{2,1,0:T(8,128)(2,1)}), bf16[16,32,128]{2,1,0:T(8,128)(2,1)S(1)}, u32[]{:S(2)}, u32[]{:S(2)}) async-start(bf16[16,32,128]{2,1,0:T(8,128)(2,1)} %bitcast.2), calls=%async_computation.1 | async-start | bytes 262144 | tf_op jit(solution)/shard_map/all_to_all | solution.py:227
  59.8 0.0 copy-done.2
  59.8 0.7 add_select_fusion.delay_ref
  60.5 7.2 %all-to-all-done.1 = bf16[16,32,128]{2,1,0:T(8,128)(2,1)S(1)} async-done(((bf16[16,32,128]{2,1,0:T(8,128)(2,1)}), bf16[16,32,128]{2,1,0:T(8,128)(2,1)S(1)}, u32[]{:S(2)}, u32[]{:S(2)}) %all-to-all-start.1) | async-done | bytes 131104 | tf_op jit(solution)/shard_map/all_to_all | solution.py:227
  67.7 0.0 copy-start.1
  67.7 0.6 copy-done.1
  68.4 1.9 %shift_and_add.1 = f32[32,4,64]{2,1,0:T(4,128)} custom-call(bf16[512,128]{1,0:T(8,128)(2,1)} %bitcast.8, s32[64,512]{1,0:T(8,128)} %add_select_fusion.delay_ref), custom_call_target="tpu_custom_call" | custom-call | tf_op jit(solution)/shard_map/shift_and_add/pallas_call | solution.py:161
Async XLA Ops:
  0.0 41.6 %copy-start = (bf16[128,128]{1,0:T(8,128)(2,1)S(1)}, bf16[128,128]{1,0:T(8,128)(2,1)}, u32[]{:S(2)}) copy-start(bf16[128,128]{1,0:T(8,128)(2,1)} %constant.20.clone.order_ref) | copy-start | bytes 98308
  41.6 18.1 %copy-start.2 = (s32[64,512]{1,0:T(8,128)S(1)}, s32[64,512]{1,0:T(8,128)}, u32[]{:S(2)}) copy-start(s32[64,512]{1,0:T(8,128)} %param.9) | copy-start | bytes 393220
  54.8 12.9 %all-to-all-start.1 = ((bf16[16,32,128]{2,1,0:T(8,128)(2,1)}), bf16[16,32,128]{2,1,0:T(8,128)(2,1)S(1)}, u32[]{:S(2)}, u32[]{:S(2)}) async-start(bf16[16,32,128]{2,1,0:T(8,128)(2,1)} %bitcast.2), calls=%async_computation.1 | async-start | bytes 262144 | tf_op jit(solution)/shard_map/all_to_all | solution.py:227
  67.7 0.7 copy-start.1

commit v2 on v1

v2 whole, which is shorter than its diff:
```python
import functools
import math

import jax
import jax.numpy as jnp
import ml_dtypes
import numpy as np
from jax import lax
from jax.experimental import pallas as pl
from jax.experimental.pallas import tpu as pltpu
from jax.sharding import PartitionSpec as P

OWNERS = ("wide", "sub", "pol")
ROWS = 16


def dft_parts(samples, channels):
    first = samples // 2 - channels
    bins = first + np.arange(channels, dtype=np.int64)
    turns = bins[:, None] * np.arange(samples, dtype=np.int64)[None, :] % samples
    angles = turns * (2.0 * math.pi / samples)
    exact = np.stack([np.cos(angles), -np.sin(angles)], axis=1) / math.sqrt(samples)
    upper = exact.astype(ml_dtypes.bfloat16)
    lower = (exact - upper.astype(np.float64)).astype(ml_dtypes.bfloat16)
    return upper, lower


def dft_kernel(table_ref, volt_ref, out_ref, part_ref, sem):
    steps, rows = part_ref.shape[:2]
    frames = volt_ref.shape[0]
    owners = out_ref.shape[0] // steps
    copies = [
        pltpu.make_async_copy(table_ref.at[step], part_ref.at[step], sem.at[step])
        for step in range(steps)
    ]
    for copy in copies:
        copy.start()
    for step, copy in enumerate(copies):
        copy.wait()
        for frame in range(frames):
            both = lax.dot_general(
                part_ref[step],
                volt_ref[frame],
                (((1,), (1,)), ((), ())),
                preferred_element_type=jnp.float32,
            )
            spectrum = (both[: rows // 2] + both[rows // 2 :]).astype(jnp.bfloat16)
            out_ref[step * owners : (step + 1) * owners, frame] = spectrum.reshape(
                owners, -1, spectrum.shape[-1]
            )


def spectra(volts, owners, channels):
    frames, antennas, samples = volts.shape
    own = channels // owners
    group = ROWS // 2
    step = max(1, min(owners, 256 // (2 * own)))
    while owners % step:
        step -= 1
    steps = owners // step

    def order(part):
        part = part.reshape(steps, step, own // group, group, 2, samples)
        return part.transpose(0, 1, 2, 4, 3, 5).reshape(steps, -1, samples)

    table = np.concatenate([order(part) for part in dft_parts(samples, channels)], axis=1)
    vmem = pl.BlockSpec(memory_space=pltpu.VMEM)
    return pl.pallas_call(
        dft_kernel,
        in_specs=[pl.BlockSpec(memory_space=pltpu.HBM), vmem],
        out_specs=vmem,
        out_shape=jax.ShapeDtypeStruct((owners, frames, 2 * own, antennas), jnp.bfloat16),
        scratch_shapes=[
            pltpu.VMEM(table.shape, jnp.bfloat16),
            pltpu.SemaphoreType.DMA((steps,)),
        ],
        compiler_params=pltpu.CompilerParams(vmem_limit_bytes=14 * 2**20),
        name="spectra",
    )(
        pltpu.with_memory_space_constraint(jnp.asarray(table), pltpu.HBM),
        pltpu.with_memory_space_constraint(volts, pltpu.VMEM),
    )


def beam_kernel(wides, order_ref, x_ref, re_ref, im_ref, out_ref, held_ref, sorted_ref, power_ref, sem):
    sources, frames, rows, antennas = x_ref.shape
    per_wide = sources // wides
    half = per_wide * frames
    total = half // 2
    group = ROWS // 2

    def fetch(own):
        return pltpu.make_async_copy(im_ref.at[own], held_ref.at[own], sem.at[own])

    for own in range(rows // 2):
        fetch(own).start()

    def one_group(step, carry):
        start = pl.multiple_of(step * ROWS, ROWS)
        for wide in range(wides):
            block = x_ref[pl.ds(wide * per_wide, per_wide), :, pl.ds(start, ROWS), :]
            block = block.reshape(half * ROWS, antennas)
            ordered = jnp.dot(order_ref[...], block, preferred_element_type=jnp.float32)
            sorted_ref[:, wide * antennas : (wide + 1) * antennas] = ordered.astype(jnp.bfloat16)
        for channel in range(group):
            fetch(step * group + channel).wait()
        for channel in range(group):
            own = step * group + channel
            lines = sorted_ref[channel * 2 * half : (channel + 1) * 2 * half, :]
            by_re = jnp.dot(lines, re_ref[own], preferred_element_type=jnp.float32)
            by_im = jnp.dot(lines, held_ref[own], preferred_element_type=jnp.float32)
            beam_re = by_re[:half] - by_im[half:]
            beam_im = by_im[:half] + by_re[half:]
            power = beam_re * beam_re + beam_im * beam_im
            power = power[:total] + power[total:]
            power = power - jnp.mean(power, axis=0, keepdims=True)
            power_ref[step, :, channel, :] = power
        return carry

    steps = rows // ROWS
    lax.fori_loop(0, steps, one_group, 0)
    targets, copies = out_ref.shape[:2]
    beams = power_ref.shape[3] // targets
    for target in range(targets):
        block = jnp.concatenate(
            [
                power_ref[:, f, :, target * beams : (target + 1) * beams].reshape(-1, beams)
                for f in range(total)
            ],
            axis=1,
        ).astype(jnp.bfloat16)
        for copy in range(copies):
            out_ref[target, copy] = block


def beam_power(x, real_weight, imaginary_weight, wides, subs, pols):
    sources, frames, _, _ = x.shape
    channels, antenna_total, beams = real_weight.shape
    group = ROWS // 2
    half = sources // wides * frames
    count = half * ROWS
    place = np.arange(count).reshape(subs, pols, frames, 2, group).transpose(4, 3, 1, 0, 2).reshape(-1)
    order = np.zeros((count, count), np.float32)
    order[np.arange(count), place] = 1.0
    targets = wides * subs
    width = subs * frames * (beams // targets)
    vmem = pl.BlockSpec(memory_space=pltpu.VMEM)
    return pl.pallas_call(
        functools.partial(beam_kernel, wides),
        in_specs=[vmem] * 3 + [pl.BlockSpec(memory_space=pltpu.HBM)],
        out_specs=vmem,
        out_shape=jax.ShapeDtypeStruct((targets, pols, channels, width), jnp.bfloat16),
        scratch_shapes=[
            pltpu.VMEM(imaginary_weight.shape, jnp.bfloat16),
            pltpu.VMEM((count, antenna_total), jnp.bfloat16),
            pltpu.VMEM((channels // group, subs * frames, group, beams), jnp.float32),
            pltpu.SemaphoreType.DMA((channels,)),
        ],
        compiler_params=pltpu.CompilerParams(vmem_limit_bytes=24 * 2**20),
        name="beam_power",
    )(
        jnp.asarray(order, jnp.bfloat16),
        x,
        pltpu.with_memory_space_constraint(real_weight, pltpu.VMEM),
        pltpu.with_memory_space_constraint(imaginary_weight, pltpu.HBM),
    )


def shift_kernel(scale, power_ref, delay_ref, out_ref):
    beams, frames, _ = out_ref.shape
    delays = lax.rem(delay_ref[...], frames)
    power = power_ref[...]
    sums = [None] * frames
    for delay in range(frames):
        chosen = (delays == delay).astype(jnp.float32).astype(jnp.bfloat16)
        picked = lax.dot_general(
            power, chosen, (((0,), (1,)), ((), ())), preferred_element_type=jnp.float32
        )
        for frame in range(frames):
            row = (frame + delay) % frames * beams
            term = picked[row : row + beams]
            sums[frame] = term if sums[frame] is None else sums[frame] + term
    for frame in range(frames):
        out_ref[:, frame, :] = sums[frame] * scale


def shift_and_add(power, delays, frames):
    channels, width = power.shape
    beams = width // frames
    return pl.pallas_call(
        functools.partial(shift_kernel, 1.0 / math.sqrt(channels)),
        out_shape=jax.ShapeDtypeStruct((beams, frames, delays.shape[0]), jnp.float32),
        compiler_params=pltpu.CompilerParams(vmem_limit_bytes=8 * 2**20),
        name="shift_and_add",
    )(power, delays)


def plain_spectra(volts, owners, channels):
    frames, antennas, samples = volts.shape
    upper, lower = (jnp.asarray(part) for part in dft_parts(samples, channels))
    x = sum(
        jnp.einsum("krn,fan->kfra", part, volts, preferred_element_type=jnp.float32)
        for part in (upper, lower)
    )
    x = x.astype(jnp.bfloat16).reshape(owners, channels // owners, frames, 2, antennas)
    return x


def plain_beam_power(x, real_weight, imaginary_weight, wides, subs, pols):
    _, own, frames, _, antennas = x.shape
    beams = real_weight.shape[2]
    x = x.reshape(wides, subs, pols, own, frames, 2, antennas)
    x = x.transpose(3, 5, 2, 1, 4, 0, 6).reshape(own, 2, pols * subs * frames, wides * antennas)
    by_re, by_im = (
        jnp.einsum("crfa,cab->rcfb", x, weight, preferred_element_type=jnp.float32)
        for weight in (real_weight, imaginary_weight)
    )
    power = (by_re[0] - by_im[1]) ** 2 + (by_im[0] + by_re[1]) ** 2
    power = power.reshape(own, pols, subs * frames, beams).sum(axis=1)
    power = power - jnp.mean(power, axis=1, keepdims=True)
    targets = wides * subs
    power = power.reshape(own, subs * frames, targets, beams // targets)
    return power.transpose(2, 0, 1, 3).reshape(targets, own, -1).astype(jnp.bfloat16)


def plain_shift_and_add(power, delays, frames):
    channels = power.shape[0]
    power = power.reshape(channels, frames, -1)
    chosen = (delays[None] % frames == jnp.arange(frames)[:, None, None]).astype(jnp.bfloat16)
    picked = jnp.einsum("dtc,cfb->dbft", chosen, power, preferred_element_type=jnp.float32)
    moved = sum(jnp.roll(picked[delay], -delay, axis=1) for delay in range(frames))
    return moved * (1.0 / math.sqrt(channels))


def local(voltages, real_weight, imaginary_weight, delays):
    wides, subs, pols = (lax.axis_size(name) for name in OWNERS)
    owners = wides * subs * pols
    own, _, beams = real_weight.shape
    frames = subs * voltages.shape[2]
    volts = jnp.transpose(voltages[0], (1, 0, 2))
    tiled = (
        own % ROWS == 0
        and voltages.shape[1] % 128 == 0
        and (beams // (wides * subs)) % 32 == 0
        and frames == 4
        and pols == 2
    )
    turn = functools.partial(
        lax.all_to_all, axis_name=OWNERS, split_axis=0, concat_axis=0, tiled=True
    )
    if not tiled:
        x = turn(plain_spectra(volts, owners, own * owners))
        power = plain_beam_power(x, real_weight, imaginary_weight, wides, subs, pols)
        power = jnp.broadcast_to(power[:, None], (wides * subs, pols) + power.shape[1:])
        power = turn(power.reshape(owners, own, -1))
        return plain_shift_and_add(power.reshape(owners * own, -1), delays, frames)
    x = turn(spectra(volts, owners, own * owners))
    power = beam_power(x, real_weight, imaginary_weight, wides, subs, pols)
    power = turn(power.reshape(owners, own, -1))
    return shift_and_add(power.reshape(owners * own, -1), delays, frames)


def solution(mesh):
    placed = (
        P("pol", ("group", "wide"), "sub", None),
        P(OWNERS, None, None),
        P(OWNERS, None, None),
        P("pol", None),
    )
    return jax.shard_map(
        local,
        mesh=mesh,
        in_specs=placed,
        out_specs=P(("group", "wide", "sub"), None, "pol"),
        check_vma=False,
    )
```

time: 70.6 us -> 64.3 us (0.911)
  blocking collectives: 32 us -> 44.7 us
  waiting for transfers between devices: 7.22 us -> 0 us
  starting transfers between devices: 4.99 us -> 0 us
  Pallas kernels: 21.5 us -> 16.7 us
  local copies, waits for them, and re-layouts: 3.8 us -> 2.65 us
    all_to_all x1 -> x2, blocking collectives: 32 us -> 44.7 us  [the longest x1 32 us: local(): x = turn(spectra(volts, owners, own * owners))]
    all_to_all x1 -> x0, waiting for transfers between devices: 7.22 us -> none  [local(): lax.all_to_all(power, OWNERS, split_axis=0, concat_axis=0, tiled=True)]
    all_to_all x1 -> x0, starting transfers between devices: 4.99 us -> none  [local(): lax.all_to_all(power, OWNERS, split_axis=0, concat_axis=0, tiled=True)]
    pallas_call x2, Pallas kernels: 19.6 us -> 15.7 us  [the longest x1 8.19 us: beam_power(): pl.pallas_call(functools.partial(beam_kernel, wides), in_specs=[vmem] * 3...]
    pallas_call x1, Pallas kernels: 1.94 us -> 0.98 us  [shift_and_add(): pl.pallas_call(functools.partial(shift_kernel, 1.0 / math.sqrt(channels))...]
  transfers between devices with their start and end apart: 1 -> 0, of which waited for: 1 -> 0; matrix products, arithmetic and copies ran while one was open for 1% -> 0% of each run, Pallas kernels for 0% -> 0%
where the time goes in v2:
time: 64.3 us; the launch traced here: 64.1 us
  blocking collectives  44.7 us (70%)
  Pallas kernels  16.7 us (26%)
  local copies, waits for them, and re-layouts  2.65 us (4%)
    all_to_all x1, blocking collectives, local(): x = turn(spectra(volts, owners, own * owners))  32 us
    all_to_all x1, blocking collectives, local(): power = turn(power.reshape(owners, own, -1))  12.7 us
    pallas_call x1, Pallas kernels, beam_power(): pl.pallas_call(functools.partial(beam_kernel, wides), in_specs=[vmem] * 3...  8.19 us
    pallas_call x1, Pallas kernels, spectra(): pl.pallas_call(dft_kernel, in_specs=[pl.BlockSpec(memory_space=pltpu.HBM)...  7.54 us
    unnamed x7, local copies, waits for them, and re-layouts  2.65 us

profile of v2, /device:TPU:0, one launch (start us, length us, event | category | flops | bytes accessed | tf_op | source)
XLA Modules:
  0.0 64.1 jit_solution(11541081791010458951)
XLA Ops:
  0.0 0.0 copy-start.2
  0.0 0.0 copy-start
  0.0 2.6 %copy.9 = bf16[1,256,2,2048]{3,1,2,0:T(8,128)(2,1)S(1)} copy(bf16[1,256,2,2048]{3,2,1,0:T(2,128)(2,1)} %param.6) | data formatting | bytes 4194304 | tf_op args[0]
  2.7 7.5 %spectra.1 = bf16[16,2,64,256]{3,2,1,0:T(8,128)(2,1)S(1)} custom-call(bf16[4,512,2048]{2,1,0:T(8,128)(2,1)} %constant.4.clone.table_ref, bf16[2,256,2048]{2,1,0:T(8,128)(2,1)S(1)} %bitcast.7), custom_call_target="tpu_custom_call" | custom-call | tf_op jit(solution)/shard_map/spectra/pallas_call | solution.py:68
  10.2 32.0 %all_to_all.10.x_ref = bf16[16,2,64,256]{3,2,1,0:T(8,128)(2,1)S(1)} all-to-all(bf16[16,2,64,256]{3,2,1,0:T(8,128)(2,1)S(1)} %spectra.1), channel_id=1, replica_groups=mesh['group'=2,'wide'=4,'sub'=2,'pol'=2] {'wide','sub','pol'}, dimensions={0} | all-to-all | bytes 2097152 | tf_op jit(solution)/shard_map/all_to_all | solution.py:257
  42.2 0.0 copy-done.2
  42.2 0.0 copy-done
  42.2 0.0 copy-start.1
  42.2 8.2 %beam_power.1 = bf16[8,2,32,128]{3,2,1,0:T(8,128)(2,1)S(1)} custom-call(bf16[128,128]{1,0:T(8,128)(2,1)S(1)} %copy-done.2, bf16[16,2,64,256]{3,2,1,0:T(8,128)(2,1)S(1)} %all_to_all.10.x_ref, bf16[32,1024,256]{2,1,0:T(8,128)(2,1)S(1)} %copy-done, bf16[32,1024,256]{2,1,0:T(8,128)(2,1)} %im_ref.1), custom_call_target="tpu_custom_call" | custom-call | tf_op jit(solution)/shard_map/beam_power/pallas_call | solution.py:148
  50.4 12.7 %all_to_all.11 = bf16[16,32,128]{2,1,0:T(8,128)(2,1)S(1)} all-to-all(bf16[16,32,128]{2,1,0:T(8,128)(2,1)S(1)} %bitcast.8), channel_id=1, replica_groups=mesh['group'=2,'wide'=4,'sub'=2,'pol'=2] {'wide','sub','pol'}, dimensions={0} | all-to-all | bytes 262144 | tf_op jit(solution)/shard_map/all_to_all | solution.py:259
  63.1 0.0 copy-done.1
  63.1 1.0 %shift_and_add.1 = f32[32,4,64]{2,1,0:T(4,128)} custom-call(bf16[512,128]{1,0:T(8,128)(2,1)S(1)} %bitcast.9, s32[64,512]{1,0:T(8,128)S(1)} %copy-done.1), custom_call_target="tpu_custom_call" | custom-call | tf_op jit(solution)/shard_map/shift_and_add/pallas_call | solution.py:190
Async XLA Ops:
  0.0 42.2 %copy-start.2 = (bf16[128,128]{1,0:T(8,128)(2,1)S(1)}, bf16[128,128]{1,0:T(8,128)(2,1)}, u32[]{:S(2)}) copy-start(bf16[128,128]{1,0:T(8,128)(2,1)} %constant.5.clone.order_ref) | copy-start | bytes 98308
  0.0 42.2 %copy-start = (bf16[32,1024,256]{2,1,0:T(8,128)(2,1)S(1)}, bf16[32,1024,256]{2,1,0:T(8,128)(2,1)}, u32[]{:S(2)}) copy-start(bf16[32,1024,256]{2,1,0:T(8,128)(2,1)} %re_ref.1) | copy-start | bytes 50331652
  42.2 20.9 %copy-start.1 = (s32[64,512]{1,0:T(8,128)S(1)}, s32[64,512]{1,0:T(8,128)}, u32[]{:S(2)}) copy-start(s32[64,512]{1,0:T(8,128)} %delay_ref.1) | copy-start | bytes 393220

commit v3 on v2

v3 whole, which is shorter than its diff:
```python
import functools
import math

import jax
import jax.numpy as jnp
import ml_dtypes
import numpy as np
from jax import lax
from jax.experimental import pallas as pl
from jax.experimental.pallas import tpu as pltpu
from jax.sharding import PartitionSpec as P

OWNERS = ("wide_high", "wide_low", "sub", "pol")
ROWS = 16
COST = pl.CostEstimate(flops=0, bytes_accessed=0, transcendentals=0)


def dft_parts(samples, channels):
    first = samples // 2 - channels
    bins = first + np.arange(channels, dtype=np.int64)
    turns = bins[:, None] * np.arange(samples, dtype=np.int64)[None, :] % samples
    angles = turns * (2.0 * math.pi / samples)
    exact = np.stack([np.cos(angles), -np.sin(angles)], axis=1) / math.sqrt(samples)
    upper = exact.astype(ml_dtypes.bfloat16)
    lower = (exact - upper.astype(np.float64)).astype(ml_dtypes.bfloat16)
    return upper, lower


def keep_weights(place_ref, first, refs, kept_refs, sem):
    copies = []
    for part, (ref, kept) in enumerate(zip(refs, kept_refs)):
        antennas = kept.shape[2]
        for index in range(kept.shape[0]):
            start = pl.multiple_of(place_ref[first + index] * antennas, antennas)
            copies.append(
                pltpu.make_async_copy(
                    ref.at[:, pl.ds(start, antennas), :], kept.at[index], sem.at[part, index]
                )
            )
    return copies


def dft_kernel(counts, here_ref, table_ref, volt_ref, *refs):
    steps, subs, pols, parts = counts
    weight_refs, refs = refs[:parts], refs[parts:]
    out_refs, refs = refs[: steps * subs], refs[steps * subs :]
    kept_refs, refs = refs[:parts], refs[parts:]
    part_ref, hold_ref, sem = refs[:3]
    frames = volt_ref.shape[0]
    copies = [
        pltpu.make_async_copy(table_ref.at[here_ref[step]], part_ref.at[step], sem.at[step])
        for step in range(steps)
    ]
    keeps = keep_weights(here_ref, 0, weight_refs, kept_refs, refs[-1])
    for copy in copies + keeps:
        copy.start()
    here = here_ref[steps]
    half = part_ref.shape[1] // 2
    for step, copy in enumerate(copies):
        copy.wait()
        for frame in range(frames):
            both = lax.dot_general(
                part_ref[step],
                volt_ref[frame],
                (((1,), (1,)), ((), ())),
                preferred_element_type=jnp.float32,
            )
            spectrum = (both[:half] + both[half:]).astype(jnp.bfloat16)
            hold_ref[step * frames + frame] = spectrum.reshape(
                subs * pols, -1, spectrum.shape[-1]
            )
            for sub in range(subs):
                for pol in range(pols):
                    out_refs[step * subs + sub][pol, frame] = hold_ref[
                        step * frames + frame, (sub * pols + pol) ^ here
                    ]
    for copy in keeps:
        copy.wait()


def spectra(volts, table, here, steps, subs, pols, weights=()):
    frames, antennas, samples = volts.shape
    rows = table.shape[1] // (2 * subs * pols)
    vmem = pl.BlockSpec(memory_space=pltpu.VMEM)
    hbm = pl.BlockSpec(memory_space=pltpu.HBM)
    kept = [
        pltpu.VMEM((steps, weight.shape[0], antennas, weight.shape[2]), weight.dtype)
        for weight in weights
    ]
    pieces = [jax.ShapeDtypeStruct((pols, frames, rows, antennas), jnp.bfloat16)] * (steps * subs)
    outs = pl.pallas_call(
        functools.partial(dft_kernel, (steps, subs, pols, len(weights))),
        in_specs=[pl.BlockSpec(memory_space=pltpu.SMEM), hbm, vmem] + [hbm] * len(weights),
        out_specs=[vmem] * (len(pieces) + len(kept)),
        out_shape=pieces + kept,
        scratch_shapes=[
            pltpu.VMEM((steps,) + table.shape[1:], jnp.bfloat16),
            pltpu.VMEM((steps * frames, subs * pols, rows, antennas), jnp.bfloat16),
            pltpu.SemaphoreType.DMA((steps,)),
            pltpu.SemaphoreType.DMA((2, steps)),
        ],
        compiler_params=pltpu.CompilerParams(vmem_limit_bytes=14 * 2**20),
        name="spectra",
    )(here, table, volts, *weights)
    return list(outs[: len(pieces)]), list(outs[len(pieces) :])


def beam_rows(x_refs, at, pols, order_ref):
    blocks = []
    for pol in range(pols):
        for refs in x_refs:
            frames, _, antennas = refs[pol].shape[1:]
            block = refs[pol][pol, :, at * ROWS : (at + 1) * ROWS, :]
            blocks.append(block.reshape(frames * ROWS, antennas))
    block = jnp.concatenate(blocks, axis=0)
    return jnp.dot(order_ref[...], block, preferred_element_type=jnp.float32).astype(jnp.bfloat16)


def beam_part(lines, half, weights):
    by_re = by_im = None
    for line, re, im in zip(lines, *weights):
        re, im = (
            jnp.dot(line, weight, preferred_element_type=jnp.float32) for weight in (re, im)
        )
        by_re = re if by_re is None else by_re + re
        by_im = im if by_im is None else by_im + im
    return by_re[:half] - by_im[half:], by_im[:half] + by_re[half:]


def first_kernel(counts, place_ref, order_ref, re_ref, im_ref, *refs):
    later, subs, pols = counts
    x_refs = [refs[sub * pols : (sub + 1) * pols] for sub in range(subs)]
    out_ref, re_kept, im_kept, re_held, im_held, sem, kept_sem = refs[subs * pols :]
    groups, group, antennas, _ = re_held.shape
    frames = x_refs[0][0].shape[1]
    half = subs * pols * frames

    start = pl.multiple_of(place_ref[0] * antennas, antennas)
    copies = [
        [
            pltpu.make_async_copy(
                ref.at[pl.ds(at * group, group), pl.ds(start, antennas), :],
                held.at[at],
                sem.at[part, at],
            )
            for part, (ref, held) in enumerate(((re_ref, re_held), (im_ref, im_held)))
        ]
        for at in range(groups)
    ]
    keeps = keep_weights(place_ref, 1, (re_ref, im_ref), (re_kept, im_kept), kept_sem)
    for pair in copies:
        for copy in pair:
            copy.start()
    for copy in keeps:
        copy.start()
    for at in range(groups):
        rows = beam_rows(x_refs, at, pols, order_ref)
        for copy in copies[at]:
            copy.wait()
        for index in range(group):
            line = rows[index * 2 * half : (index + 1) * 2 * half]
            beams = beam_part([line], half, ([re_held[at, index]], [im_held[at, index]]))
            out_ref[at * group + index, :half] = beams[0]
            out_ref[at * group + index, half:] = beams[1]
    for copy in keeps:
        copy.wait()


def last_kernel(counts, place_ref, order_ref, *refs):
    lots, subs, pols = counts
    weight_refs, sum_ref, refs = refs[: 2 * lots], refs[2 * lots], refs[2 * lots + 1 :]
    at_refs = [
        tuple(ref.at[k] for ref in weight_refs[2 * lot : 2 * lot + 2])
        for lot in range(lots)
        for k in range(weight_refs[2 * lot].shape[0])
    ]
    later = len(at_refs)
    x_refs = [
        [refs[(index * subs + sub) * pols :][:pols] for sub in range(subs)]
        for index in range(later)
    ]
    out_ref, power_ref = refs[later * subs * pols :]
    channels = sum_ref.shape[0]
    group = ROWS // 2
    frames = x_refs[0][0][0].shape[1]
    half = subs * pols * frames
    for at in range(channels // group):
        rows = [beam_rows(refs, at, pols, order_ref) for refs in x_refs]
        for index in range(group):
            channel = at * group + index
            weights = [[refs[part][channel] for refs in at_refs] for part in range(2)]
            lines = [row[index * 2 * half : (index + 1) * 2 * half] for row in rows]
            beam_re, beam_im = beam_part(lines, half, weights)
            beam_re = beam_re + sum_ref[channel, :half]
            beam_im = beam_im + sum_ref[channel, half:]
            power = beam_re * beam_re + beam_im * beam_im
            power = sum(power[k * subs * frames : (k + 1) * subs * frames] for k in range(pols))
            power = power - jnp.mean(power, axis=0, keepdims=True)
            for sub in range(subs):
                start = (place_ref[0] ^ sub) * frames
                for frame in range(frames):
                    power_ref[start + frame, channel] = power[sub * frames + frame]
    targets, cores = out_ref.shape[:2]
    beams = power_ref.shape[2] // targets
    for target in range(targets):
        block = jnp.concatenate(
            [power_ref[f, :, target * beams : (target + 1) * beams] for f in range(subs * frames)],
            axis=1,
        ).astype(jnp.bfloat16)
        for core in range(cores):
            out_ref[target, core] = block


def sorting(subs, pols, frames):
    group = ROWS // 2
    count = subs * pols * frames * ROWS
    spot = np.arange(count).reshape(pols, subs, frames, 2, group).transpose(4, 3, 0, 1, 2).reshape(-1)
    order = np.zeros((count, count), np.float32)
    order[np.arange(count), spot] = 1.0
    return jnp.asarray(order, jnp.bfloat16)


def first_beams(xs, place, weights, subs, pols):
    _, frames, _, antennas = xs[0].shape
    channels, _, beams = weights[0].shape
    group = ROWS // 2
    later = place.shape[0] - 1
    vmem = pl.BlockSpec(memory_space=pltpu.VMEM)
    hbm = pl.BlockSpec(memory_space=pltpu.HBM)
    kept = pltpu.VMEM((later, channels, antennas, beams), jnp.bfloat16)
    sums = jax.ShapeDtypeStruct((channels, 2 * subs * pols * frames, beams), jnp.float32)
    held = pltpu.VMEM((channels // group, group, antennas, beams), jnp.bfloat16)
    return pl.pallas_call(
        functools.partial(first_kernel, (later, subs, pols)),
        in_specs=[pl.BlockSpec(memory_space=pltpu.SMEM), vmem, hbm, hbm] + [vmem] * len(xs),
        out_specs=[vmem] * 3,
        out_shape=[sums, kept, kept],
        scratch_shapes=[
            held,
            held,
            pltpu.SemaphoreType.DMA((2, channels // group)),
            pltpu.SemaphoreType.DMA((2, later)),
        ],
        compiler_params=pltpu.CompilerParams(vmem_limit_bytes=14 * 2**20),
        name="first_beams",
    )(place, sorting(subs, pols, frames), *weights, *xs)


def beam_power(xs, place, kept, sums, wides, subs, pols):
    frames = xs[0].shape[1]
    _, channels, _, beams = kept[0].shape
    targets = wides * subs
    width = subs * frames * (beams // targets)
    vmem = pl.BlockSpec(memory_space=pltpu.VMEM)
    return pl.pallas_call(
        functools.partial(last_kernel, (len(kept) // 2, subs, pols)),
        in_specs=[pl.BlockSpec(memory_space=pltpu.SMEM)] + [vmem] * (2 + len(kept) + len(xs)),
        out_specs=vmem,
        out_shape=jax.ShapeDtypeStruct((targets, pols, channels, width), jnp.bfloat16),
        scratch_shapes=[pltpu.VMEM((subs * frames, channels, beams), jnp.float32)],
        compiler_params=pltpu.CompilerParams(vmem_limit_bytes=8 * 2**20),
        name="beam_power",
    )(
        place,
        sorting(subs, pols, frames),
        *(pltpu.with_memory_space_constraint(part, pltpu.VMEM) for part in kept),
        sums,
        *xs,
    )


def exchange(x, offset, names):
    count = math.prod(lax.axis_size(name) for name in names)
    return lax.ppermute(x, names, [(k, k ^ offset) for k in range(count)])


def dft_table(samples, channels, wides, owners):
    own = channels // owners
    group = ROWS // 2

    def order(part):
        part = part.reshape(wides, owners // wides, own // group, group, 2, samples)
        return part.transpose(0, 1, 2, 4, 3, 5).reshape(wides, -1, samples)

    return np.concatenate([order(part) for part in dft_parts(samples, channels)], axis=1)


def shift_kernel(scale, power_ref, delay_ref, out_ref):
    beams, frames, _ = out_ref.shape
    delays = lax.rem(delay_ref[...], frames)
    power = power_ref[...]
    sums = [None] * frames
    for delay in range(frames):
        chosen = (delays == delay).astype(jnp.float32).astype(jnp.bfloat16)
        picked = lax.dot_general(
            power, chosen, (((0,), (1,)), ((), ())), preferred_element_type=jnp.float32
        )
        for frame in range(frames):
            row = (frame + delay) % frames * beams
            term = picked[row : row + beams]
            sums[frame] = term if sums[frame] is None else sums[frame] + term
    for frame in range(frames):
        out_ref[:, frame, :] = sums[frame] * scale


def shift_and_add(power, delays, frames):
    channels, width = power.shape
    beams = width // frames
    return pl.pallas_call(
        functools.partial(shift_kernel, 1.0 / math.sqrt(channels)),
        out_shape=jax.ShapeDtypeStruct((beams, frames, delays.shape[0]), jnp.float32),
        compiler_params=pltpu.CompilerParams(vmem_limit_bytes=8 * 2**20),
        name="shift_and_add",
    )(power, delays)


def plain_spectra(volts, owners, channels):
    frames, antennas, samples = volts.shape
    upper, lower = (jnp.asarray(part) for part in dft_parts(samples, channels))
    x = sum(
        jnp.einsum("krn,fan->kfra", part, volts, preferred_element_type=jnp.float32)
        for part in (upper, lower)
    )
    x = x.astype(jnp.bfloat16).reshape(owners, channels // owners, frames, 2, antennas)
    return x


def plain_beam_power(x, real_weight, imaginary_weight, wides, subs, pols):
    _, own, frames, _, antennas = x.shape
    beams = real_weight.shape[2]
    x = x.reshape(wides, subs, pols, own, frames, 2, antennas)
    x = x.transpose(3, 5, 2, 1, 4, 0, 6).reshape(own, 2, pols * subs * frames, wides * antennas)
    by_re, by_im = (
        jnp.einsum("crfa,cab->rcfb", x, weight, preferred_element_type=jnp.float32)
        for weight in (real_weight, imaginary_weight)
    )
    power = (by_re[0] - by_im[1]) ** 2 + (by_im[0] + by_re[1]) ** 2
    power = power.reshape(own, pols, subs * frames, beams).sum(axis=1)
    power = power - jnp.mean(power, axis=1, keepdims=True)
    targets = wides * subs
    power = power.reshape(own, subs * frames, targets, beams // targets)
    return power.transpose(2, 0, 1, 3).reshape(targets, own, -1).astype(jnp.bfloat16)


def plain_shift_and_add(power, delays, frames):
    channels = power.shape[0]
    power = power.reshape(channels, frames, -1)
    chosen = (delays[None] % frames == jnp.arange(frames)[:, None, None]).astype(jnp.bfloat16)
    picked = jnp.einsum("dtc,cfb->dbft", chosen, power, preferred_element_type=jnp.float32)
    moved = sum(jnp.roll(picked[delay], -delay, axis=1) for delay in range(frames))
    return moved * (1.0 / math.sqrt(channels))


def local(voltages, real_weight, imaginary_weight, delays):
    highs, lows, subs, pols = (lax.axis_size(name) for name in OWNERS)
    wides = highs * lows
    owners = wides * subs * pols
    own, _, beams = real_weight.shape
    frames = subs * voltages.shape[2]
    volts = jnp.transpose(voltages[0], (1, 0, 2))
    tiled = (
        own % ROWS == 0
        and voltages.shape[1] % 128 == 0
        and (beams // (wides * subs)) % 32 == 0
        and frames == 4
        and (wides, subs, pols) == (4, 2, 2)
    )
    turn = functools.partial(
        lax.all_to_all, axis_name=OWNERS, split_axis=0, concat_axis=0, tiled=True
    )
    if not tiled:
        x = turn(plain_spectra(volts, owners, own * owners))
        power = plain_beam_power(x, real_weight, imaginary_weight, wides, subs, pols)
        power = jnp.broadcast_to(power[:, None], (wides * subs, pols) + power.shape[1:])
        power = turn(power.reshape(owners, own, -1))
        return plain_shift_and_add(power.reshape(owners * own, -1), delays, frames)
    high, low, sub, pol = (lax.axis_index(name) for name in OWNERS)
    side, core = lax.axis_size("wide_low"), sub * pols + pol
    table = jnp.asarray(dft_table(voltages.shape[3], own * owners, wides, owners))
    table = pltpu.with_memory_space_constraint(table, pltpu.HBM)
    volts = pltpu.with_memory_space_constraint(volts, pltpu.VMEM)
    weights = [
        pltpu.with_memory_space_constraint(weight, pltpu.HBM)
        for weight in (real_weight, imaginary_weight)
    ]

    def numbers(*values):
        return jnp.stack(values).astype(jnp.int32)

    wide = high * side + low
    offsets = list(range(side, wides)) + list(range(side))[::-1]
    at = [wide ^ offset for offset in offsets]
    far, _ = spectra(volts, table, numbers(*at[:side], core), side, subs, pols)
    volts, _ = lax.optimization_barrier((volts, far[0]))
    near, near_kept = spectra(
        volts, table, numbers(*at[side:], core), side, subs, pols, weights
    )
    moved = []
    for k, piece in enumerate(far + near):
        offset = (offsets[k // subs] * subs + k % subs) * pols
        moved.append(exchange(piece, offset, OWNERS) if offset else piece)

    def both(pieces):
        return [part for mine in pieces for part in (mine, exchange(mine, 1, ("pol",)))]

    first, _ = lax.optimization_barrier((moved[:subs], near[0]))
    sums, *kept = first_beams(both(first), numbers(*at[:side]), weights, subs, pols)
    rest, sums = lax.optimization_barrier((moved[subs:], sums))
    total = beam_power(both(rest), numbers(sub), kept + near_kept, sums, wides, subs, pols)
    power = turn(total.reshape(owners, own, -1))
    return shift_and_add(power.reshape(owners * own, -1), delays, frames)


def solution(mesh):
    names = dict(zip(mesh.axis_names, mesh.devices.shape))
    low = max(1, names["wide"] // 2)
    sizes = (names["group"], names["wide"] // low, low, names["sub"], names["pol"])
    split = jax.sharding.Mesh(mesh.devices.reshape(sizes), ("group",) + OWNERS)
    placed = (
        P("pol", ("group", "wide_high", "wide_low"), "sub", None),
        P(OWNERS, None, None),
        P(OWNERS, None, None),
        P("pol", None),
    )
    return jax.shard_map(
        local,
        mesh=split,
        in_specs=placed,
        out_specs=P(("group", "wide_high", "wide_low", "sub"), None, "pol"),
        check_vma=False,
    )
```

time: 64.3 us -> 61.1 us (0.950)
  blocking collectives: 44.7 us -> 12.6 us
  starting transfers between devices: 0 us -> 14.4 us
  Pallas kernels: 16.7 us -> 24 us
  waiting for transfers between devices: 0 us -> 7.25 us
    all_to_all x2 -> x1, blocking collectives: 44.7 us -> 12.6 us  [local(): power = turn(total.reshape(owners, own, -1))]
    ppermute x0 -> x15, starting transfers between devices: none -> 14.4 us  [exchange(): return lax.ppermute(x, names, [(k, k ^ offset) for k in range(count)])]
    pallas_call x2 -> x4, Pallas kernels: 15.7 us -> 23.1 us  [the longest x2 12.6 us: spectra(): pl.pallas_call(functools.partial(dft_kernel, (steps, subs, pols, len(weig...]
    ppermute x0 -> x15, waiting for transfers between devices: none -> 7.25 us  [exchange(): return lax.ppermute(x, names, [(k, k ^ offset) for k in range(count)])]
    unnamed x7 -> x5, local copies, waits for them, and re-layouts: 2.65 us -> 2.48 us
  transfers between devices with their start and end apart: 0 -> 15, of which waited for: 0 -> 10; matrix products, arithmetic and copies ran while one was open for 0% -> 0% of each run, Pallas kernels for 0% -> 23%
where the time goes in v3:
time: 61.1 us; the launch traced here: 60.9 us
  Pallas kernels  24 us (39%)
  starting transfers between devices  14.4 us (24%)
  blocking collectives  12.6 us (21%)
  waiting for transfers between devices  7.25 us (12%)
  local copies, waits for them, and re-layouts  2.48 us (4%)
    ppermute x15, starting transfers between devices, exchange(): return lax.ppermute(x, names, [(k, k ^ offset) for k in range(count)])  14.4 us
    all_to_all x1, blocking collectives, local(): power = turn(total.reshape(owners, own, -1))  12.6 us
    pallas_call x2, Pallas kernels, spectra(): pl.pallas_call(functools.partial(dft_kernel, (steps, subs, pols, len(weig...  12.6 us
    ppermute x15, waiting for transfers between devices, exchange(): return lax.ppermute(x, names, [(k, k ^ offset) for k in range(count)])  7.25 us
    pallas_call x1, Pallas kernels, first_beams(): pl.pallas_call(functools.partial(first_kernel, (later, subs, pols)), in_s...  6.51 us
    pallas_call x1, Pallas kernels, beam_power(): pl.pallas_call(functools.partial(last_kernel, (len(kept) // 2, subs, pols...  3.99 us
    unnamed x5, local copies, waits for them, and re-layouts  2.48 us
  transfers between devices with their start and end apart: 15, of which 10 were waited for; matrix products, arithmetic and copies ran while one was open for 0% of the time, Pallas kernels for 23%

profile of v3, /device:TPU:0, one launch (start us, length us, event | category | flops | bytes accessed | tf_op | source)
XLA Modules:
  0.0 60.9 jit_solution(17808836902330413890)
XLA Ops:
  0.0 2.5 %copy.10 = bf16[1,256,2,2048]{3,1,2,0:T(8,128)(2,1)S(1)} copy(bf16[1,256,2,2048]{3,2,1,0:T(2,128)(2,1)} %param.7) | data formatting | bytes 4194304 | tf_op args[0]
  2.5 0.1 add_add_fusion
  2.6 4.8 %spectra.2 = (bf16[2,2,64,256]{3,2,1,0:T(8,128)(2,1)S(1)}, bf16[2,2,64,256]{3,2,1,0:T(8,128)(2,1)S(1)}, bf16[2,2,64,256]{3,2,1,0:T(8,128)(2,1)S(1)}, bf16[2,2,64,256]{3,2,1,0:T(8,128)(2,1)S(1)}) custom-call(s32[3]{0:T(128)S(1)} %get-tuple-element.51.here_ref, bf16[4,512,2048]{2,1,0:T(8,128)(2,1)} %constant.24.clone.table_ref, bf16[2,256,2048]{2,1,0:T(8,128)(2,1)S(1)} %bitcast.13), custom_call_target="tpu_custom_call" | custom-call | tf_op jit(solution)/shard_map/spectra/pallas_call | solution.py:91
  7.4 5.0 %collective-permute-start.1 = (bf16[2,2,64,256]{3,2,1,0:T(8,128)(2,1)S(1)}, bf16[2,2,64,256]{3,2,1,0:T(8,128)(2,1)S(1)}, u32[]{:S(2)}, u32[]{:S(2)}) collective-permute-start(bf16[2,2,64,256]{3,2,1,0:T(8,128)(2,1)S(1)} %get-tuple-element.29), channel_id=1, source_target_pairs={{0,10},{1,11},{2,8},{3,9},{4,14},{5,15},{6,12},{7,13},{8,2},{9,3},... | collective-permute-start | bytes 393224 | tf_op jit(solution)/shard_map/ppermute | solution.py:274
  12.4 0.3 collective-permute-start
  12.7 0.0 copy-start.1
  12.7 7.8 %spectra.3 = (bf16[2,2,64,256]{3,2,1,0:T(8,128)(2,1)S(1)}, bf16[2,2,64,256]{3,2,1,0:T(8,128)(2,1)S(1)}, bf16[2,2,64,256]{3,2,1,0:T(8,128)(2,1)S(1)}, bf16[2,2,64...) custom-call(s32[3]{0:T(128)S(1)} %get-tuple-element.52.here_ref, ...), custom_call_target="tpu_custom_call" | custom-call | tf_op jit(solution)/shard_map/spectra/pallas_call | solution.py:91
  20.5 1.8 %collective-permute-done.1.refs_2_ = bf16[2,2,64,256]{3,2,1,0:T(8,128)(2,1)S(1)} collective-permute-done((bf16[2,2,64,256]{3,2,1,0:T(8,128)(2,1)S(1)}, bf16[2,2,64,256]{3,2,1,0:T(8,128)(2,1)S(1)}, u32[]{:S(2)}, u32[]{:S(2)}) %collective-permute-start.1) | collective-permute-done | bytes 131104 | tf_op jit(solution)/shard_map/ppermute | solution.py:274
  22.4 2.0 %collective-permute-done.refs_0_ = bf16[2,2,64,256]{3,2,1,0:T(8,128)(2,1)S(1)} collective-permute-done((bf16[2,2,64,256]{3,2,1,0:T(8,128)(2,1)S(1)}, bf16[2,2,64,256]{3,2,1,0:T(8,128)(2,1)S(1)}, u32[]{:S(2)}, u32[]{:S(2)}) %collective-permute-start) | collective-permute-done | bytes 131104 | tf_op jit(solution)/shard_map/ppermute | solution.py:274
  24.4 0.0 collective-permute-start.2
  24.4 0.5 collective-permute-start.3
  24.9 3.5 %collective-permute-start.4 = (bf16[2,2,64,256]{3,2,1,0:T(8,128)(2,1)S(1)}, bf16[2,2,64,256]{3,2,1,0:T(8,128)(2,1)S(1)}, u32[]{:S(2)}, u32[]{:S(2)}) collective-permute-start(bf16[2,2,64,256]{3,2,1,0:T(8,128)(2,1)S(1)} %get-tuple-element.38), channel_id=1, source_target_pairs={{0,12},{1,13},{2,14},{3,15},{4,8},{5,9},{6,10},{7,11},{8,4},{9,5},... | collective-permute-start | bytes 393224 | tf_op jit(solution)/shard_map/ppermute | solution.py:274
  28.4 0.3 collective-permute-start.5
  28.7 0.0 collective-permute-start.7
  28.7 0.0 collective-permute-done.2.refs_1_
  28.7 1.5 %collective-permute-start.8 = (bf16[2,2,64,256]{3,2,1,0:T(8,128)(2,1)S(1)}, bf16[2,2,64,256]{3,2,1,0:T(8,128)(2,1)S(1)}, u32[]{:S(2)}, u32[]{:S(2)}) collective-permute-start(bf16[2,2,64,256]{3,2,1,0:T(8,128)(2,1)S(1)} %get-tuple-element.42), channel_id=1, source_target_pairs={{0,2},{1,3},{2,0},{3,1},{4,6},{5,7},{6,4},{7,5},{8,10},{9,11},{10,... | collective-permute-start | bytes 393224 | tf_op jit(solution)/shard_map/ppermute | solution.py:274
  30.2 0.0 collective-permute-done.3.refs_3_
  30.2 2.0 %collective-permute-start.6 = (bf16[2,2,64,256]{3,2,1,0:T(8,128)(2,1)S(1)}, bf16[2,2,64,256]{3,2,1,0:T(8,128)(2,1)S(1)}, u32[]{:S(2)}, u32[]{:S(2)}) collective-permute-start(bf16[2,2,64,256]{3,2,1,0:T(8,128)(2,1)S(1)} %get-tuple-element.31), channel_id=1, source_target_pairs={{0,4},{1,5},{2,6},{3,7},{4,0},{5,1},{6,2},{7,3},{8,12},{9,13},{10,... | collective-permute-start | bytes 393224 | tf_op jit(solution)/shard_map/ppermute | solution.py:274
  32.2 0.1 pad_add_fusion.place_ref
  32.2 0.0 copy-done.1
  32.2 6.5 %first_beams.1 = (f32[32,16,256]{2,1,0:T(8,128)S(1)}, bf16[1,32,256,256]{3,2,1,0:T(8,128)(2,1)S(1)}, bf16[1,32,256,256]{3,2,1,0:T(8,128)(2,1)S(1)}) custom-call(s32[2]{0:T(128)S(1)} %pad_add_fusion.place_ref, bf16[128,128]{1,0:T(8,128)(2,1)S(1)} %copy-done.1, bf16[32,1024,256]{2,1,0:T(8,128)(2,1)} %re_ref.1, bf16[32,1024,256]{2,1,0:T(8,128)(2,1)} %im_ref.1, ...), custom_call_target="tpu_custom_call" | custom-call | tf_op jit(solution)/shard_map/first_beams/pallas_call | solution.py:233
  38.8 0.0 collective-permute-done.4.refs_5_
  38.8 0.0 collective-permute-done.5.refs_7_
  38.8 0.1 collective-permute-done.7.refs_11_
  38.9 0.4 collective-permute-done.8.refs_15_
  39.2 1.5 %collective-permute-done.6.refs_9_ = bf16[2,2,64,256]{3,2,1,0:T(8,128)(2,1)S(1)} collective-permute-done((bf16[2,2,64,256]{3,2,1,0:T(8,128)(2,1)S(1)}, bf16[2,2,64,256]{3,2,1,0:T(8,128)(2,1)S(1)}, u32[]{:S(2)}, u32[]{:S(2)}) %collective-permute-start.6) | collective-permute-done | bytes 131104 | tf_op jit(solution)/shard_map/ppermute | solution.py:274
  40.7 0.0 collective-permute-start.9
  40.7 0.5 collective-permute-start.10
  41.2 0.0 collective-permute-start.11
  41.2 0.5 collective-permute-start.12
  41.7 0.0 collective-permute-start.13
  41.7 0.3 collective-permute-done.9.refs_6_
  42.0 0.2 collective-permute-start.14
  42.2 0.0 collective-permute-done.10.refs_8_
  42.2 0.3 collective-permute-done.11.refs_10_
  42.5 0.2 collective-permute-done.12.refs_12_
  42.7 0.3 collective-permute-done.13.refs_14_
  43.0 0.3 collective-permute-done.14.refs_16_
  43.4 0.0 copy-start
  43.4 4.0 %beam_power.1 = bf16[8,2,32,128]{3,2,1,0:T(8,128)(2,1)S(1)} custom-call(s32[1]{0:T(128)} %bitcast.place_ref, bf16[128,128]{1,0:T(8,128)(2,1)S(1)} %copy-done.1, bf16[1,32,256,256]{3,2,1,0:T(8,128)(2,1)S(1)} %get-tuple-element.34.refs_0_, bf16[1,32,256,256]{3,2,1,0:T(8,128)(2,1)S(1)} %get-tuple-element.35.refs_1_, ...), custom_call_target="tpu_custom_call" | custom-call | tf_op jit(solution)/shard_map/beam_power/pallas_call | solution.py:255
  47.4 12.6 %all_to_all.5 = bf16[16,32,128]{2,1,0:T(8,128)(2,1)S(1)} all-to-all(bf16[16,32,128]{2,1,0:T(8,128)(2,1)S(1)} %bitcast.15), channel_id=1, replica_groups=mesh['group'=2,'wide_high'=2,'wide_low'=2,'sub'=2,'pol'=2] {'wide_high',..., dimensions={0} | all-to-all | bytes 262144 | tf_op jit(solution)/shard_map/all_to_all | solution.py:410
  59.9 0.0 copy-done
  59.9 1.0 %shift_and_add.1 = f32[32,4,64]{2,1,0:T(4,128)} custom-call(bf16[512,128]{1,0:T(8,128)(2,1)S(1)} %bitcast.16, s32[64,512]{1,0:T(8,128)S(1)} %copy-done), custom_call_target="tpu_custom_call" | custom-call | tf_op jit(solution)/shard_map/shift_and_add/pallas_call | solution.py:309
Async XLA Ops:
  7.4 15.0 %collective-permute-start.1 = (bf16[2,2,64,256]{3,2,1,0:T(8,128)(2,1)S(1)}, bf16[2,2,64,256]{3,2,1,0:T(8,128)(2,1)S(1)}, u32[]{:S(2)}, u32[]{:S(2)}) collective-permute-start(bf16[2,2,64,256]{3,2,1,0:T(8,128)(2,1)S(1)} %get-tuple-element.29), channel_id=1, source_target_pairs={{0,10},{1,11},{2,8},{3,9},{4,14},{5,15},{6,12},{7,13},{8,2},{9,3},... | collective-permute-start | bytes 393224 | tf_op jit(solution)/shard_map/ppermute | solution.py:274
  12.4 12.0 %collective-permute-start = (bf16[2,2,64,256]{3,2,1,0:T(8,128)(2,1)S(1)}, bf16[2,2,64,256]{3,2,1,0:T(8,128)(2,1)S(1)}, u32[]{:S(2)}, u32[]{:S(2)}) collective-permute-start(bf16[2,2,64,256]{3,2,1,0:T(8,128)(2,1)S(1)} %get-tuple-element.28), channel_id=1, source_target_pairs={{0,8},{1,9},{2,10},{3,11},{4,12},{5,13},{6,14},{7,15},{8,0},{9,1},... | collective-permute-start | bytes 393224 | tf_op jit(solution)/shard_map/ppermute | solution.py:274
  12.7 19.5 %copy-start.1 = (bf16[128,128]{1,0:T(8,128)(2,1)S(1)}, bf16[128,128]{1,0:T(8,128)(2,1)}, u32[]{:S(2)}) copy-start(bf16[128,128]{1,0:T(8,128)(2,1)} %constant.25.clone.order_ref) | copy-start | bytes 98308
  24.4 4.3 %collective-permute-start.2 = (bf16[2,2,64,256]{3,2,1,0:T(8,128)(2,1)S(1)}, bf16[2,2,64,256]{3,2,1,0:T(8,128)(2,1)S(1)}, u32[]{:S(2)}, u32[]{:S(2)}) collective-permute-start(bf16[2,2,64,256]{3,2,1,0:T(8,128)(2,1)S(1)} %collective-permute-done.refs_0_), channel_id=1, source_target_pairs={{0,1},{1,0},{2,3},{3,2},{4,5},{5,4},{6,7},{7,6},{8,9},{9,8},{10,11... | collective-permute-start | bytes 393224 | tf_op jit(solution)/shard_map/ppermute | solution.py:274
  24.4 5.8 %collective-permute-start.3 = (bf16[2,2,64,256]{3,2,1,0:T(8,128)(2,1)S(1)}, bf16[2,2,64,256]{3,2,1,0:T(8,128)(2,1)S(1)}, u32[]{:S(2)}, u32[]{:S(2)}) collective-permute-start(bf16[2,2,64,256]{3,2,1,0:T(8,128)(2,1)S(1)} %collective-permute-done.1.refs_2_), channel_id=1, source_target_pairs={{0,1},{1,0},{2,3},{3,2},{4,5},{5,4},{6,7},{7,6},{8,9},{9,8},{10,11... | collective-permute-start | bytes 393224 | tf_op jit(solution)/shard_map/ppermute | solution.py:274
  24.9 13.9 %collective-permute-start.4 = (bf16[2,2,64,256]{3,2,1,0:T(8,128)(2,1)S(1)}, bf16[2,2,64,256]{3,2,1,0:T(8,128)(2,1)S(1)}, u32[]{:S(2)}, u32[]{:S(2)}) collective-permute-start(bf16[2,2,64,256]{3,2,1,0:T(8,128)(2,1)S(1)} %get-tuple-element.38), channel_id=1, source_target_pairs={{0,12},{1,13},{2,14},{3,15},{4,8},{5,9},{6,10},{7,11},{8,4},{9,5},... | collective-permute-start | bytes 393224 | tf_op jit(solution)/shard_map/ppermute | solution.py:274
  28.4 10.4 %collective-permute-start.5 = (bf16[2,2,64,256]{3,2,1,0:T(8,128)(2,1)S(1)}, bf16[2,2,64,256]{3,2,1,0:T(8,128)(2,1)S(1)}, u32[]{:S(2)}, u32[]{:S(2)}) collective-permute-start(bf16[2,2,64,256]{3,2,1,0:T(8,128)(2,1)S(1)} %get-tuple-element.39), channel_id=1, source_target_pairs={{0,14},{1,15},{2,12},{3,13},{4,10},{5,11},{6,8},{7,9},{8,6},{9,7},... | collective-permute-start | bytes 393224 | tf_op jit(solution)/shard_map/ppermute | solution.py:274
  28.7 10.2 %collective-permute-start.7 = (bf16[2,2,64,256]{3,2,1,0:T(8,128)(2,1)S(1)}, bf16[2,2,64,256]{3,2,1,0:T(8,128)(2,1)S(1)}, u32[]{:S(2)}, u32[]{:S(2)}) collective-permute-start(bf16[2,2,64,256]{3,2,1,0:T(8,128)(2,1)S(1)} %get-tuple-element.40), channel_id=1, source_target_pairs={{0,6},{1,7},{2,4},{3,5},{4,2},{5,3},{6,0},{7,1},{8,14},{9,15},{10,... | collective-permute-start | bytes 393224 | tf_op jit(solution)/shard_map/ppermute | solution.py:274
  28.7 10.5 %collective-permute-start.8 = (bf16[2,2,64,256]{3,2,1,0:T(8,128)(2,1)S(1)}, bf16[2,2,64,256]{3,2,1,0:T(8,128)(2,1)S(1)}, u32[]{:S(2)}, u32[]{:S(2)}) collective-permute-start(bf16[2,2,64,256]{3,2,1,0:T(8,128)(2,1)S(1)} %get-tuple-element.42), channel_id=1, source_target_pairs={{0,2},{1,3},{2,0},{3,1},{4,6},{5,7},{6,4},{7,5},{8,10},{9,11},{10,... | collective-permute-start | bytes 393224 | tf_op jit(solution)/shard_map/ppermute | solution.py:274
  30.2 10.5 %collective-permute-start.6 = (bf16[2,2,64,256]{3,2,1,0:T(8,128)(2,1)S(1)}, bf16[2,2,64,256]{3,2,1,0:T(8,128)(2,1)S(1)}, u32[]{:S(2)}, u32[]{:S(2)}) collective-permute-start(bf16[2,2,64,256]{3,2,1,0:T(8,128)(2,1)S(1)} %get-tuple-element.31), channel_id=1, source_target_pairs={{0,4},{1,5},{2,6},{3,7},{4,0},{5,1},{6,2},{7,3},{8,12},{9,13},{10,... | collective-permute-start | bytes 393224 | tf_op jit(solution)/shard_map/ppermute | solution.py:274
  40.7 1.3 %collective-permute-start.9 = (bf16[2,2,64,256]{3,2,1,0:T(8,128)(2,1)S(1)}, bf16[2,2,64,256]{3,2,1,0:T(8,128)(2,1)S(1)}, u32[]{:S(2)}, u32[]{:S(2)}) collective-permute-start(bf16[2,2,64,256]{3,2,1,0:T(8,128)(2,1)S(1)} %collective-permute-done.4.refs_5_), channel_id=1, source_target_pairs={{0,1},{1,0},{2,3},{3,2},{4,5},{5,4},{6,7},{7,6},{8,9},{9,8},{10,11... | collective-permute-start | bytes 393224 | tf_op jit(solution)/shard_map/ppermute | solution.py:274
  40.7 1.5 %collective-permute-start.10 = (bf16[2,2,64,256]{3,2,1,0:T(8,128)(2,1)S(1)}, bf16[2,2,64,256]{3,2,1,0:T(8,128)(2,1)S(1)}, u32[]{:S(2)}, u32[]{:S(2)}) collective-permute-start(bf16[2,2,64,256]{3,2,1,0:T(8,128)(2,1)S(1)} %collective-permute-done.5.refs_7_), channel_id=1, source_target_pairs={{0,1},{1,0},{2,3},{3,2},{4,5},{5,4},{6,7},{7,6},{8,9},{9,8},{10,11... | collective-permute-start | bytes 393224 | tf_op jit(solution)/shard_map/ppermute | solution.py:274
  41.2 1.3 %collective-permute-start.11 = (bf16[2,2,64,256]{3,2,1,0:T(8,128)(2,1)S(1)}, bf16[2,2,64,256]{3,2,1,0:T(8,128)(2,1)S(1)}, u32[]{:S(2)}, u32[]{:S(2)}) collective-permute-start(bf16[2,2,64,256]{3,2,1,0:T(8,128)(2,1)S(1)} %collective-permute-done.6.refs_9_), channel_id=1, source_target_pairs={{0,1},{1,0},{2,3},{3,2},{4,5},{5,4},{6,7},{7,6},{8,9},{9,8},{10,11... | collective-permute-start | bytes 393224 | tf_op jit(solution)/shard_map/ppermute | solution.py:274
  41.2 1.5 %collective-permute-start.12 = (bf16[2,2,64,256]{3,2,1,0:T(8,128)(2,1)S(1)}, bf16[2,2,64,256]{3,2,1,0:T(8,128)(2,1)S(1)}, u32[]{:S(2)}, u32[]{:S(2)}) collective-permute-start(bf16[2,2,64,256]{3,2,1,0:T(8,128)(2,1)S(1)} %collective-permute-done.7.refs_11_), channel_id=1, source_target_pairs={{0,1},{1,0},{2,3},{3,2},{4,5},{5,4},{6,7},{7,6},{8,9},{9,8},{10,11... | collective-permute-start | bytes 393224 | tf_op jit(solution)/shard_map/ppermute | solution.py:274
  41.7 1.3 %collective-permute-start.13 = (bf16[2,2,64,256]{3,2,1,0:T(8,128)(2,1)S(1)}, bf16[2,2,64,256]{3,2,1,0:T(8,128)(2,1)S(1)}, u32[]{:S(2)}, u32[]{:S(2)}) collective-permute-start(bf16[2,2,64,256]{3,2,1,0:T(8,128)(2,1)S(1)} %get-tuple-element.49.refs_13_), channel_id=1, source_target_pairs={{0,1},{1,0},{2,3},{3,2},{4,5},{5,4},{6,7},{7,6},{8,9},{9,8},{10,11... | collective-permute-start | bytes 393224 | tf_op jit(solution)/shard_map/ppermute | solution.py:274
  42.0 1.3 %collective-permute-start.14 = (bf16[2,2,64,256]{3,2,1,0:T(8,128)(2,1)S(1)}, bf16[2,2,64,256]{3,2,1,0:T(8,128)(2,1)S(1)}, u32[]{:S(2)}, u32[]{:S(2)}) collective-permute-start(bf16[2,2,64,256]{3,2,1,0:T(8,128)(2,1)S(1)} %collective-permute-done.8.refs_15_), channel_id=1, source_target_pairs={{0,1},{1,0},{2,3},{3,2},{4,5},{5,4},{6,7},{7,6},{8,9},{9,8},{10,11... | collective-permute-start | bytes 393224 | tf_op jit(solution)/shard_map/ppermute | solution.py:274
  43.4 16.6 %copy-start = (s32[64,512]{1,0:T(8,128)S(1)}, s32[64,512]{1,0:T(8,128)}, u32[]{:S(2)}) copy-start(s32[64,512]{1,0:T(8,128)} %delay_ref.1) | copy-start | bytes 393220

commit v4 on v3

--- a/solution.py
+++ b/solution.py
@@ -41,19 +41,37 @@
 
 
 def dft_kernel(counts, here_ref, table_ref, volt_ref, *refs):
-    steps, subs, pols, parts = counts
+    steps, subs, pols, parts, first = counts
     weight_refs, refs = refs[:parts], refs[parts:]
     out_refs, refs = refs[: steps * subs], refs[steps * subs :]
     kept_refs, refs = refs[:parts], refs[parts:]
+    moved_ref, refs = (refs[0], refs[1:]) if first else (volt_ref, refs)
     part_ref, hold_ref, sem = refs[:3]
-    frames = volt_ref.shape[0]
+    frames = moved_ref.shape[0]
     copies = [
         pltpu.make_async_copy(table_ref.at[here_ref[step]], part_ref.at[step], sem.at[step])
         for step in range(steps)
     ]
-    keeps = keep_weights(here_ref, 0, weight_refs, kept_refs, refs[-1])
-    for copy in copies + keeps:
-        copy.start()
+    if first:
+        raw_ref, raw_sem = refs[3:]
+        count = raw_ref.shape[0] // raw_sem.shape[0]
+        reads = []
+        for index in range(raw_sem.shape[0]):
+            rows = pl.ds(index * count, count)
+            reads.append(
+                pltpu.make_async_copy(volt_ref.at[0, rows], raw_ref.at[rows], raw_sem.at[index])
+            )
+        for copy in reads + copies:
+            copy.start()
+        for index, copy in enumerate(reads):
+            copy.wait()
+            rows = pl.ds(index * count, count)
+            moved_ref[:, rows, :] = raw_ref[rows].transpose(1, 0, 2)
+        keeps = []
+    else:
+        keeps = keep_weights(here_ref, steps - kept_refs[0].shape[0], weight_refs, kept_refs, refs[3])
+        for copy in copies + keeps:
+            copy.start()
     here = here_ref[steps]
     half = part_ref.shape[1] // 2
     for step, copy in enumerate(copies):
@@ -61,7 +79,7 @@
         for frame in range(frames):
             both = lax.dot_general(
                 part_ref[step],
-                volt_ref[frame],
+                moved_ref[frame],
                 (((1,), (1,)), ((), ())),
                 preferred_element_type=jnp.float32,
             )
@@ -78,28 +96,39 @@
         copy.wait()
 
 
-def spectra(volts, table, here, steps, subs, pols, weights=()):
-    frames, antennas, samples = volts.shape
+def spectra(volts, table, here, steps, subs, pols, weights=(), keep=0):
+    first = volts.ndim == 4
+    frames, antennas = volts.shape[:2] if not first else volts.shape[2:0:-1]
+    samples = volts.shape[-1]
     rows = table.shape[1] // (2 * subs * pols)
     vmem = pl.BlockSpec(memory_space=pltpu.VMEM)
     hbm = pl.BlockSpec(memory_space=pltpu.HBM)
     kept = [
-        pltpu.VMEM((steps, weight.shape[0], antennas, weight.shape[2]), weight.dtype)
+        pltpu.VMEM((keep, weight.shape[0], antennas, weight.shape[2]), weight.dtype)
         for weight in weights
     ]
     pieces = [jax.ShapeDtypeStruct((pols, frames, rows, antennas), jnp.bfloat16)] * (steps * subs)
+    scratch = [
+        pltpu.VMEM((steps,) + table.shape[1:], jnp.bfloat16),
+        pltpu.VMEM((steps * frames, subs * pols, rows, antennas), jnp.bfloat16),
+        pltpu.SemaphoreType.DMA((steps,)),
+    ]
+    if first:
+        kept.append(pltpu.VMEM((frames, antennas, samples), volts.dtype))
+        scratch.append(pltpu.VMEM((antennas, frames, samples), volts.dtype))
+        scratch.append(pltpu.SemaphoreType.DMA((4,)))
+        volts = pltpu.with_memory_space_constraint(volts, pltpu.HBM)
+    else:
+        scratch.append(pltpu.SemaphoreType.DMA((2, keep)))
+        volts = pltpu.with_memory_space_constraint(volts, pltpu.VMEM)
     outs = pl.pallas_call(
-        functools.partial(dft_kernel, (steps, subs, pols, len(weights))),
-        in_specs=[pl.BlockSpec(memory_space=pltpu.SMEM), hbm, vmem] + [hbm] * len(weights),
+        functools.partial(dft_kernel, (steps, subs, pols, len(weights), first)),
+        in_specs=[pl.BlockSpec(memory_space=pltpu.SMEM), hbm, hbm if first else vmem]
+        + [hbm] * len(weights),
         out_specs=[vmem] * (len(pieces) + len(kept)),
         out_shape=pieces + kept,
-        scratch_shapes=[
-            pltpu.VMEM((steps,) + table.shape[1:], jnp.bfloat16),
-            pltpu.VMEM((steps * frames, subs * pols, rows, antennas), jnp.bfloat16),
-            pltpu.SemaphoreType.DMA((steps,)),
-            pltpu.SemaphoreType.DMA((2, steps)),
-        ],
-        compiler_params=pltpu.CompilerParams(vmem_limit_bytes=14 * 2**20),
+        scratch_shapes=scratch,
+        compiler_params=pltpu.CompilerParams(vmem_limit_bytes=12 * 2**20),
         name="spectra",
     )(here, table, volts, *weights)
     return list(outs[: len(pieces)]), list(outs[len(pieces) :])
@@ -110,7 +139,7 @@
     for pol in range(pols):
         for refs in x_refs:
             frames, _, antennas = refs[pol].shape[1:]
-            block = refs[pol][pol, :, at * ROWS : (at + 1) * ROWS, :]
+            block = refs[pol][0, :, at * ROWS : (at + 1) * ROWS, :]
             blocks.append(block.reshape(frames * ROWS, antennas))
     block = jnp.concatenate(blocks, axis=0)
     return jnp.dot(order_ref[...], block, preferred_element_type=jnp.float32).astype(jnp.bfloat16)
@@ -241,7 +270,8 @@
             pltpu.SemaphoreType.DMA((2, channels // group)),
             pltpu.SemaphoreType.DMA((2, later)),
         ],
-        compiler_params=pltpu.CompilerParams(vmem_limit_bytes=14 * 2**20),
+        compiler_params=pltpu.CompilerParams(vmem_limit_bytes=12 * 2**20),
+        cost_estimate=pl.CostEstimate(flops=4*10**10, bytes_accessed=4*10**8, transcendentals=0),
         name="first_beams",
     )(place, sorting(subs, pols, frames), *weights, *xs)
 
@@ -357,7 +387,6 @@
     owners = wides * subs * pols
     own, _, beams = real_weight.shape
     frames = subs * voltages.shape[2]
-    volts = jnp.transpose(voltages[0], (1, 0, 2))
     tiled = (
         own % ROWS == 0
         and voltages.shape[1] % 128 == 0
@@ -369,6 +398,7 @@
         lax.all_to_all, axis_name=OWNERS, split_axis=0, concat_axis=0, tiled=True
     )
     if not tiled:
+        volts = jnp.transpose(voltages[0], (1, 0, 2))
         x = turn(plain_spectra(volts, owners, own * owners))
         power = plain_beam_power(x, real_weight, imaginary_weight, wides, subs, pols)
         power = jnp.broadcast_to(power[:, None], (wides * subs, pols) + power.shape[1:])
@@ -378,7 +408,6 @@
     side, core = lax.axis_size("wide_low"), sub * pols + pol
     table = jnp.asarray(dft_table(voltages.shape[3], own * owners, wides, owners))
     table = pltpu.with_memory_space_constraint(table, pltpu.HBM)
-    volts = pltpu.with_memory_space_constraint(volts, pltpu.VMEM)
     weights = [
         pltpu.with_memory_space_constraint(weight, pltpu.HBM)
         for weight in (real_weight, imaginary_weight)
@@ -390,10 +419,9 @@
     wide = high * side + low
     offsets = list(range(side, wides)) + list(range(side))[::-1]
     at = [wide ^ offset for offset in offsets]
-    far, _ = spectra(volts, table, numbers(*at[:side], core), side, subs, pols)
-    volts, _ = lax.optimization_barrier((volts, far[0]))
+    far, (volts,) = spectra(voltages, table, numbers(at[0], core), 1, subs, pols)
     near, near_kept = spectra(
-        volts, table, numbers(*at[side:], core), side, subs, pols, weights
+        volts, table, numbers(*at[1:], core), wides - 1, subs, pols, weights, side
     )
     moved = []
     for k, piece in enumerate(far + near):
@@ -401,7 +429,7 @@
         moved.append(exchange(piece, offset, OWNERS) if offset else piece)
 
     def both(pieces):
-        return [part for mine in pieces for part in (mine, exchange(mine, 1, ("pol",)))]
+        return [part for mine in pieces for part in (mine, exchange(mine[1:], 1, ("pol",)))]
 
     first, _ = lax.optimization_barrier((moved[:subs], near[0]))
     sums, *kept = first_beams(both(first), numbers(*at[:side]), weights, subs, pols)

time: 61.1 us -> 53.9 us (0.88)
  waiting for transfers between devices: 7.25 us -> 2.58 us
  local copies, waits for them, and re-layouts: 2.48 us -> 0.06 us
    ppermute x15, waiting for transfers between devices: 7.25 us -> 2.58 us  [exchange(): return lax.ppermute(x, names, [(k, k ^ offset) for k in range(count)])]
    unnamed x5 -> x4, local copies, waits for them, and re-layouts: 2.48 us -> 0.01 us
  transfers between devices with their start and end apart: 15 -> 15, of which waited for: 10 -> 6; matrix products, arithmetic and copies ran while one was open for 0% -> 0% of each run, Pallas kernels for 23% -> 28%
where the time goes in v4:
time: 53.9 us; the launch traced here: 53.8 us
  Pallas kernels  24 us (45%)
  starting transfers between devices  14.7 us (27%)
  blocking collectives  12.1 us (22%)
  waiting for transfers between devices  2.58 us (5%)
    ppermute x15, starting transfers between devices, exchange(): return lax.ppermute(x, names, [(k, k ^ offset) for k in range(count)])  14.7 us
    pallas_call x2, Pallas kernels, spectra(): pl.pallas_call(functools.partial(dft_kernel, (steps, subs, pols, len(weig...  12.5 us
    all_to_all x1, blocking collectives, local(): power = turn(total.reshape(owners, own, -1))  12.1 us
    pallas_call x1, Pallas kernels, first_beams(): pl.pallas_call(functools.partial(first_kernel, (later, subs, pols)), in_s...  6.51 us
    pallas_call x1, Pallas kernels, beam_power(): pl.pallas_call(functools.partial(last_kernel, (len(kept) // 2, subs, pols...  4.03 us
    ppermute x15, waiting for transfers between devices, exchange(): return lax.ppermute(x, names, [(k, k ^ offset) for k in range(count)])  2.58 us
  transfers between devices with their start and end apart: 15, of which 6 were waited for; matrix products, arithmetic and copies ran while one was open for 0% of the time, Pallas kernels for 28%

profile of v4, /device:TPU:0, one launch (start us, length us, event | category | flops | bytes accessed | tf_op | source)
XLA Modules:
  0.0 53.8 jit_solution(3848408505687531482)
XLA Ops:
  0.0 0.1 pad_add_fusion.1.here_ref
  0.1 4.1 %spectra.2 = (bf16[2,2,64,256]{3,2,1,0:T(8,128)(2,1)S(1)}, bf16[2,2,64,256]{3,2,1,0:T(8,128)(2,1)S(1)}, bf16[2,256,2048]{2,1,0:T(8,128)(2,1)S(1)}) custom-call(s32[2]{0:T(128)S(1)} %pad_add_fusion.1.here_ref, bf16[4,512,2048]{2,1,0:T(8,128)(2,1)} %constant.24.clone.table_ref, bf16[1,256,2,2048]{3,2,1,0:T(2,128)(2,1)} %volt_ref.1), custom_call_target="tpu_custom_call" | custom-call | tf_op jit(solution)/shard_map/spectra/pallas_call | solution.py:124
  4.2 4.1 %collective-permute-start = (bf16[2,2,64,256]{3,2,1,0:T(8,128)(2,1)S(1)}, bf16[2,2,64,256]{3,2,1,0:T(8,128)(2,1)S(1)}, u32[]{:S(2)}, u32[]{:S(2)}) collective-permute-start(bf16[2,2,64,256]{3,2,1,0:T(8,128)(2,1)S(1)} %get-tuple-element.28), channel_id=1, source_target_pairs={{0,8},{1,9},{2,10},{3,11},{4,12},{5,13},{6,14},{7,15},{8,0},{9,1},... | collective-permute-start | bytes 393224 | tf_op jit(solution)/shard_map/ppermute | solution.py:304
  8.3 1.3 %collective-permute-start.1 = (bf16[2,2,64,256]{3,2,1,0:T(8,128)(2,1)S(1)}, bf16[2,2,64,256]{3,2,1,0:T(8,128)(2,1)S(1)}, u32[]{:S(2)}, u32[]{:S(2)}) collective-permute-start(bf16[2,2,64,256]{3,2,1,0:T(8,128)(2,1)S(1)} %get-tuple-element.29), channel_id=1, source_target_pairs={{0,10},{1,11},{2,8},{3,9},{4,14},{5,15},{6,12},{7,13},{8,2},{9,3},... | collective-permute-start | bytes 393224 | tf_op jit(solution)/shard_map/ppermute | solution.py:304
  9.6 0.1 pad_add_fusion.2.here_ref
  9.7 0.0 copy-start.1
  9.7 8.4 %spectra.3 = (bf16[2,2,64,256]{3,2,1,0:T(8,128)(2,1)S(1)}, bf16[2,2,64,256]{3,2,1,0:T(8,128)(2,1)S(1)}, bf16[2,2,64,256]{3,2,1,0:T(8,128)(2,1)S(1)}, bf16[2,2,64...) custom-call(s32[4]{0:T(128)S(1)} %pad_add_fusion.2.here_ref, ...), custom_call_target="tpu_custom_call" | custom-call | tf_op jit(solution)/shard_map/spectra/pallas_call | solution.py:124
  18.0 3.6 %collective-permute-start.5 = (bf16[2,2,64,256]{3,2,1,0:T(8,128)(2,1)S(1)}, bf16[2,2,64,256]{3,2,1,0:T(8,128)(2,1)S(1)}, u32[]{:S(2)}, u32[]{:S(2)}) collective-permute-start(bf16[2,2,64,256]{3,2,1,0:T(8,128)(2,1)S(1)} %get-tuple-element.38), channel_id=1, source_target_pairs={{0,14},{1,15},{2,12},{3,13},{4,10},{5,11},{6,8},{7,9},{8,6},{9,7},... | collective-permute-start | bytes 393224 | tf_op jit(solution)/shard_map/ppermute | solution.py:304
  21.7 0.0 collective-permute-start.6
  21.7 0.9 %collective-permute-start.4 = (bf16[2,2,64,256]{3,2,1,0:T(8,128)(2,1)S(1)}, bf16[2,2,64,256]{3,2,1,0:T(8,128)(2,1)S(1)}, u32[]{:S(2)}, u32[]{:S(2)}) collective-permute-start(bf16[2,2,64,256]{3,2,1,0:T(8,128)(2,1)S(1)} %get-tuple-element.31), channel_id=1, source_target_pairs={{0,12},{1,13},{2,14},{3,15},{4,8},{5,9},{6,10},{7,11},{8,4},{9,5},... | collective-permute-start | bytes 393224 | tf_op jit(solution)/shard_map/ppermute | solution.py:304
  22.6 0.0 collective-permute-done.refs_0_
  22.6 0.0 collective-permute-done.1.refs_2_
  22.6 0.1 collective-permute-start.3
  22.7 0.5 collective-permute-start.2
  23.2 0.1 pad_add_fusion.place_ref
  23.3 0.7 %collective-permute-done.3.refs_3_ = bf16[1,2,64,256]{3,2,1,0:T(8,128)(2,1)S(1)} collective-permute-done((bf16[1,2,64,256]{3,2,1,0:T(8,128)(2,1)S(1)}, bf16[1,2,64,256]{3,2,1,0:T(8,128)(2,1)S(1)}, u32[]{:S(2)}, u32[]{:S(2)}) %collective-permute-start.3) | collective-permute-done | bytes 65568 | tf_op jit(solution)/shard_map/ppermute | solution.py:304
  23.9 2.1 %collective-permute-start.7 = (bf16[2,2,64,256]{3,2,1,0:T(8,128)(2,1)S(1)}, bf16[2,2,64,256]{3,2,1,0:T(8,128)(2,1)S(1)}, u32[]{:S(2)}, u32[]{:S(2)}) collective-permute-start(bf16[2,2,64,256]{3,2,1,0:T(8,128)(2,1)S(1)} %get-tuple-element.40), channel_id=1, source_target_pairs={{0,6},{1,7},{2,4},{3,5},{4,2},{5,3},{6,0},{7,1},{8,14},{9,15},{10,... | collective-permute-start | bytes 393224 | tf_op jit(solution)/shard_map/ppermute | solution.py:304
  26.0 0.0 collective-permute-done.2.refs_1_
  26.0 0.5 collective-permute-start.8
  26.5 0.0 copy-done.1
  26.5 6.5 %first_beams.1 = (f32[32,16,256]{2,1,0:T(8,128)S(1)}, bf16[1,32,256,256]{3,2,1,0:T(8,128)(2,1)S(1)}, bf16[1,32,256,256]{3,2,1,0:T(8,128)(2,1)S(1)}) custom-call(s32[2]{0:T(128)S(1)} %pad_add_fusion.place_ref, bf16[128,128]{1,0:T(8,128)(2,1)S(1)} %copy-done.1, bf16[32,1024,256]{2,1,0:T(8,128)(2,1)} %re_ref.1, bf16[32,1024,256]{2,1,0:T(8,128)(2,1)} %im_ref.1, ...), custom_call_target="tpu_custom_call" | custom-call | flops 40000000000 | bytes 400000000 | tf_op jit(solution)/shard_map/first_beams/pallas_call | solution.py:262
  33.1 0.0 collective-permute-done.5.refs_7_
  33.1 0.0 collective-permute-done.6.refs_9_
  33.1 1.0 %collective-permute-done.7.refs_11_ = bf16[2,2,64,256]{3,2,1,0:T(8,128)(2,1)S(1)} collective-permute-done((bf16[2,2,64,256]{3,2,1,0:T(8,128)(2,1)S(1)}, bf16[2,2,64,256]{3,2,1,0:T(8,128)(2,1)S(1)}, u32[]{:S(2)}, u32[]{:S(2)}) %collective-permute-start.7) | collective-permute-done | bytes 131104 | tf_op jit(solution)/shard_map/ppermute | solution.py:304
  34.0 0.0 collective-permute-done.8.refs_15_
  34.0 0.0 collective-permute-done.4.refs_5_
  34.1 0.1 collective-permute-start.14
  34.2 0.5 %collective-permute-start.13 = (bf16[1,2,64,256]{3,2,1,0:T(8,128)(2,1)S(1)}, bf16[1,2,64,256]{3,2,1,0:T(8,128)(2,1)S(1)}, u32[]{:S(2)}, u32[]{:S(2)}) collective-permute-start(bf16[1,2,64,256]{3,2,1,0:T(8,128)(2,1)S(1)} %slice.30), channel_id=1, source_target_pairs={{0,1},{1,0},{2,3},{3,2},{4,5},{5,4},{6,7},{7,6},{8,9},{9,8},{10,11... | collective-permute-start | bytes 196616 | tf_op jit(solution)/shard_map/ppermute | solution.py:304
  34.8 0.1 collective-permute-start.12
  34.8 0.4 collective-permute-start.11
  35.3 0.1 collective-permute-start.10
  35.3 0.0 collective-permute-done.14.refs_16_
  35.4 0.4 collective-permute-start.9
  35.8 0.0 collective-permute-done.13.refs_14_
  35.8 0.2 collective-permute-done.12.refs_12_
  36.0 0.2 collective-permute-done.11.refs_10_
  36.2 0.4 collective-permute-done.10.refs_8_
  36.5 0.2 collective-permute-done.9.refs_6_
  36.7 0.0 copy-start
  36.7 4.0 %beam_power.1 = bf16[8,2,32,128]{3,2,1,0:T(8,128)(2,1)S(1)} custom-call(s32[1]{0:T(128)} %bitcast.place_ref, bf16[128,128]{1,0:T(8,128)(2,1)S(1)} %copy-done.1, bf16[1,32,256,256]{3,2,1,0:T(8,128)(2,1)S(1)} %get-tuple-element.34.refs_0_, bf16[1,32,256,256]{3,2,1,0:T(8,128)(2,1)S(1)} %get-tuple-element.35.refs_1_, ...), custom_call_target="tpu_custom_call" | custom-call | tf_op jit(solution)/shard_map/beam_power/pallas_call | solution.py:285
  40.7 12.1 %all_to_all.5 = bf16[16,32,128]{2,1,0:T(8,128)(2,1)S(1)} all-to-all(bf16[16,32,128]{2,1,0:T(8,128)(2,1)S(1)} %bitcast.8), channel_id=1, replica_groups=mesh['group'=2,'wide_high'=2,'wide_low'=2,'sub'=2,'pol'=2] {'wide_high',..., dimensions={0} | all-to-all | bytes 262144 | tf_op jit(solution)/shard_map/all_to_all | solution.py:438
  52.8 0.0 copy-done
  52.8 1.0 %shift_and_add.1 = f32[32,4,64]{2,1,0:T(4,128)} custom-call(bf16[512,128]{1,0:T(8,128)(2,1)S(1)} %bitcast.9, s32[64,512]{1,0:T(8,128)S(1)} %copy-done), custom_call_target="tpu_custom_call" | custom-call | tf_op jit(solution)/shard_map/shift_and_add/pallas_call | solution.py:339
  (8 shorter events, 0.0 us)
Async XLA Ops:
  4.2 18.4 %collective-permute-start = (bf16[2,2,64,256]{3,2,1,0:T(8,128)(2,1)S(1)}, bf16[2,2,64,256]{3,2,1,0:T(8,128)(2,1)S(1)}, u32[]{:S(2)}, u32[]{:S(2)}) collective-permute-start(bf16[2,2,64,256]{3,2,1,0:T(8,128)(2,1)S(1)} %get-tuple-element.28), channel_id=1, source_target_pairs={{0,8},{1,9},{2,10},{3,11},{4,12},{5,13},{6,14},{7,15},{8,0},{9,1},... | collective-permute-start | bytes 393224 | tf_op jit(solution)/shard_map/ppermute | solution.py:304
  8.3 14.3 %collective-permute-start.1 = (bf16[2,2,64,256]{3,2,1,0:T(8,128)(2,1)S(1)}, bf16[2,2,64,256]{3,2,1,0:T(8,128)(2,1)S(1)}, u32[]{:S(2)}, u32[]{:S(2)}) collective-permute-start(bf16[2,2,64,256]{3,2,1,0:T(8,128)(2,1)S(1)} %get-tuple-element.29), channel_id=1, source_target_pairs={{0,10},{1,11},{2,8},{3,9},{4,14},{5,15},{6,12},{7,13},{8,2},{9,3},... | collective-permute-start | bytes 393224 | tf_op jit(solution)/shard_map/ppermute | solution.py:304
  9.7 16.9 %copy-start.1 = (bf16[128,128]{1,0:T(8,128)(2,1)S(1)}, bf16[128,128]{1,0:T(8,128)(2,1)}, u32[]{:S(2)}) copy-start(bf16[128,128]{1,0:T(8,128)(2,1)} %constant.25.clone.order_ref) | copy-start | bytes 98308
  18.0 15.0 %collective-permute-start.5 = (bf16[2,2,64,256]{3,2,1,0:T(8,128)(2,1)S(1)}, bf16[2,2,64,256]{3,2,1,0:T(8,128)(2,1)S(1)}, u32[]{:S(2)}, u32[]{:S(2)}) collective-permute-start(bf16[2,2,64,256]{3,2,1,0:T(8,128)(2,1)S(1)} %get-tuple-element.38), channel_id=1, source_target_pairs={{0,14},{1,15},{2,12},{3,13},{4,10},{5,11},{6,8},{7,9},{8,6},{9,7},... | collective-permute-start | bytes 393224 | tf_op jit(solution)/shard_map/ppermute | solution.py:304
  21.7 11.4 %collective-permute-start.6 = (bf16[2,2,64,256]{3,2,1,0:T(8,128)(2,1)S(1)}, bf16[2,2,64,256]{3,2,1,0:T(8,128)(2,1)S(1)}, u32[]{:S(2)}, u32[]{:S(2)}) collective-permute-start(bf16[2,2,64,256]{3,2,1,0:T(8,128)(2,1)S(1)} %get-tuple-element.39), channel_id=1, source_target_pairs={{0,4},{1,5},{2,6},{3,7},{4,0},{5,1},{6,2},{7,3},{8,12},{9,13},{10,... | collective-permute-start | bytes 393224 | tf_op jit(solution)/shard_map/ppermute | solution.py:304
  21.7 12.4 %collective-permute-start.4 = (bf16[2,2,64,256]{3,2,1,0:T(8,128)(2,1)S(1)}, bf16[2,2,64,256]{3,2,1,0:T(8,128)(2,1)S(1)}, u32[]{:S(2)}, u32[]{:S(2)}) collective-permute-start(bf16[2,2,64,256]{3,2,1,0:T(8,128)(2,1)S(1)} %get-tuple-element.31), channel_id=1, source_target_pairs={{0,12},{1,13},{2,14},{3,15},{4,8},{5,9},{6,10},{7,11},{8,4},{9,5},... | collective-permute-start | bytes 393224 | tf_op jit(solution)/shard_map/ppermute | solution.py:304
  22.6 1.3 %collective-permute-start.3 = (bf16[1,2,64,256]{3,2,1,0:T(8,128)(2,1)S(1)}, bf16[1,2,64,256]{3,2,1,0:T(8,128)(2,1)S(1)}, u32[]{:S(2)}, u32[]{:S(2)}) collective-permute-start(bf16[1,2,64,256]{3,2,1,0:T(8,128)(2,1)S(1)} %slice.25), channel_id=1, source_target_pairs={{0,1},{1,0},{2,3},{3,2},{4,5},{5,4},{6,7},{7,6},{8,9},{9,8},{10,11... | collective-permute-start | bytes 196616 | tf_op jit(solution)/shard_map/ppermute | solution.py:304
  22.7 3.3 %collective-permute-start.2 = (bf16[1,2,64,256]{3,2,1,0:T(8,128)(2,1)S(1)}, bf16[1,2,64,256]{3,2,1,0:T(8,128)(2,1)S(1)}, u32[]{:S(2)}, u32[]{:S(2)}) collective-permute-start(bf16[1,2,64,256]{3,2,1,0:T(8,128)(2,1)S(1)} %slice.24), channel_id=1, source_target_pairs={{0,1},{1,0},{2,3},{3,2},{4,5},{5,4},{6,7},{7,6},{8,9},{9,8},{10,11... | collective-permute-start | bytes 196616 | tf_op jit(solution)/shard_map/ppermute | solution.py:304
  23.9 10.1 %collective-permute-start.7 = (bf16[2,2,64,256]{3,2,1,0:T(8,128)(2,1)S(1)}, bf16[2,2,64,256]{3,2,1,0:T(8,128)(2,1)S(1)}, u32[]{:S(2)}, u32[]{:S(2)}) collective-permute-start(bf16[2,2,64,256]{3,2,1,0:T(8,128)(2,1)S(1)} %get-tuple-element.40), channel_id=1, source_target_pairs={{0,6},{1,7},{2,4},{3,5},{4,2},{5,3},{6,0},{7,1},{8,14},{9,15},{10,... | collective-permute-start | bytes 393224 | tf_op jit(solution)/shard_map/ppermute | solution.py:304
  26.0 8.0 %collective-permute-start.8 = (bf16[2,2,64,256]{3,2,1,0:T(8,128)(2,1)S(1)}, bf16[2,2,64,256]{3,2,1,0:T(8,128)(2,1)S(1)}, u32[]{:S(2)}, u32[]{:S(2)}) collective-permute-start(bf16[2,2,64,256]{3,2,1,0:T(8,128)(2,1)S(1)} %get-tuple-element.42), channel_id=1, source_target_pairs={{0,2},{1,3},{2,0},{3,1},{4,6},{5,7},{6,4},{7,5},{8,10},{9,11},{10,... | collective-permute-start | bytes 393224 | tf_op jit(solution)/shard_map/ppermute | solution.py:304
  34.1 1.3 %collective-permute-start.14 = (bf16[1,2,64,256]{3,2,1,0:T(8,128)(2,1)S(1)}, bf16[1,2,64,256]{3,2,1,0:T(8,128)(2,1)S(1)}, u32[]{:S(2)}, u32[]{:S(2)}) collective-permute-start(bf16[1,2,64,256]{3,2,1,0:T(8,128)(2,1)S(1)} %slice.31), channel_id=1, source_target_pairs={{0,1},{1,0},{2,3},{3,2},{4,5},{5,4},{6,7},{7,6},{8,9},{9,8},{10,11... | collective-permute-start | bytes 196616 | tf_op jit(solution)/shard_map/ppermute | solution.py:304
  34.2 1.6 %collective-permute-start.13 = (bf16[1,2,64,256]{3,2,1,0:T(8,128)(2,1)S(1)}, bf16[1,2,64,256]{3,2,1,0:T(8,128)(2,1)S(1)}, u32[]{:S(2)}, u32[]{:S(2)}) collective-permute-start(bf16[1,2,64,256]{3,2,1,0:T(8,128)(2,1)S(1)} %slice.30), channel_id=1, source_target_pairs={{0,1},{1,0},{2,3},{3,2},{4,5},{5,4},{6,7},{7,6},{8,9},{9,8},{10,11... | collective-permute-start | bytes 196616 | tf_op jit(solution)/shard_map/ppermute | solution.py:304
  34.8 1.3 %collective-permute-start.12 = (bf16[1,2,64,256]{3,2,1,0:T(8,128)(2,1)S(1)}, bf16[1,2,64,256]{3,2,1,0:T(8,128)(2,1)S(1)}, u32[]{:S(2)}, u32[]{:S(2)}) collective-permute-start(bf16[1,2,64,256]{3,2,1,0:T(8,128)(2,1)S(1)} %slice.29), channel_id=1, source_target_pairs={{0,1},{1,0},{2,3},{3,2},{4,5},{5,4},{6,7},{7,6},{8,9},{9,8},{10,11... | collective-permute-start | bytes 196616 | tf_op jit(solution)/shard_map/ppermute | solution.py:304
  34.8 1.3 %collective-permute-start.11 = (bf16[1,2,64,256]{3,2,1,0:T(8,128)(2,1)S(1)}, bf16[1,2,64,256]{3,2,1,0:T(8,128)(2,1)S(1)}, u32[]{:S(2)}, u32[]{:S(2)}) collective-permute-start(bf16[1,2,64,256]{3,2,1,0:T(8,128)(2,1)S(1)} %slice.28), channel_id=1, source_target_pairs={{0,1},{1,0},{2,3},{3,2},{4,5},{5,4},{6,7},{7,6},{8,9},{9,8},{10,11... | collective-permute-start | bytes 196616 | tf_op jit(solution)/shard_map/ppermute | solution.py:304
  35.3 1.3 %collective-permute-start.10 = (bf16[1,2,64,256]{3,2,1,0:T(8,128)(2,1)S(1)}, bf16[1,2,64,256]{3,2,1,0:T(8,128)(2,1)S(1)}, u32[]{:S(2)}, u32[]{:S(2)}) collective-permute-start(bf16[1,2,64,256]{3,2,1,0:T(8,128)(2,1)S(1)} %slice.27), channel_id=1, source_target_pairs={{0,1},{1,0},{2,3},{3,2},{4,5},{5,4},{6,7},{7,6},{8,9},{9,8},{10,11... | collective-permute-start | bytes 196616 | tf_op jit(solution)/shard_map/ppermute | solution.py:304
  35.4 1.3 %collective-permute-start.9 = (bf16[1,2,64,256]{3,2,1,0:T(8,128)(2,1)S(1)}, bf16[1,2,64,256]{3,2,1,0:T(8,128)(2,1)S(1)}, u32[]{:S(2)}, u32[]{:S(2)}) collective-permute-start(bf16[1,2,64,256]{3,2,1,0:T(8,128)(2,1)S(1)} %slice.26), channel_id=1, source_target_pairs={{0,1},{1,0},{2,3},{3,2},{4,5},{5,4},{6,7},{7,6},{8,9},{9,8},{10,11... | collective-permute-start | bytes 196616 | tf_op jit(solution)/shard_map/ppermute | solution.py:304
  36.7 16.1 %copy-start = (s32[64,512]{1,0:T(8,128)S(1)}, s32[64,512]{1,0:T(8,128)}, u32[]{:S(2)}) copy-start(s32[64,512]{1,0:T(8,128)} %delay_ref.1) | copy-start | bytes 393220

commit v5 on v4

--- a/solution.py
+++ b/solution.py
@@ -134,12 +134,18 @@
     return list(outs[: len(pieces)]), list(outs[len(pieces) :])
 
 
-def beam_rows(x_refs, at, pols, order_ref):
+def beam_rows(x_refs, index, subs, at, order_ref):
     blocks = []
-    for pol in range(pols):
-        for refs in x_refs:
-            frames, _, antennas = refs[pol].shape[1:]
-            block = refs[pol][0, :, at * ROWS : (at + 1) * ROWS, :]
+    for own in (True, False):
+        for piece in range(index * subs, (index + 1) * subs):
+            if own:
+                ref, lead = x_refs[piece], 0
+            elif len(x_refs) % 2:
+                ref, lead = x_refs[-1], piece
+            else:
+                ref, lead = x_refs[len(x_refs) // 2 + piece], 0
+            frames, _, antennas = ref.shape[1:]
+            block = ref[lead, :, at * ROWS : (at + 1) * ROWS, :]
             blocks.append(block.reshape(frames * ROWS, antennas))
     block = jnp.concatenate(blocks, axis=0)
     return jnp.dot(order_ref[...], block, preferred_element_type=jnp.float32).astype(jnp.bfloat16)
@@ -158,10 +164,10 @@
 
 def first_kernel(counts, place_ref, order_ref, re_ref, im_ref, *refs):
     later, subs, pols = counts
-    x_refs = [refs[sub * pols : (sub + 1) * pols] for sub in range(subs)]
+    x_refs = refs[: subs * pols]
     out_ref, re_kept, im_kept, re_held, im_held, sem, kept_sem = refs[subs * pols :]
     groups, group, antennas, _ = re_held.shape
-    frames = x_refs[0][0].shape[1]
+    frames = x_refs[0].shape[1]
     half = subs * pols * frames
 
     start = pl.multiple_of(place_ref[0] * antennas, antennas)
@@ -183,7 +189,7 @@
     for copy in keeps:
         copy.start()
     for at in range(groups):
-        rows = beam_rows(x_refs, at, pols, order_ref)
+        rows = beam_rows(x_refs, 0, subs, at, order_ref)
         for copy in copies[at]:
             copy.wait()
         for index in range(group):
@@ -203,18 +209,13 @@
         for lot in range(lots)
         for k in range(weight_refs[2 * lot].shape[0])
     ]
-    later = len(at_refs)
-    x_refs = [
-        [refs[(index * subs + sub) * pols :][:pols] for sub in range(subs)]
-        for index in range(later)
-    ]
-    out_ref, power_ref = refs[later * subs * pols :]
+    x_refs, (out_ref, power_ref) = refs[:-2], refs[-2:]
     channels = sum_ref.shape[0]
     group = ROWS // 2
-    frames = x_refs[0][0][0].shape[1]
+    frames = x_refs[0].shape[1]
     half = subs * pols * frames
     for at in range(channels // group):
-        rows = [beam_rows(refs, at, pols, order_ref) for refs in x_refs]
+        rows = [beam_rows(x_refs, k, subs, at, order_ref) for k in range(len(at_refs))]
         for index in range(group):
             channel = at * group + index
             weights = [[refs[part][channel] for refs in at_refs] for part in range(2)]
@@ -428,13 +429,15 @@
         offset = (offsets[k // subs] * subs + k % subs) * pols
         moved.append(exchange(piece, offset, OWNERS) if offset else piece)
 
-    def both(pieces):
-        return [part for mine in pieces for part in (mine, exchange(mine[1:], 1, ("pol",)))]
+    def both(pieces, join):
+        theirs = [piece[1:] for piece in pieces]
+        theirs = [jnp.concatenate(theirs)] if join else theirs
+        return [*pieces, *(exchange(part, 1, ("pol",)) for part in theirs)]
 
     first, _ = lax.optimization_barrier((moved[:subs], near[0]))
-    sums, *kept = first_beams(both(first), numbers(*at[:side]), weights, subs, pols)
+    sums, *kept = first_beams(both(first, False), numbers(*at[:side]), weights, subs, pols)
     rest, sums = lax.optimization_barrier((moved[subs:], sums))
-    total = beam_power(both(rest), numbers(sub), kept + near_kept, sums, wides, subs, pols)
+    total = beam_power(both(rest, True), numbers(sub), kept + near_kept, sums, wides, subs, pols)
     power = turn(total.reshape(owners, own, -1))
     return shift_and_add(power.reshape(owners * own, -1), delays, frames)
 

time: 53.9 us -> 53.2 us (0.987)
  starting transfers between devices: 14.7 us -> 13.1 us
  waiting for transfers between devices: 2.58 us -> 3.36 us
    ppermute x15 -> x10, starting transfers between devices: 14.7 us -> 13.1 us  [exchange(): return lax.ppermute(x, names, [(k, k ^ offset) for k in range(count)])]
    ppermute x15 -> x10, waiting for transfers between devices: 2.58 us -> 3.36 us  [exchange(): return lax.ppermute(x, names, [(k, k ^ offset) for k in range(count)])]
  transfers between devices with their start and end apart: 15 -> 10, of which waited for: 6 -> 3; matrix products, arithmetic and copies ran while one was open for 0% -> 0% of each run, Pallas kernels for 28% -> 28%
where the time goes in v5:
time: 53.2 us; the launch traced here: 53 us
  Pallas kernels  24 us (45%)
  starting transfers between devices  13.1 us (25%)
  blocking collectives  12.1 us (23%)
  waiting for transfers between devices  3.36 us (6%)
    ppermute x10, starting transfers between devices, exchange(): return lax.ppermute(x, names, [(k, k ^ offset) for k in range(count)])  13.1 us
    pallas_call x2, Pallas kernels, spectra(): pl.pallas_call(functools.partial(dft_kernel, (steps, subs, pols, len(weig...  12.5 us
    all_to_all x1, blocking collectives, local(): power = turn(total.reshape(owners, own, -1))  12.1 us
    pallas_call x1, Pallas kernels, first_beams(): pl.pallas_call(functools.partial(first_kernel, (later, subs, pols)), in_s...  6.51 us
    pallas_call x1, Pallas kernels, beam_power(): pl.pallas_call(functools.partial(last_kernel, (len(kept) // 2, subs, pols...  4.02 us
    ppermute x10, waiting for transfers between devices, exchange(): return lax.ppermute(x, names, [(k, k ^ offset) for k in range(count)])  3.36 us
  transfers between devices with their start and end apart: 10, of which 3 were waited for; matrix products, arithmetic and copies ran while one was open for 0% of the time, Pallas kernels for 28%

profile of v5, /device:TPU:0, one launch (start us, length us, event | category | flops | bytes accessed | tf_op | source)
XLA Modules:
  0.0 53.0 jit_solution(919305887237678942)
XLA Ops:
  0.0 0.1 pad_add_fusion.1.here_ref
  0.1 4.1 %spectra.2 = (bf16[2,2,64,256]{3,2,1,0:T(8,128)(2,1)S(1)}, bf16[2,2,64,256]{3,2,1,0:T(8,128)(2,1)S(1)}, bf16[2,256,2048]{2,1,0:T(8,128)(2,1)S(1)}) custom-call(s32[2]{0:T(128)S(1)} %pad_add_fusion.1.here_ref, bf16[4,512,2048]{2,1,0:T(8,128)(2,1)} %constant.24.clone.table_ref, bf16[1,256,2,2048]{3,2,1,0:T(2,128)(2,1)} %volt_ref.1), custom_call_target="tpu_custom_call" | custom-call | tf_op jit(solution)/shard_map/spectra/pallas_call | solution.py:124
  4.2 4.1 %collective-permute-start = (bf16[2,2,64,256]{3,2,1,0:T(8,128)(2,1)S(1)}, bf16[2,2,64,256]{3,2,1,0:T(8,128)(2,1)S(1)}, u32[]{:S(2)}, u32[]{:S(2)}) collective-permute-start(bf16[2,2,64,256]{3,2,1,0:T(8,128)(2,1)S(1)} %get-tuple-element.28), channel_id=1, source_target_pairs={{0,8},{1,9},{2,10},{3,11},{4,12},{5,13},{6,14},{7,15},{8,0},{9,1},... | collective-permute-start | bytes 393224 | tf_op jit(solution)/shard_map/ppermute | solution.py:305
  8.3 1.3 %collective-permute-start.1 = (bf16[2,2,64,256]{3,2,1,0:T(8,128)(2,1)S(1)}, bf16[2,2,64,256]{3,2,1,0:T(8,128)(2,1)S(1)}, u32[]{:S(2)}, u32[]{:S(2)}) collective-permute-start(bf16[2,2,64,256]{3,2,1,0:T(8,128)(2,1)S(1)} %get-tuple-element.29), channel_id=1, source_target_pairs={{0,10},{1,11},{2,8},{3,9},{4,14},{5,15},{6,12},{7,13},{8,2},{9,3},... | collective-permute-start | bytes 393224 | tf_op jit(solution)/shard_map/ppermute | solution.py:305
  9.6 0.1 pad_add_fusion.2.here_ref
  9.7 0.0 copy-start.1
  9.7 8.4 %spectra.3 = (bf16[2,2,64,256]{3,2,1,0:T(8,128)(2,1)S(1)}, bf16[2,2,64,256]{3,2,1,0:T(8,128)(2,1)S(1)}, bf16[2,2,64,256]{3,2,1,0:T(8,128)(2,1)S(1)}, bf16[2,2,64...) custom-call(s32[4]{0:T(128)S(1)} %pad_add_fusion.2.here_ref, ...), custom_call_target="tpu_custom_call" | custom-call | tf_op jit(solution)/shard_map/spectra/pallas_call | solution.py:124
  18.0 3.6 %collective-permute-start.5 = (bf16[2,2,64,256]{3,2,1,0:T(8,128)(2,1)S(1)}, bf16[2,2,64,256]{3,2,1,0:T(8,128)(2,1)S(1)}, u32[]{:S(2)}, u32[]{:S(2)}) collective-permute-start(bf16[2,2,64,256]{3,2,1,0:T(8,128)(2,1)S(1)} %get-tuple-element.38), channel_id=1, source_target_pairs={{0,14},{1,15},{2,12},{3,13},{4,10},{5,11},{6,8},{7,9},{8,6},{9,7},... | collective-permute-start | bytes 393224 | tf_op jit(solution)/shard_map/ppermute | solution.py:305
  21.7 0.0 collective-permute-start.6
  21.7 0.9 %collective-permute-start.4 = (bf16[2,2,64,256]{3,2,1,0:T(8,128)(2,1)S(1)}, bf16[2,2,64,256]{3,2,1,0:T(8,128)(2,1)S(1)}, u32[]{:S(2)}, u32[]{:S(2)}) collective-permute-start(bf16[2,2,64,256]{3,2,1,0:T(8,128)(2,1)S(1)} %get-tuple-element.31), channel_id=1, source_target_pairs={{0,12},{1,13},{2,14},{3,15},{4,8},{5,9},{6,10},{7,11},{8,4},{9,5},... | collective-permute-start | bytes 393224 | tf_op jit(solution)/shard_map/ppermute | solution.py:305
  22.6 0.0 collective-permute-done.refs_0_
  22.6 0.0 collective-permute-done.1.refs_1_
  22.6 0.1 collective-permute-start.3
  22.7 0.5 collective-permute-start.2
  23.2 0.1 pad_add_fusion.place_ref
  23.3 0.7 %collective-permute-done.3.refs_3_ = bf16[1,2,64,256]{3,2,1,0:T(8,128)(2,1)S(1)} collective-permute-done((bf16[1,2,64,256]{3,2,1,0:T(8,128)(2,1)S(1)}, bf16[1,2,64,256]{3,2,1,0:T(8,128)(2,1)S(1)}, u32[]{:S(2)}, u32[]{:S(2)}) %collective-permute-start.3) | collective-permute-done | bytes 65568 | tf_op jit(solution)/shard_map/ppermute | solution.py:305
  23.9 2.1 %collective-permute-start.7 = (bf16[2,2,64,256]{3,2,1,0:T(8,128)(2,1)S(1)}, bf16[2,2,64,256]{3,2,1,0:T(8,128)(2,1)S(1)}, u32[]{:S(2)}, u32[]{:S(2)}) collective-permute-start(bf16[2,2,64,256]{3,2,1,0:T(8,128)(2,1)S(1)} %get-tuple-element.40), channel_id=1, source_target_pairs={{0,6},{1,7},{2,4},{3,5},{4,2},{5,3},{6,0},{7,1},{8,14},{9,15},{10,... | collective-permute-start | bytes 393224 | tf_op jit(solution)/shard_map/ppermute | solution.py:305
  26.0 0.0 collective-permute-done.2.refs_2_
  26.0 0.5 %collective-permute-start.8 = (bf16[2,2,64,256]{3,2,1,0:T(8,128)(2,1)S(1)}, bf16[2,2,64,256]{3,2,1,0:T(8,128)(2,1)S(1)}, u32[]{:S(2)}, u32[]{:S(2)}) collective-permute-start(bf16[2,2,64,256]{3,2,1,0:T(8,128)(2,1)S(1)} %get-tuple-element.42), channel_id=1, source_target_pairs={{0,2},{1,3},{2,0},{3,1},{4,6},{5,7},{6,4},{7,5},{8,10},{9,11},{10,... | collective-permute-start | bytes 393224 | tf_op jit(solution)/shard_map/ppermute | solution.py:305
  26.5 0.0 copy-done.1
  26.5 6.5 %first_beams.1 = (f32[32,16,256]{2,1,0:T(8,128)S(1)}, bf16[1,32,256,256]{3,2,1,0:T(8,128)(2,1)S(1)}, bf16[1,32,256,256]{3,2,1,0:T(8,128)(2,1)S(1)}) custom-call(s32[2]{0:T(128)S(1)} %pad_add_fusion.place_ref, bf16[128,128]{1,0:T(8,128)(2,1)S(1)} %copy-done.1, bf16[32,1024,256]{2,1,0:T(8,128)(2,1)} %re_ref.1, bf16[32,1024,256]{2,1,0:T(8,128)(2,1)} %im_ref.1, ...), custom_call_target="tpu_custom_call" | custom-call | flops 40000000000 | bytes 400000000 | tf_op jit(solution)/shard_map/first_beams/pallas_call | solution.py:263
  33.1 0.0 collective-permute-done.5.refs_6_
  33.1 0.0 collective-permute-done.6.refs_7_
  33.1 1.0 %collective-permute-done.7.refs_8_ = bf16[2,2,64,256]{3,2,1,0:T(8,128)(2,1)S(1)} collective-permute-done((bf16[2,2,64,256]{3,2,1,0:T(8,128)(2,1)S(1)}, bf16[2,2,64,256]{3,2,1,0:T(8,128)(2,1)S(1)}, u32[]{:S(2)}, u32[]{:S(2)}) %collective-permute-start.7) | collective-permute-done | bytes 131104 | tf_op jit(solution)/shard_map/ppermute | solution.py:305
  34.0 0.0 collective-permute-done.8.refs_10_
  34.0 0.0 collective-permute-done.4.refs_5_
  34.1 0.1 collective-permute-start.9
  34.2 1.7 %collective-permute-done.9.refs_11_ = bf16[6,2,64,256]{3,2,1,0:T(8,128)(2,1)S(1)} collective-permute-done((bf16[6,2,64,256]{3,2,1,0:T(8,128)(2,1)S(1)}, bf16[6,2,64,256]{3,2,1,0:T(8,128)(2,1)S(1)}, u32[]{:S(2)}, u32[]{:S(2)}) %collective-permute-start.9) | collective-permute-done | bytes 393248 | tf_op jit(solution)/shard_map/ppermute | solution.py:305
  35.9 0.0 copy-start
  35.9 4.0 %beam_power.1 = bf16[8,2,32,128]{3,2,1,0:T(8,128)(2,1)S(1)} custom-call(s32[1]{0:T(128)} %bitcast.place_ref, bf16[128,128]{1,0:T(8,128)(2,1)S(1)} %copy-done.1, bf16[1,32,256,256]{3,2,1,0:T(8,128)(2,1)S(1)} %get-tuple-element.34.refs_0_, bf16[1,32,256,256]{3,2,1,0:T(8,128)(2,1)S(1)} %get-tuple-element.35.refs_1_, ...), custom_call_target="tpu_custom_call" | custom-call | tf_op jit(solution)/shard_map/beam_power/pallas_call | solution.py:286
  40.0 12.1 %all_to_all.5 = bf16[16,32,128]{2,1,0:T(8,128)(2,1)S(1)} all-to-all(bf16[16,32,128]{2,1,0:T(8,128)(2,1)S(1)} %bitcast.8), channel_id=1, replica_groups=mesh['group'=2,'wide_high'=2,'wide_low'=2,'sub'=2,'pol'=2] {'wide_high',..., dimensions={0} | all-to-all | bytes 262144 | tf_op jit(solution)/shard_map/all_to_all | solution.py:441
  52.0 0.0 copy-done
  52.0 1.0 %shift_and_add.1 = f32[32,4,64]{2,1,0:T(4,128)} custom-call(bf16[512,128]{1,0:T(8,128)(2,1)S(1)} %bitcast.9, s32[64,512]{1,0:T(8,128)S(1)} %copy-done), custom_call_target="tpu_custom_call" | custom-call | tf_op jit(solution)/shard_map/shift_and_add/pallas_call | solution.py:340
  (8 shorter events, 0.1 us)
Async XLA Ops:
  4.2 18.4 %collective-permute-start = (bf16[2,2,64,256]{3,2,1,0:T(8,128)(2,1)S(1)}, bf16[2,2,64,256]{3,2,1,0:T(8,128)(2,1)S(1)}, u32[]{:S(2)}, u32[]{:S(2)}) collective-permute-start(bf16[2,2,64,256]{3,2,1,0:T(8,128)(2,1)S(1)} %get-tuple-element.28), channel_id=1, source_target_pairs={{0,8},{1,9},{2,10},{3,11},{4,12},{5,13},{6,14},{7,15},{8,0},{9,1},... | collective-permute-start | bytes 393224 | tf_op jit(solution)/shard_map/ppermute | solution.py:305
  8.3 14.3 %collective-permute-start.1 = (bf16[2,2,64,256]{3,2,1,0:T(8,128)(2,1)S(1)}, bf16[2,2,64,256]{3,2,1,0:T(8,128)(2,1)S(1)}, u32[]{:S(2)}, u32[]{:S(2)}) collective-permute-start(bf16[2,2,64,256]{3,2,1,0:T(8,128)(2,1)S(1)} %get-tuple-element.29), channel_id=1, source_target_pairs={{0,10},{1,11},{2,8},{3,9},{4,14},{5,15},{6,12},{7,13},{8,2},{9,3},... | collective-permute-start | bytes 393224 | tf_op jit(solution)/shard_map/ppermute | solution.py:305
  9.7 16.9 %copy-start.1 = (bf16[128,128]{1,0:T(8,128)(2,1)S(1)}, bf16[128,128]{1,0:T(8,128)(2,1)}, u32[]{:S(2)}) copy-start(bf16[128,128]{1,0:T(8,128)(2,1)} %constant.25.clone.order_ref) | copy-start | bytes 98308
  18.0 15.0 %collective-permute-start.5 = (bf16[2,2,64,256]{3,2,1,0:T(8,128)(2,1)S(1)}, bf16[2,2,64,256]{3,2,1,0:T(8,128)(2,1)S(1)}, u32[]{:S(2)}, u32[]{:S(2)}) collective-permute-start(bf16[2,2,64,256]{3,2,1,0:T(8,128)(2,1)S(1)} %get-tuple-element.38), channel_id=1, source_target_pairs={{0,14},{1,15},{2,12},{3,13},{4,10},{5,11},{6,8},{7,9},{8,6},{9,7},... | collective-permute-start | bytes 393224 | tf_op jit(solution)/shard_map/ppermute | solution.py:305
  21.7 11.4 %collective-permute-start.6 = (bf16[2,2,64,256]{3,2,1,0:T(8,128)(2,1)S(1)}, bf16[2,2,64,256]{3,2,1,0:T(8,128)(2,1)S(1)}, u32[]{:S(2)}, u32[]{:S(2)}) collective-permute-start(bf16[2,2,64,256]{3,2,1,0:T(8,128)(2,1)S(1)} %get-tuple-element.39), channel_id=1, source_target_pairs={{0,4},{1,5},{2,6},{3,7},{4,0},{5,1},{6,2},{7,3},{8,12},{9,13},{10,... | collective-permute-start | bytes 393224 | tf_op jit(solution)/shard_map/ppermute | solution.py:305
  21.7 12.4 %collective-permute-start.4 = (bf16[2,2,64,256]{3,2,1,0:T(8,128)(2,1)S(1)}, bf16[2,2,64,256]{3,2,1,0:T(8,128)(2,1)S(1)}, u32[]{:S(2)}, u32[]{:S(2)}) collective-permute-start(bf16[2,2,64,256]{3,2,1,0:T(8,128)(2,1)S(1)} %get-tuple-element.31), channel_id=1, source_target_pairs={{0,12},{1,13},{2,14},{3,15},{4,8},{5,9},{6,10},{7,11},{8,4},{9,5},... | collective-permute-start | bytes 393224 | tf_op jit(solution)/shard_map/ppermute | solution.py:305
  22.6 1.3 %collective-permute-start.3 = (bf16[1,2,64,256]{3,2,1,0:T(8,128)(2,1)S(1)}, bf16[1,2,64,256]{3,2,1,0:T(8,128)(2,1)S(1)}, u32[]{:S(2)}, u32[]{:S(2)}) collective-permute-start(bf16[1,2,64,256]{3,2,1,0:T(8,128)(2,1)S(1)} %slice.25), channel_id=1, source_target_pairs={{0,1},{1,0},{2,3},{3,2},{4,5},{5,4},{6,7},{7,6},{8,9},{9,8},{10,11... | collective-permute-start | bytes 196616 | tf_op jit(solution)/shard_map/ppermute | solution.py:305
  22.7 3.3 %collective-permute-start.2 = (bf16[1,2,64,256]{3,2,1,0:T(8,128)(2,1)S(1)}, bf16[1,2,64,256]{3,2,1,0:T(8,128)(2,1)S(1)}, u32[]{:S(2)}, u32[]{:S(2)}) collective-permute-start(bf16[1,2,64,256]{3,2,1,0:T(8,128)(2,1)S(1)} %slice.24), channel_id=1, source_target_pairs={{0,1},{1,0},{2,3},{3,2},{4,5},{5,4},{6,7},{7,6},{8,9},{9,8},{10,11... | collective-permute-start | bytes 196616 | tf_op jit(solution)/shard_map/ppermute | solution.py:305
  23.9 10.1 %collective-permute-start.7 = (bf16[2,2,64,256]{3,2,1,0:T(8,128)(2,1)S(1)}, bf16[2,2,64,256]{3,2,1,0:T(8,128)(2,1)S(1)}, u32[]{:S(2)}, u32[]{:S(2)}) collective-permute-start(bf16[2,2,64,256]{3,2,1,0:T(8,128)(2,1)S(1)} %get-tuple-element.40), channel_id=1, source_target_pairs={{0,6},{1,7},{2,4},{3,5},{4,2},{5,3},{6,0},{7,1},{8,14},{9,15},{10,... | collective-permute-start | bytes 393224 | tf_op jit(solution)/shard_map/ppermute | solution.py:305
  26.0 8.0 %collective-permute-start.8 = (bf16[2,2,64,256]{3,2,1,0:T(8,128)(2,1)S(1)}, bf16[2,2,64,256]{3,2,1,0:T(8,128)(2,1)S(1)}, u32[]{:S(2)}, u32[]{:S(2)}) collective-permute-start(bf16[2,2,64,256]{3,2,1,0:T(8,128)(2,1)S(1)} %get-tuple-element.42), channel_id=1, source_target_pairs={{0,2},{1,3},{2,0},{3,1},{4,6},{5,7},{6,4},{7,5},{8,10},{9,11},{10,... | collective-permute-start | bytes 393224 | tf_op jit(solution)/shard_map/ppermute | solution.py:305
  34.1 1.8 %collective-permute-start.9 = (bf16[6,2,64,256]{3,2,1,0:T(8,128)(2,1)S(1)}, bf16[6,2,64,256]{3,2,1,0:T(8,128)(2,1)S(1)}, u32[]{:S(2)}, u32[]{:S(2)}) collective-permute-start(bf16[6,2,64,256]{3,2,1,0:T(8,128)(2,1)S(1)} %slice_dynamic-update-slice_fusion), channel_id=1, source_target_pairs={{0,1},{1,0},{2,3},{3,2},{4,5},{5,4},{6,7},{7,6},{8,9},{9,8},{10,11... | collective-permute-start | bytes 1179656 | tf_op jit(solution)/shard_map/ppermute | solution.py:305
  35.9 16.1 %copy-start = (s32[64,512]{1,0:T(8,128)S(1)}, s32[64,512]{1,0:T(8,128)}, u32[]{:S(2)}) copy-start(s32[64,512]{1,0:T(8,128)} %delay_ref.1) | copy-start | bytes 393220

commit v6 on v5

--- a/solution.py
+++ b/solution.py
@@ -12,6 +12,7 @@
 
 OWNERS = ("wide_high", "wide_low", "sub", "pol")
 ROWS = 16
+LOTS = 4
 COST = pl.CostEstimate(flops=0, bytes_accessed=0, transcendentals=0)
 
 
@@ -29,14 +30,19 @@
 def keep_weights(place_ref, first, refs, kept_refs, sem):
     copies = []
     for part, (ref, kept) in enumerate(zip(refs, kept_refs)):
-        antennas = kept.shape[2]
-        for index in range(kept.shape[0]):
+        count, channels, antennas, _ = kept.shape
+        lots = sem.shape[2]
+        for index in range(count):
             start = pl.multiple_of(place_ref[first + index] * antennas, antennas)
-            copies.append(
-                pltpu.make_async_copy(
-                    ref.at[:, pl.ds(start, antennas), :], kept.at[index], sem.at[part, index]
+            for lot in range(lots):
+                some = pl.ds(lot * (channels // lots), channels // lots)
+                copies.append(
+                    pltpu.make_async_copy(
+                        ref.at[some, pl.ds(start, antennas), :],
+                        kept.at[index, some],
+                        sem.at[part, index, lot],
+                    )
                 )
-            )
     return copies
 
 
@@ -119,7 +125,7 @@
         scratch.append(pltpu.SemaphoreType.DMA((4,)))
         volts = pltpu.with_memory_space_constraint(volts, pltpu.HBM)
     else:
-        scratch.append(pltpu.SemaphoreType.DMA((2, keep)))
+        scratch.append(pltpu.SemaphoreType.DMA((2, keep, LOTS)))
         volts = pltpu.with_memory_space_constraint(volts, pltpu.VMEM)
     outs = pl.pallas_call(
         functools.partial(dft_kernel, (steps, subs, pols, len(weights), first)),
@@ -162,63 +168,50 @@
     return by_re[:half] - by_im[half:], by_im[:half] + by_re[half:]
 
 
-def first_kernel(counts, place_ref, order_ref, re_ref, im_ref, *refs):
-    later, subs, pols = counts
-    x_refs = refs[: subs * pols]
-    out_ref, re_kept, im_kept, re_held, im_held, sem, kept_sem = refs[subs * pols :]
+def antenna_lines(place_ref, index, antennas):
+    return pl.ds(pl.multiple_of(place_ref[index] * antennas, antennas), antennas)
+
+
+def first_kernel(subs, place_ref, order_ref, re_ref, im_ref, *refs):
+    x_refs, (out_ref, re_kept, re_held, sem, kept_sem) = refs[:-5], refs[-5:]
     groups, group, antennas, _ = re_held.shape
-    frames = x_refs[0].shape[1]
-    half = subs * pols * frames
-
-    start = pl.multiple_of(place_ref[0] * antennas, antennas)
+    half = out_ref.shape[1] // 2
+    own = antenna_lines(place_ref, 0, antennas)
     copies = [
-        [
-            pltpu.make_async_copy(
-                ref.at[pl.ds(at * group, group), pl.ds(start, antennas), :],
-                held.at[at],
-                sem.at[part, at],
-            )
-            for part, (ref, held) in enumerate(((re_ref, re_held), (im_ref, im_held)))
-        ]
+        pltpu.make_async_copy(
+            re_ref.at[pl.ds(at * group, group), own, :], re_held.at[at], sem.at[at]
+        )
         for at in range(groups)
     ]
-    keeps = keep_weights(place_ref, 1, (re_ref, im_ref), (re_kept, im_kept), kept_sem)
-    for pair in copies:
-        for copy in pair:
-            copy.start()
-    for copy in keeps:
+    keeps = keep_weights(place_ref, 1, (re_ref,), (re_kept,), kept_sem)
+    for copy in copies + keeps:
         copy.start()
     for at in range(groups):
         rows = beam_rows(x_refs, 0, subs, at, order_ref)
-        for copy in copies[at]:
-            copy.wait()
+        copies[at].wait()
         for index in range(group):
+            channel = at * group + index
             line = rows[index * 2 * half : (index + 1) * 2 * half]
-            beams = beam_part([line], half, ([re_held[at, index]], [im_held[at, index]]))
-            out_ref[at * group + index, :half] = beams[0]
-            out_ref[at * group + index, half:] = beams[1]
+            weights = [re_held[at, index]], [im_ref[channel, place_ref[0]]]
+            out_ref[channel, :half], out_ref[channel, half:] = beam_part([line], half, weights)
     for copy in keeps:
         copy.wait()
 
 
-def last_kernel(counts, place_ref, order_ref, *refs):
-    lots, subs, pols = counts
-    weight_refs, sum_ref, refs = refs[: 2 * lots], refs[2 * lots], refs[2 * lots + 1 :]
-    at_refs = [
-        tuple(ref.at[k] for ref in weight_refs[2 * lot : 2 * lot + 2])
-        for lot in range(lots)
-        for k in range(weight_refs[2 * lot].shape[0])
-    ]
+def last_kernel(subs, lots, place_ref, order_ref, *refs):
+    kept_refs, im_ref, sum_ref, refs = refs[:lots], refs[lots], refs[lots + 1], refs[lots + 2 :]
     x_refs, (out_ref, power_ref) = refs[:-2], refs[-2:]
-    channels = sum_ref.shape[0]
+    re_refs = [ref.at[k] for ref in kept_refs for k in range(ref.shape[0])]
+    channels, half = sum_ref.shape[0], sum_ref.shape[1] // 2
+    frames = x_refs[0].shape[1]
+    pols = half // (subs * frames)
     group = ROWS // 2
-    frames = x_refs[0].shape[1]
-    half = subs * pols * frames
+    owns = [place_ref[1 + k] for k in range(len(re_refs))]
     for at in range(channels // group):
-        rows = [beam_rows(x_refs, k, subs, at, order_ref) for k in range(len(at_refs))]
+        rows = [beam_rows(x_refs, k, subs, at, order_ref) for k in range(len(re_refs))]
         for index in range(group):
             channel = at * group + index
-            weights = [[refs[part][channel] for refs in at_refs] for part in range(2)]
+            weights = [ref[channel] for ref in re_refs], [im_ref[channel, own] for own in owns]
             lines = [row[index * 2 * half : (index + 1) * 2 * half] for row in rows]
             beam_re, beam_im = beam_part(lines, half, weights)
             beam_re = beam_re + sum_ref[channel, :half]
@@ -250,51 +243,52 @@
     return jnp.asarray(order, jnp.bfloat16)
 
 
-def first_beams(xs, place, weights, subs, pols):
+def first_beams(xs, place, real_weight, imaginary_weight, subs, pols):
     _, frames, _, antennas = xs[0].shape
-    channels, _, beams = weights[0].shape
+    channels, _, beams = real_weight.shape
     group = ROWS // 2
     later = place.shape[0] - 1
     vmem = pl.BlockSpec(memory_space=pltpu.VMEM)
     hbm = pl.BlockSpec(memory_space=pltpu.HBM)
-    kept = pltpu.VMEM((later, channels, antennas, beams), jnp.bfloat16)
+    kept = pltpu.VMEM((later, channels, antennas, beams), real_weight.dtype)
     sums = jax.ShapeDtypeStruct((channels, 2 * subs * pols * frames, beams), jnp.float32)
-    held = pltpu.VMEM((channels // group, group, antennas, beams), jnp.bfloat16)
     return pl.pallas_call(
-        functools.partial(first_kernel, (later, subs, pols)),
-        in_specs=[pl.BlockSpec(memory_space=pltpu.SMEM), vmem, hbm, hbm] + [vmem] * len(xs),
-        out_specs=[vmem] * 3,
-        out_shape=[sums, kept, kept],
+        functools.partial(first_kernel, subs),
+        in_specs=[pl.BlockSpec(memory_space=pltpu.SMEM), vmem, hbm] + [vmem] * (1 + len(xs)),
+        out_specs=[vmem] * 2,
+        out_shape=[sums, kept],
         scratch_shapes=[
-            held,
-            held,
-            pltpu.SemaphoreType.DMA((2, channels // group)),
-            pltpu.SemaphoreType.DMA((2, later)),
+            pltpu.VMEM((channels // group, group, antennas, beams), real_weight.dtype),
+            pltpu.SemaphoreType.DMA((channels // group,)),
+            pltpu.SemaphoreType.DMA((1, later, LOTS)),
         ],
-        compiler_params=pltpu.CompilerParams(vmem_limit_bytes=12 * 2**20),
-        cost_estimate=pl.CostEstimate(flops=4*10**10, bytes_accessed=4*10**8, transcendentals=0),
+        compiler_params=pltpu.CompilerParams(vmem_limit_bytes=8 * 2**20),
+        cost_estimate=pl.CostEstimate(
+            flops=4 * 10**10, bytes_accessed=4 * 10**8, transcendentals=0
+        ),
         name="first_beams",
-    )(place, sorting(subs, pols, frames), *weights, *xs)
-
-
-def beam_power(xs, place, kept, sums, wides, subs, pols):
+    )(place, sorting(subs, pols, frames), real_weight, imaginary_weight, *xs)
+
+
+def beam_power(xs, place, kept, imaginary_weight, sums, wides, subs, pols):
     frames = xs[0].shape[1]
-    _, channels, _, beams = kept[0].shape
+    channels, _, beams = sums.shape
     targets = wides * subs
     width = subs * frames * (beams // targets)
     vmem = pl.BlockSpec(memory_space=pltpu.VMEM)
     return pl.pallas_call(
-        functools.partial(last_kernel, (len(kept) // 2, subs, pols)),
-        in_specs=[pl.BlockSpec(memory_space=pltpu.SMEM)] + [vmem] * (2 + len(kept) + len(xs)),
+        functools.partial(last_kernel, subs, len(kept)),
+        in_specs=[pl.BlockSpec(memory_space=pltpu.SMEM)] + [vmem] * (3 + len(kept) + len(xs)),
         out_specs=vmem,
         out_shape=jax.ShapeDtypeStruct((targets, pols, channels, width), jnp.bfloat16),
         scratch_shapes=[pltpu.VMEM((subs * frames, channels, beams), jnp.float32)],
-        compiler_params=pltpu.CompilerParams(vmem_limit_bytes=8 * 2**20),
+        compiler_params=pltpu.CompilerParams(vmem_limit_bytes=4 * 2**20),
         name="beam_power",
     )(
         place,
         sorting(subs, pols, frames),
         *(pltpu.with_memory_space_constraint(part, pltpu.VMEM) for part in kept),
+        imaginary_weight,
         sums,
         *xs,
     )
@@ -409,10 +403,7 @@
     side, core = lax.axis_size("wide_low"), sub * pols + pol
     table = jnp.asarray(dft_table(voltages.shape[3], own * owners, wides, owners))
     table = pltpu.with_memory_space_constraint(table, pltpu.HBM)
-    weights = [
-        pltpu.with_memory_space_constraint(weight, pltpu.HBM)
-        for weight in (real_weight, imaginary_weight)
-    ]
+    real_weight = pltpu.with_memory_space_constraint(real_weight, pltpu.HBM)
 
     def numbers(*values):
         return jnp.stack(values).astype(jnp.int32)
@@ -421,8 +412,11 @@
     offsets = list(range(side, wides)) + list(range(side))[::-1]
     at = [wide ^ offset for offset in offsets]
     far, (volts,) = spectra(voltages, table, numbers(at[0], core), 1, subs, pols)
+    imaginary_weight = imaginary_weight.reshape(own, wides, -1, beams)
+    imaginary_weight, _ = lax.optimization_barrier((imaginary_weight, far[0]))
+    imaginary_weight = pltpu.with_memory_space_constraint(imaginary_weight, pltpu.VMEM)
     near, near_kept = spectra(
-        volts, table, numbers(*at[1:], core), wides - 1, subs, pols, weights, side
+        volts, table, numbers(*at[1:], core), wides - 1, subs, pols, [real_weight], side
     )
     moved = []
     for k, piece in enumerate(far + near):
@@ -435,9 +429,23 @@
         return [*pieces, *(exchange(part, 1, ("pol",)) for part in theirs)]
 
     first, _ = lax.optimization_barrier((moved[:subs], near[0]))
-    sums, *kept = first_beams(both(first, False), numbers(*at[:side]), weights, subs, pols)
-    rest, sums = lax.optimization_barrier((moved[subs:], sums))
-    total = beam_power(both(rest, True), numbers(sub), kept + near_kept, sums, wides, subs, pols)
+    sums, kept = first_beams(
+        both(first, False), numbers(*at[:side]), real_weight, imaginary_weight, subs, pols
+    )
+    rest = moved[subs:]
+    longest = rest.pop(2 * subs - 1)
+    longest, rest, sums = lax.optimization_barrier((longest, rest, sums))
+    rest.insert(2 * subs - 1, longest)
+    total = beam_power(
+        both(rest, True),
+        numbers(sub, *at[1:]),
+        [kept] + near_kept,
+        imaginary_weight,
+        sums,
+        wides,
+        subs,
+        pols,
+    )
     power = turn(total.reshape(owners, own, -1))
     return shift_and_add(power.reshape(owners * own, -1), delays, frames)
 

time: 53.2 us -> 52.6 us (0.989)
  Pallas kernels: 24 us -> 21.8 us
  waiting for transfers between devices: 3.36 us -> 5.44 us
    ppermute x10, waiting for transfers between devices: 3.36 us -> 5.44 us  [exchange(): return lax.ppermute(x, names, [(k, k ^ offset) for k in range(count)])]
    pallas_call x2, Pallas kernels: 10.5 us -> 8.64 us  [the longest x1 4.52 us: beam_power(): pl.pallas_call(functools.partial(last_kernel, subs, len(kept)), in_specs=...]
  transfers between devices with their start and end apart: 10 -> 10, of which waited for: 3 -> 4; matrix products, arithmetic and copies ran while one was open for 0% -> 0% of each run, Pallas kernels for 28% -> 23%
where the time goes in v6:
time: 52.6 us; the launch traced here: 52.5 us
  Pallas kernels  21.8 us (41%)
  starting transfers between devices  13 us (25%)
  blocking collectives  11.8 us (22%)
  waiting for transfers between devices  5.44 us (10%)
    ppermute x10, starting transfers between devices, exchange(): return lax.ppermute(x, names, [(k, k ^ offset) for k in range(count)])  13 us
    pallas_call x2, Pallas kernels, spectra(): pl.pallas_call(functools.partial(dft_kernel, (steps, subs, pols, len(weig...  12.2 us
    all_to_all x1, blocking collectives, local(): power = turn(total.reshape(owners, own, -1))  11.8 us
    ppermute x10, waiting for transfers between devices, exchange(): return lax.ppermute(x, names, [(k, k ^ offset) for k in range(count)])  5.44 us
    pallas_call x1, Pallas kernels, beam_power(): pl.pallas_call(functools.partial(last_kernel, subs, len(kept)), in_specs=...  4.52 us
    pallas_call x1, Pallas kernels, first_beams(): pl.pallas_call(functools.partial(first_kernel, subs), in_specs=[pl.BlockS...  4.13 us
  transfers between devices with their start and end apart: 10, of which 4 were waited for; matrix products, arithmetic and copies ran while one was open for 0% of the time, Pallas kernels for 23%

profile of v6, /device:TPU:0, one launch (start us, length us, event | category | flops | bytes accessed | tf_op | source)
XLA Modules:
  0.0 52.5 jit_solution(6920799416086250129)
XLA Ops:
  0.0 0.1 pad_add_fusion.2.here_ref
  0.1 4.1 %spectra.2 = (bf16[2,2,64,256]{3,2,1,0:T(8,128)(2,1)S(1)}, bf16[2,2,64,256]{3,2,1,0:T(8,128)(2,1)S(1)}, bf16[2,256,2048]{2,1,0:T(8,128)(2,1)S(1)}) custom-call(s32[2]{0:T(128)S(1)} %pad_add_fusion.2.here_ref, bf16[4,512,2048]{2,1,0:T(8,128)(2,1)} %constant.24.clone.table_ref, bf16[1,256,2,2048]{3,2,1,0:T(2,128)(2,1)} %volt_ref.1), custom_call_target="tpu_custom_call" | custom-call | tf_op jit(solution)/shard_map/spectra/pallas_call | solution.py:130
  4.2 5.0 %collective-permute-start.1 = (bf16[2,2,64,256]{3,2,1,0:T(8,128)(2,1)S(1)}, bf16[2,2,64,256]{3,2,1,0:T(8,128)(2,1)S(1)}, u32[]{:S(2)}, u32[]{:S(2)}) collective-permute-start(bf16[2,2,64,256]{3,2,1,0:T(8,128)(2,1)S(1)} %get-tuple-element.29), channel_id=1, source_target_pairs={{0,10},{1,11},{2,8},{3,9},{4,14},{5,15},{6,12},{7,13},{8,2},{9,3},... | collective-permute-start | bytes 393224 | tf_op jit(solution)/shard_map/ppermute | solution.py:299
  9.2 0.3 collective-permute-start
  9.6 0.1 pad_add_fusion.3.here_ref
  9.7 0.0 copy-start
  9.7 0.0 copy-start.2
  9.7 8.0 %spectra.3 = (bf16[2,2,64,256]{3,2,1,0:T(8,128)(2,1)S(1)}, bf16[2,2,64,256]{3,2,1,0:T(8,128)(2,1)S(1)}, bf16[2,2,64,256]{3,2,1,0:T(8,128)(2,1)S(1)}, bf16[2,2,64...) custom-call(s32[4]{0:T(128)S(1)} %pad_add_fusion.3.here_ref, ...), custom_call_target="tpu_custom_call" | custom-call | tf_op jit(solution)/shard_map/spectra/pallas_call | solution.py:130
  17.7 1.6 %collective-permute-start.4 = (bf16[2,2,64,256]{3,2,1,0:T(8,128)(2,1)S(1)}, bf16[2,2,64,256]{3,2,1,0:T(8,128)(2,1)S(1)}, u32[]{:S(2)}, u32[]{:S(2)}) collective-permute-start(bf16[2,2,64,256]{3,2,1,0:T(8,128)(2,1)S(1)} %get-tuple-element.36), channel_id=1, source_target_pairs={{0,6},{1,7},{2,4},{3,5},{4,2},{5,3},{6,0},{7,1},{8,14},{9,15},{10,... | collective-permute-start | bytes 393224 | tf_op jit(solution)/shard_map/ppermute | solution.py:299
  19.3 3.4 %collective-permute-start.6 = (bf16[2,2,64,256]{3,2,1,0:T(8,128)(2,1)S(1)}, bf16[2,2,64,256]{3,2,1,0:T(8,128)(2,1)S(1)}, u32[]{:S(2)}, u32[]{:S(2)}) collective-permute-start(bf16[2,2,64,256]{3,2,1,0:T(8,128)(2,1)S(1)} %get-tuple-element.37), channel_id=1, source_target_pairs={{0,14},{1,15},{2,12},{3,13},{4,10},{5,11},{6,8},{7,9},{8,6},{9,7},... | collective-permute-start | bytes 393224 | tf_op jit(solution)/shard_map/ppermute | solution.py:299
  22.7 1.3 %collective-permute-start.5 = (bf16[2,2,64,256]{3,2,1,0:T(8,128)(2,1)S(1)}, bf16[2,2,64,256]{3,2,1,0:T(8,128)(2,1)S(1)}, u32[]{:S(2)}, u32[]{:S(2)}) collective-permute-start(bf16[2,2,64,256]{3,2,1,0:T(8,128)(2,1)S(1)} %get-tuple-element.31), channel_id=1, source_target_pairs={{0,12},{1,13},{2,14},{3,15},{4,8},{5,9},{6,10},{7,11},{8,4},{9,5},... | collective-permute-start | bytes 393224 | tf_op jit(solution)/shard_map/ppermute | solution.py:299
  24.1 0.0 collective-permute-done.1.refs_1_
  24.1 0.0 collective-permute-done.refs_0_
  24.1 0.1 collective-permute-start.3
  24.2 0.5 collective-permute-start.2
  24.7 0.1 pad_add_fusion.1.place_ref
  24.7 0.7 %collective-permute-done.3.refs_3_ = bf16[1,2,64,256]{3,2,1,0:T(8,128)(2,1)S(1)} collective-permute-done((bf16[1,2,64,256]{3,2,1,0:T(8,128)(2,1)S(1)}, bf16[1,2,64,256]{3,2,1,0:T(8,128)(2,1)S(1)}, u32[]{:S(2)}, u32[]{:S(2)}) %collective-permute-start.3) | collective-permute-done | bytes 65568 | tf_op jit(solution)/shard_map/ppermute | solution.py:299
  25.4 0.0 collective-permute-start.7
  25.4 0.2 collective-permute-done.2.refs_2_
  25.6 0.6 %collective-permute-start.8 = (bf16[2,2,64,256]{3,2,1,0:T(8,128)(2,1)S(1)}, bf16[2,2,64,256]{3,2,1,0:T(8,128)(2,1)S(1)}, u32[]{:S(2)}, u32[]{:S(2)}) collective-permute-start(bf16[2,2,64,256]{3,2,1,0:T(8,128)(2,1)S(1)} %get-tuple-element.40), channel_id=1, source_target_pairs={{0,2},{1,3},{2,0},{3,1},{4,6},{5,7},{6,4},{7,5},{8,10},{9,11},{10,... | collective-permute-start | bytes 393224 | tf_op jit(solution)/shard_map/ppermute | solution.py:299
  26.1 0.0 copy-done
  26.1 0.0 copy-done.2
  26.1 4.1 %first_beams.1 = (f32[32,16,256]{2,1,0:T(8,128)S(1)}, bf16[1,32,256,256]{3,2,1,0:T(8,128)(2,1)S(1)}) custom-call(s32[2]{0:T(128)S(1)} %pad_add_fusion.1.place_ref, bf16[128,128]{1,0:T(8,128)(2,1)S(1)} %copy-done.2, bf16[32,1024,256]{2,1,0:T(8,128)(2,1)} %re_ref.1, bf16[32,4,256,256]{3,2,1,0:T(8,128)(2,1)S(1)} %bitcast.9, ...), custom_call_target="tpu_custom_call" | custom-call | flops 40000000000 | bytes 400000000 | tf_op jit(solution)/shard_map/first_beams/pallas_call | solution.py:255
  30.3 0.0 collective-permute-done.4.refs_7_
  30.3 0.0 collective-permute-done.6.refs_5_
  30.3 3.0 %collective-permute-done.7.refs_6_ = bf16[2,2,64,256]{3,2,1,0:T(8,128)(2,1)S(1)} collective-permute-done((bf16[2,2,64,256]{3,2,1,0:T(8,128)(2,1)S(1)}, bf16[2,2,64,256]{3,2,1,0:T(8,128)(2,1)S(1)}, u32[]{:S(2)}, u32[]{:S(2)}) %collective-permute-start.7) | collective-permute-done | bytes 131104 | tf_op jit(solution)/shard_map/ppermute | solution.py:299
  33.3 0.0 collective-permute-done.8.refs_9_
  33.3 0.0 collective-permute-done.5.refs_4_
  33.4 0.1 collective-permute-start.9
  33.5 0.1 pad_add_fusion.place_ref
  33.6 1.6 %collective-permute-done.9.refs_10_ = bf16[6,2,64,256]{3,2,1,0:T(8,128)(2,1)S(1)} collective-permute-done((bf16[6,2,64,256]{3,2,1,0:T(8,128)(2,1)S(1)}, bf16[6,2,64,256]{3,2,1,0:T(8,128)(2,1)S(1)}, u32[]{:S(2)}, u32[]{:S(2)}) %collective-permute-start.9) | collective-permute-done | bytes 393248 | tf_op jit(solution)/shard_map/ppermute | solution.py:299
  35.2 0.0 copy-start.1
  35.2 4.5 %beam_power.1 = bf16[8,2,32,128]{3,2,1,0:T(8,128)(2,1)S(1)} custom-call(s32[4]{0:T(128)S(1)} %pad_add_fusion.place_ref, bf16[128,128]{1,0:T(8,128)(2,1)S(1)} %copy-done.2, bf16[1,32,256,256]{3,2,1,0:T(8,128)(2,1)S(1)} %get-tuple-element.34.refs_0_, bf16[2,32,256,256]{3,2,1,0:T(8,128)(2,1)S(1)} %get-tuple-element.35.refs_1_, ...), custom_call_target="tpu_custom_call" | custom-call | tf_op jit(solution)/shard_map/beam_power/pallas_call | solution.py:279
  39.7 11.8 %all_to_all.5 = bf16[16,32,128]{2,1,0:T(8,128)(2,1)S(1)} all-to-all(bf16[16,32,128]{2,1,0:T(8,128)(2,1)S(1)} %bitcast.11), channel_id=1, replica_groups=mesh['group'=2,'wide_high'=2,'wide_low'=2,'sub'=2,'pol'=2] {'wide_high',..., dimensions={0} | all-to-all | bytes 262144 | tf_op jit(solution)/shard_map/all_to_all | solution.py:449
  51.5 0.0 copy-done.1
  51.5 1.0 %shift_and_add.1 = f32[32,4,64]{2,1,0:T(4,128)} custom-call(bf16[512,128]{1,0:T(8,128)(2,1)S(1)} %bitcast.12, s32[64,512]{1,0:T(8,128)S(1)} %copy-done.1), custom_call_target="tpu_custom_call" | custom-call | tf_op jit(solution)/shard_map/shift_and_add/pallas_call | solution.py:334
  (8 shorter events, 0.1 us)
Async XLA Ops:
  4.2 19.9 %collective-permute-start.1 = (bf16[2,2,64,256]{3,2,1,0:T(8,128)(2,1)S(1)}, bf16[2,2,64,256]{3,2,1,0:T(8,128)(2,1)S(1)}, u32[]{:S(2)}, u32[]{:S(2)}) collective-permute-start(bf16[2,2,64,256]{3,2,1,0:T(8,128)(2,1)S(1)} %get-tuple-element.29), channel_id=1, source_target_pairs={{0,10},{1,11},{2,8},{3,9},{4,14},{5,15},{6,12},{7,13},{8,2},{9,3},... | collective-permute-start | bytes 393224 | tf_op jit(solution)/shard_map/ppermute | solution.py:299
  9.2 14.8 %collective-permute-start = (bf16[2,2,64,256]{3,2,1,0:T(8,128)(2,1)S(1)}, bf16[2,2,64,256]{3,2,1,0:T(8,128)(2,1)S(1)}, u32[]{:S(2)}, u32[]{:S(2)}) collective-permute-start(bf16[2,2,64,256]{3,2,1,0:T(8,128)(2,1)S(1)} %get-tuple-element.27), channel_id=1, source_target_pairs={{0,8},{1,9},{2,10},{3,11},{4,12},{5,13},{6,14},{7,15},{8,0},{9,1},... | collective-permute-start | bytes 393224 | tf_op jit(solution)/shard_map/ppermute | solution.py:299
  9.7 16.5 %copy-start = (bf16[32,1024,256]{2,1,0:T(8,128)(2,1)S(1)}, bf16[32,1024,256]{2,1,0:T(8,128)(2,1)}, u32[]{:S(2)}) copy-start(bf16[32,1024,256]{2,1,0:T(8,128)(2,1)} %param.9) | copy-start | bytes 50331652
  9.7 16.5 %copy-start.2 = (bf16[128,128]{1,0:T(8,128)(2,1)S(1)}, bf16[128,128]{1,0:T(8,128)(2,1)}, u32[]{:S(2)}) copy-start(bf16[128,128]{1,0:T(8,128)(2,1)} %constant.25.clone.order_ref) | copy-start | bytes 98308
  17.7 12.6 %collective-permute-start.4 = (bf16[2,2,64,256]{3,2,1,0:T(8,128)(2,1)S(1)}, bf16[2,2,64,256]{3,2,1,0:T(8,128)(2,1)S(1)}, u32[]{:S(2)}, u32[]{:S(2)}) collective-permute-start(bf16[2,2,64,256]{3,2,1,0:T(8,128)(2,1)S(1)} %get-tuple-element.36), channel_id=1, source_target_pairs={{0,6},{1,7},{2,4},{3,5},{4,2},{5,3},{6,0},{7,1},{8,14},{9,15},{10,... | collective-permute-start | bytes 393224 | tf_op jit(solution)/shard_map/ppermute | solution.py:299
  19.3 11.0 %collective-permute-start.6 = (bf16[2,2,64,256]{3,2,1,0:T(8,128)(2,1)S(1)}, bf16[2,2,64,256]{3,2,1,0:T(8,128)(2,1)S(1)}, u32[]{:S(2)}, u32[]{:S(2)}) collective-permute-start(bf16[2,2,64,256]{3,2,1,0:T(8,128)(2,1)S(1)} %get-tuple-element.37), channel_id=1, source_target_pairs={{0,14},{1,15},{2,12},{3,13},{4,10},{5,11},{6,8},{7,9},{8,6},{9,7},... | collective-permute-start | bytes 393224 | tf_op jit(solution)/shard_map/ppermute | solution.py:299
  22.7 10.6 %collective-permute-start.5 = (bf16[2,2,64,256]{3,2,1,0:T(8,128)(2,1)S(1)}, bf16[2,2,64,256]{3,2,1,0:T(8,128)(2,1)S(1)}, u32[]{:S(2)}, u32[]{:S(2)}) collective-permute-start(bf16[2,2,64,256]{3,2,1,0:T(8,128)(2,1)S(1)} %get-tuple-element.31), channel_id=1, source_target_pairs={{0,12},{1,13},{2,14},{3,15},{4,8},{5,9},{6,10},{7,11},{8,4},{9,5},... | collective-permute-start | bytes 393224 | tf_op jit(solution)/shard_map/ppermute | solution.py:299
  24.1 1.3 %collective-permute-start.3 = (bf16[1,2,64,256]{3,2,1,0:T(8,128)(2,1)S(1)}, bf16[1,2,64,256]{3,2,1,0:T(8,128)(2,1)S(1)}, u32[]{:S(2)}, u32[]{:S(2)}) collective-permute-start(bf16[1,2,64,256]{3,2,1,0:T(8,128)(2,1)S(1)} %slice.25), channel_id=1, source_target_pairs={{0,1},{1,0},{2,3},{3,2},{4,5},{5,4},{6,7},{7,6},{8,9},{9,8},{10,11... | collective-permute-start | bytes 196616 | tf_op jit(solution)/shard_map/ppermute | solution.py:299
  24.2 1.4 %collective-permute-start.2 = (bf16[1,2,64,256]{3,2,1,0:T(8,128)(2,1)S(1)}, bf16[1,2,64,256]{3,2,1,0:T(8,128)(2,1)S(1)}, u32[]{:S(2)}, u32[]{:S(2)}) collective-permute-start(bf16[1,2,64,256]{3,2,1,0:T(8,128)(2,1)S(1)} %slice.24), channel_id=1, source_target_pairs={{0,1},{1,0},{2,3},{3,2},{4,5},{5,4},{6,7},{7,6},{8,9},{9,8},{10,11... | collective-permute-start | bytes 196616 | tf_op jit(solution)/shard_map/ppermute | solution.py:299
  25.4 7.9 %collective-permute-start.7 = (bf16[2,2,64,256]{3,2,1,0:T(8,128)(2,1)S(1)}, bf16[2,2,64,256]{3,2,1,0:T(8,128)(2,1)S(1)}, u32[]{:S(2)}, u32[]{:S(2)}) collective-permute-start(bf16[2,2,64,256]{3,2,1,0:T(8,128)(2,1)S(1)} %get-tuple-element.38), channel_id=1, source_target_pairs={{0,4},{1,5},{2,6},{3,7},{4,0},{5,1},{6,2},{7,3},{8,12},{9,13},{10,... | collective-permute-start | bytes 393224 | tf_op jit(solution)/shard_map/ppermute | solution.py:299
  25.6 7.7 %collective-permute-start.8 = (bf16[2,2,64,256]{3,2,1,0:T(8,128)(2,1)S(1)}, bf16[2,2,64,256]{3,2,1,0:T(8,128)(2,1)S(1)}, u32[]{:S(2)}, u32[]{:S(2)}) collective-permute-start(bf16[2,2,64,256]{3,2,1,0:T(8,128)(2,1)S(1)} %get-tuple-element.40), channel_id=1, source_target_pairs={{0,2},{1,3},{2,0},{3,1},{4,6},{5,7},{6,4},{7,5},{8,10},{9,11},{10,... | collective-permute-start | bytes 393224 | tf_op jit(solution)/shard_map/ppermute | solution.py:299
  33.4 1.8 %collective-permute-start.9 = (bf16[6,2,64,256]{3,2,1,0:T(8,128)(2,1)S(1)}, bf16[6,2,64,256]{3,2,1,0:T(8,128)(2,1)S(1)}, u32[]{:S(2)}, u32[]{:S(2)}) collective-permute-start(bf16[6,2,64,256]{3,2,1,0:T(8,128)(2,1)S(1)} %slice_dynamic-update-slice_fusion), channel_id=1, source_target_pairs={{0,1},{1,0},{2,3},{3,2},{4,5},{5,4},{6,7},{7,6},{8,9},{9,8},{10,11... | collective-permute-start | bytes 1179656 | tf_op jit(solution)/shard_map/ppermute | solution.py:299
  35.2 16.3 %copy-start.1 = (s32[64,512]{1,0:T(8,128)S(1)}, s32[64,512]{1,0:T(8,128)}, u32[]{:S(2)}) copy-start(s32[64,512]{1,0:T(8,128)} %delay_ref.1) | copy-start | bytes 393220

commit v7 on v6

--- a/solution.py
+++ b/solution.py
@@ -13,6 +13,7 @@
 OWNERS = ("wide_high", "wide_low", "sub", "pol")
 ROWS = 16
 LOTS = 4
+PARTS = 4
 COST = pl.CostEstimate(flops=0, bytes_accessed=0, transcendentals=0)
 
 
@@ -54,50 +55,65 @@
     moved_ref, refs = (refs[0], refs[1:]) if first else (volt_ref, refs)
     part_ref, hold_ref, sem = refs[:3]
     frames = moved_ref.shape[0]
+    here = here_ref[steps]
+
+    def give(step, frame, both):
+        half = both.shape[0] // 2
+        spectrum = (both[:half] + both[half:]).astype(jnp.bfloat16)
+        hold_ref[step * frames + frame] = spectrum.reshape(subs * pols, -1, spectrum.shape[-1])
+        for sub in range(subs):
+            for pol in range(pols):
+                out_refs[step * subs + sub][pol, frame] = hold_ref[
+                    step * frames + frame, (sub * pols + pol) ^ here
+                ]
+
+    def product(part, volts):
+        return lax.dot_general(
+            part, volts, (((1,), (1,)), ((), ())), preferred_element_type=jnp.float32
+        )
+
+    if first:
+        raw_ref, raw_sem = refs[3:]
+        lots, _, _, width = raw_ref.shape
+        copies = []
+        for lot in range(lots):
+            some = pl.ds(lot * width, width)
+            copies.append(
+                (
+                    pltpu.make_async_copy(
+                        volt_ref.at[0, :, :, some], raw_ref.at[lot], raw_sem.at[0, lot]
+                    ),
+                    pltpu.make_async_copy(
+                        table_ref.at[here_ref[0], :, some], part_ref.at[lot], raw_sem.at[1, lot]
+                    ),
+                )
+            )
+        for pair in copies:
+            for copy in pair:
+                copy.start()
+        sums = [None] * frames
+        for lot, (read, part) in enumerate(copies):
+            some = pl.ds(lot * width, width)
+            read.wait()
+            moved_ref[:, :, some] = raw_ref[lot].transpose(1, 0, 2)
+            part.wait()
+            for frame in range(frames):
+                term = product(part_ref[lot], moved_ref[frame, :, some])
+                sums[frame] = term if lot == 0 else sums[frame] + term
+        for frame in range(frames):
+            give(0, frame, sums[frame])
+        return
     copies = [
         pltpu.make_async_copy(table_ref.at[here_ref[step]], part_ref.at[step], sem.at[step])
         for step in range(steps)
     ]
-    if first:
-        raw_ref, raw_sem = refs[3:]
-        count = raw_ref.shape[0] // raw_sem.shape[0]
-        reads = []
-        for index in range(raw_sem.shape[0]):
-            rows = pl.ds(index * count, count)
-            reads.append(
-                pltpu.make_async_copy(volt_ref.at[0, rows], raw_ref.at[rows], raw_sem.at[index])
-            )
-        for copy in reads + copies:
-            copy.start()
-        for index, copy in enumerate(reads):
-            copy.wait()
-            rows = pl.ds(index * count, count)
-            moved_ref[:, rows, :] = raw_ref[rows].transpose(1, 0, 2)
-        keeps = []
-    else:
-        keeps = keep_weights(here_ref, steps - kept_refs[0].shape[0], weight_refs, kept_refs, refs[3])
-        for copy in copies + keeps:
-            copy.start()
-    here = here_ref[steps]
-    half = part_ref.shape[1] // 2
+    keeps = keep_weights(here_ref, steps - kept_refs[0].shape[0], weight_refs, kept_refs, refs[3])
+    for copy in copies + keeps:
+        copy.start()
     for step, copy in enumerate(copies):
         copy.wait()
         for frame in range(frames):
-            both = lax.dot_general(
-                part_ref[step],
-                moved_ref[frame],
-                (((1,), (1,)), ((), ())),
-                preferred_element_type=jnp.float32,
-            )
-            spectrum = (both[:half] + both[half:]).astype(jnp.bfloat16)
-            hold_ref[step * frames + frame] = spectrum.reshape(
-                subs * pols, -1, spectrum.shape[-1]
-            )
-            for sub in range(subs):
-                for pol in range(pols):
-                    out_refs[step * subs + sub][pol, frame] = hold_ref[
-                        step * frames + frame, (sub * pols + pol) ^ here
-                    ]
+            give(step, frame, product(part_ref[step], moved_ref[frame]))
     for copy in keeps:
         copy.wait()
 
@@ -114,15 +130,18 @@
         for weight in weights
     ]
     pieces = [jax.ShapeDtypeStruct((pols, frames, rows, antennas), jnp.bfloat16)] * (steps * subs)
+    part = (steps,) + table.shape[1:]
+    if first:
+        part = (PARTS, table.shape[1], samples // PARTS)
     scratch = [
-        pltpu.VMEM((steps,) + table.shape[1:], jnp.bfloat16),
+        pltpu.VMEM(part, jnp.bfloat16),
         pltpu.VMEM((steps * frames, subs * pols, rows, antennas), jnp.bfloat16),
         pltpu.SemaphoreType.DMA((steps,)),
     ]
     if first:
         kept.append(pltpu.VMEM((frames, antennas, samples), volts.dtype))
-        scratch.append(pltpu.VMEM((antennas, frames, samples), volts.dtype))
-        scratch.append(pltpu.SemaphoreType.DMA((4,)))
+        scratch.append(pltpu.VMEM((PARTS, antennas, frames, samples // PARTS), volts.dtype))
+        scratch.append(pltpu.SemaphoreType.DMA((2, PARTS)))
         volts = pltpu.with_memory_space_constraint(volts, pltpu.HBM)
     else:
         scratch.append(pltpu.SemaphoreType.DMA((2, keep, LOTS)))

time: 52.6 us -> 52.5 us (level)
  no operation moved by 1% of the time
where the time goes in v7:
time: 52.5 us; the launch traced here: 52.3 us
  Pallas kernels  21.6 us (41%)
  starting transfers between devices  13 us (25%)
  blocking collectives  11.8 us (22%)
  waiting for transfers between devices  5.44 us (10%)
    ppermute x10, starting transfers between devices, exchange(): return lax.ppermute(x, names, [(k, k ^ offset) for k in range(count)])  13 us
    pallas_call x2, Pallas kernels, spectra(): pl.pallas_call(functools.partial(dft_kernel, (steps, subs, pols, len(weig...  12 us
    all_to_all x1, blocking collectives, local(): power = turn(total.reshape(owners, own, -1))  11.8 us
    ppermute x10, waiting for transfers between devices, exchange(): return lax.ppermute(x, names, [(k, k ^ offset) for k in range(count)])  5.44 us
    pallas_call x1, Pallas kernels, beam_power(): pl.pallas_call(functools.partial(last_kernel, subs, len(kept)), in_specs=...  4.52 us
    pallas_call x1, Pallas kernels, first_beams(): pl.pallas_call(functools.partial(first_kernel, subs), in_specs=[pl.BlockS...  4.13 us
  transfers between devices with their start and end apart: 10, of which 4 were waited for; matrix products, arithmetic and copies ran while one was open for 0% of the time, Pallas kernels for 23%

profile of v7, /device:TPU:0, one launch (start us, length us, event | category | flops | bytes accessed | tf_op | source)
XLA Modules:
  0.0 52.3 jit_solution(11364626102760381620)
XLA Ops:
  0.0 0.1 pad_add_fusion.2.here_ref
  0.1 4.0 %spectra.2 = (bf16[2,2,64,256]{3,2,1,0:T(8,128)(2,1)S(1)}, bf16[2,2,64,256]{3,2,1,0:T(8,128)(2,1)S(1)}, bf16[2,256,2048]{2,1,0:T(8,128)(2,1)S(1)}) custom-call(s32[2]{0:T(128)S(1)} %pad_add_fusion.2.here_ref, bf16[4,512,2048]{2,1,0:T(8,128)(2,1)} %constant.24.clone.table_ref, bf16[1,256,2,2048]{3,2,1,0:T(2,128)(2,1)} %volt_ref.1), custom_call_target="tpu_custom_call" | custom-call | tf_op jit(solution)/shard_map/spectra/pallas_call | solution.py:149
  4.1 5.0 %collective-permute-start.1 = (bf16[2,2,64,256]{3,2,1,0:T(8,128)(2,1)S(1)}, bf16[2,2,64,256]{3,2,1,0:T(8,128)(2,1)S(1)}, u32[]{:S(2)}, u32[]{:S(2)}) collective-permute-start(bf16[2,2,64,256]{3,2,1,0:T(8,128)(2,1)S(1)} %get-tuple-element.29), channel_id=1, source_target_pairs={{0,10},{1,11},{2,8},{3,9},{4,14},{5,15},{6,12},{7,13},{8,2},{9,3},... | collective-permute-start | bytes 393224 | tf_op jit(solution)/shard_map/ppermute | solution.py:318
  9.1 0.3 collective-permute-start
  9.4 0.1 pad_add_fusion.3.here_ref
  9.5 0.0 copy-start
  9.5 0.0 copy-start.2
  9.5 8.0 %spectra.3 = (bf16[2,2,64,256]{3,2,1,0:T(8,128)(2,1)S(1)}, bf16[2,2,64,256]{3,2,1,0:T(8,128)(2,1)S(1)}, bf16[2,2,64,256]{3,2,1,0:T(8,128)(2,1)S(1)}, bf16[2,2,64...) custom-call(s32[4]{0:T(128)S(1)} %pad_add_fusion.3.here_ref, ...), custom_call_target="tpu_custom_call" | custom-call | tf_op jit(solution)/shard_map/spectra/pallas_call | solution.py:149
  17.5 1.6 %collective-permute-start.4 = (bf16[2,2,64,256]{3,2,1,0:T(8,128)(2,1)S(1)}, bf16[2,2,64,256]{3,2,1,0:T(8,128)(2,1)S(1)}, u32[]{:S(2)}, u32[]{:S(2)}) collective-permute-start(bf16[2,2,64,256]{3,2,1,0:T(8,128)(2,1)S(1)} %get-tuple-element.36), channel_id=1, source_target_pairs={{0,6},{1,7},{2,4},{3,5},{4,2},{5,3},{6,0},{7,1},{8,14},{9,15},{10,... | collective-permute-start | bytes 393224 | tf_op jit(solution)/shard_map/ppermute | solution.py:318
  19.2 3.4 %collective-permute-start.6 = (bf16[2,2,64,256]{3,2,1,0:T(8,128)(2,1)S(1)}, bf16[2,2,64,256]{3,2,1,0:T(8,128)(2,1)S(1)}, u32[]{:S(2)}, u32[]{:S(2)}) collective-permute-start(bf16[2,2,64,256]{3,2,1,0:T(8,128)(2,1)S(1)} %get-tuple-element.37), channel_id=1, source_target_pairs={{0,14},{1,15},{2,12},{3,13},{4,10},{5,11},{6,8},{7,9},{8,6},{9,7},... | collective-permute-start | bytes 393224 | tf_op jit(solution)/shard_map/ppermute | solution.py:318
  22.6 1.4 %collective-permute-start.5 = (bf16[2,2,64,256]{3,2,1,0:T(8,128)(2,1)S(1)}, bf16[2,2,64,256]{3,2,1,0:T(8,128)(2,1)S(1)}, u32[]{:S(2)}, u32[]{:S(2)}) collective-permute-start(bf16[2,2,64,256]{3,2,1,0:T(8,128)(2,1)S(1)} %get-tuple-element.31), channel_id=1, source_target_pairs={{0,12},{1,13},{2,14},{3,15},{4,8},{5,9},{6,10},{7,11},{8,4},{9,5},... | collective-permute-start | bytes 393224 | tf_op jit(solution)/shard_map/ppermute | solution.py:318
  23.9 0.0 collective-permute-done.1.refs_1_
  23.9 0.0 collective-permute-done.refs_0_
  23.9 0.1 collective-permute-start.3
  24.0 0.5 collective-permute-start.2
  24.5 0.1 pad_add_fusion.1.place_ref
  24.6 0.7 %collective-permute-done.3.refs_3_ = bf16[1,2,64,256]{3,2,1,0:T(8,128)(2,1)S(1)} collective-permute-done((bf16[1,2,64,256]{3,2,1,0:T(8,128)(2,1)S(1)}, bf16[1,2,64,256]{3,2,1,0:T(8,128)(2,1)S(1)}, u32[]{:S(2)}, u32[]{:S(2)}) %collective-permute-start.3) | collective-permute-done | bytes 65568 | tf_op jit(solution)/shard_map/ppermute | solution.py:318
  25.3 0.0 collective-permute-start.7
  25.3 0.2 collective-permute-done.2.refs_2_
  25.4 0.5 %collective-permute-start.8 = (bf16[2,2,64,256]{3,2,1,0:T(8,128)(2,1)S(1)}, bf16[2,2,64,256]{3,2,1,0:T(8,128)(2,1)S(1)}, u32[]{:S(2)}, u32[]{:S(2)}) collective-permute-start(bf16[2,2,64,256]{3,2,1,0:T(8,128)(2,1)S(1)} %get-tuple-element.40), channel_id=1, source_target_pairs={{0,2},{1,3},{2,0},{3,1},{4,6},{5,7},{6,4},{7,5},{8,10},{9,11},{10,... | collective-permute-start | bytes 393224 | tf_op jit(solution)/shard_map/ppermute | solution.py:318
  26.0 0.0 copy-done
  26.0 0.0 copy-done.2
  26.0 4.1 %first_beams.1 = (f32[32,16,256]{2,1,0:T(8,128)S(1)}, bf16[1,32,256,256]{3,2,1,0:T(8,128)(2,1)S(1)}) custom-call(s32[2]{0:T(128)S(1)} %pad_add_fusion.1.place_ref, bf16[128,128]{1,0:T(8,128)(2,1)S(1)} %copy-done.2, bf16[32,1024,256]{2,1,0:T(8,128)(2,1)} %re_ref.1, bf16[32,4,256,256]{3,2,1,0:T(8,128)(2,1)S(1)} %bitcast.9, ...), custom_call_target="tpu_custom_call" | custom-call | flops 40000000000 | bytes 400000000 | tf_op jit(solution)/shard_map/first_beams/pallas_call | solution.py:274
  30.1 0.0 collective-permute-done.4.refs_7_
  30.1 0.0 collective-permute-done.6.refs_5_
  30.1 3.0 %collective-permute-done.7.refs_6_ = bf16[2,2,64,256]{3,2,1,0:T(8,128)(2,1)S(1)} collective-permute-done((bf16[2,2,64,256]{3,2,1,0:T(8,128)(2,1)S(1)}, bf16[2,2,64,256]{3,2,1,0:T(8,128)(2,1)S(1)}, u32[]{:S(2)}, u32[]{:S(2)}) %collective-permute-start.7) | collective-permute-done | bytes 131104 | tf_op jit(solution)/shard_map/ppermute | solution.py:318
  33.1 0.0 collective-permute-done.8.refs_9_
  33.1 0.0 collective-permute-done.5.refs_4_
  33.2 0.1 collective-permute-start.9
  33.3 0.1 pad_add_fusion.place_ref
  33.4 1.6 %collective-permute-done.9.refs_10_ = bf16[6,2,64,256]{3,2,1,0:T(8,128)(2,1)S(1)} collective-permute-done((bf16[6,2,64,256]{3,2,1,0:T(8,128)(2,1)S(1)}, bf16[6,2,64,256]{3,2,1,0:T(8,128)(2,1)S(1)}, u32[]{:S(2)}, u32[]{:S(2)}) %collective-permute-start.9) | collective-permute-done | bytes 393248 | tf_op jit(solution)/shard_map/ppermute | solution.py:318
  35.0 0.0 copy-start.1
  35.0 4.5 %beam_power.1 = bf16[8,2,32,128]{3,2,1,0:T(8,128)(2,1)S(1)} custom-call(s32[4]{0:T(128)S(1)} %pad_add_fusion.place_ref, bf16[128,128]{1,0:T(8,128)(2,1)S(1)} %copy-done.2, bf16[1,32,256,256]{3,2,1,0:T(8,128)(2,1)S(1)} %get-tuple-element.34.refs_0_, bf16[2,32,256,256]{3,2,1,0:T(8,128)(2,1)S(1)} %get-tuple-element.35.refs_1_, ...), custom_call_target="tpu_custom_call" | custom-call | tf_op jit(solution)/shard_map/beam_power/pallas_call | solution.py:298
  39.5 11.8 %all_to_all.5 = bf16[16,32,128]{2,1,0:T(8,128)(2,1)S(1)} all-to-all(bf16[16,32,128]{2,1,0:T(8,128)(2,1)S(1)} %bitcast.11), channel_id=1, replica_groups=mesh['group'=2,'wide_high'=2,'wide_low'=2,'sub'=2,'pol'=2] {'wide_high',..., dimensions={0} | all-to-all | bytes 262144 | tf_op jit(solution)/shard_map/all_to_all | solution.py:468
  51.3 0.0 copy-done.1
  51.3 1.0 %shift_and_add.1 = f32[32,4,64]{2,1,0:T(4,128)} custom-call(bf16[512,128]{1,0:T(8,128)(2,1)S(1)} %bitcast.12, s32[64,512]{1,0:T(8,128)S(1)} %copy-done.1), custom_call_target="tpu_custom_call" | custom-call | tf_op jit(solution)/shard_map/shift_and_add/pallas_call | solution.py:353
  (8 shorter events, 0.1 us)
Async XLA Ops:
  4.1 19.9 %collective-permute-start.1 = (bf16[2,2,64,256]{3,2,1,0:T(8,128)(2,1)S(1)}, bf16[2,2,64,256]{3,2,1,0:T(8,128)(2,1)S(1)}, u32[]{:S(2)}, u32[]{:S(2)}) collective-permute-start(bf16[2,2,64,256]{3,2,1,0:T(8,128)(2,1)S(1)} %get-tuple-element.29), channel_id=1, source_target_pairs={{0,10},{1,11},{2,8},{3,9},{4,14},{5,15},{6,12},{7,13},{8,2},{9,3},... | collective-permute-start | bytes 393224 | tf_op jit(solution)/shard_map/ppermute | solution.py:318
  9.1 14.8 %collective-permute-start = (bf16[2,2,64,256]{3,2,1,0:T(8,128)(2,1)S(1)}, bf16[2,2,64,256]{3,2,1,0:T(8,128)(2,1)S(1)}, u32[]{:S(2)}, u32[]{:S(2)}) collective-permute-start(bf16[2,2,64,256]{3,2,1,0:T(8,128)(2,1)S(1)} %get-tuple-element.27), channel_id=1, source_target_pairs={{0,8},{1,9},{2,10},{3,11},{4,12},{5,13},{6,14},{7,15},{8,0},{9,1},... | collective-permute-start | bytes 393224 | tf_op jit(solution)/shard_map/ppermute | solution.py:318
  9.5 16.5 %copy-start = (bf16[32,1024,256]{2,1,0:T(8,128)(2,1)S(1)}, bf16[32,1024,256]{2,1,0:T(8,128)(2,1)}, u32[]{:S(2)}) copy-start(bf16[32,1024,256]{2,1,0:T(8,128)(2,1)} %param.9) | copy-start | bytes 50331652
  9.5 16.5 %copy-start.2 = (bf16[128,128]{1,0:T(8,128)(2,1)S(1)}, bf16[128,128]{1,0:T(8,128)(2,1)}, u32[]{:S(2)}) copy-start(bf16[128,128]{1,0:T(8,128)(2,1)} %constant.25.clone.order_ref) | copy-start | bytes 98308
  17.5 12.6 %collective-permute-start.4 = (bf16[2,2,64,256]{3,2,1,0:T(8,128)(2,1)S(1)}, bf16[2,2,64,256]{3,2,1,0:T(8,128)(2,1)S(1)}, u32[]{:S(2)}, u32[]{:S(2)}) collective-permute-start(bf16[2,2,64,256]{3,2,1,0:T(8,128)(2,1)S(1)} %get-tuple-element.36), channel_id=1, source_target_pairs={{0,6},{1,7},{2,4},{3,5},{4,2},{5,3},{6,0},{7,1},{8,14},{9,15},{10,... | collective-permute-start | bytes 393224 | tf_op jit(solution)/shard_map/ppermute | solution.py:318
  19.2 11.0 %collective-permute-start.6 = (bf16[2,2,64,256]{3,2,1,0:T(8,128)(2,1)S(1)}, bf16[2,2,64,256]{3,2,1,0:T(8,128)(2,1)S(1)}, u32[]{:S(2)}, u32[]{:S(2)}) collective-permute-start(bf16[2,2,64,256]{3,2,1,0:T(8,128)(2,1)S(1)} %get-tuple-element.37), channel_id=1, source_target_pairs={{0,14},{1,15},{2,12},{3,13},{4,10},{5,11},{6,8},{7,9},{8,6},{9,7},... | collective-permute-start | bytes 393224 | tf_op jit(solution)/shard_map/ppermute | solution.py:318
  22.6 10.6 %collective-permute-start.5 = (bf16[2,2,64,256]{3,2,1,0:T(8,128)(2,1)S(1)}, bf16[2,2,64,256]{3,2,1,0:T(8,128)(2,1)S(1)}, u32[]{:S(2)}, u32[]{:S(2)}) collective-permute-start(bf16[2,2,64,256]{3,2,1,0:T(8,128)(2,1)S(1)} %get-tuple-element.31), channel_id=1, source_target_pairs={{0,12},{1,13},{2,14},{3,15},{4,8},{5,9},{6,10},{7,11},{8,4},{9,5},... | collective-permute-start | bytes 393224 | tf_op jit(solution)/shard_map/ppermute | solution.py:318
  23.9 1.3 %collective-permute-start.3 = (bf16[1,2,64,256]{3,2,1,0:T(8,128)(2,1)S(1)}, bf16[1,2,64,256]{3,2,1,0:T(8,128)(2,1)S(1)}, u32[]{:S(2)}, u32[]{:S(2)}) collective-permute-start(bf16[1,2,64,256]{3,2,1,0:T(8,128)(2,1)S(1)} %slice.25), channel_id=1, source_target_pairs={{0,1},{1,0},{2,3},{3,2},{4,5},{5,4},{6,7},{7,6},{8,9},{9,8},{10,11... | collective-permute-start | bytes 196616 | tf_op jit(solution)/shard_map/ppermute | solution.py:318
  24.0 1.4 %collective-permute-start.2 = (bf16[1,2,64,256]{3,2,1,0:T(8,128)(2,1)S(1)}, bf16[1,2,64,256]{3,2,1,0:T(8,128)(2,1)S(1)}, u32[]{:S(2)}, u32[]{:S(2)}) collective-permute-start(bf16[1,2,64,256]{3,2,1,0:T(8,128)(2,1)S(1)} %slice.24), channel_id=1, source_target_pairs={{0,1},{1,0},{2,3},{3,2},{4,5},{5,4},{6,7},{7,6},{8,9},{9,8},{10,11... | collective-permute-start | bytes 196616 | tf_op jit(solution)/shard_map/ppermute | solution.py:318
  25.3 7.9 %collective-permute-start.7 = (bf16[2,2,64,256]{3,2,1,0:T(8,128)(2,1)S(1)}, bf16[2,2,64,256]{3,2,1,0:T(8,128)(2,1)S(1)}, u32[]{:S(2)}, u32[]{:S(2)}) collective-permute-start(bf16[2,2,64,256]{3,2,1,0:T(8,128)(2,1)S(1)} %get-tuple-element.38), channel_id=1, source_target_pairs={{0,4},{1,5},{2,6},{3,7},{4,0},{5,1},{6,2},{7,3},{8,12},{9,13},{10,... | collective-permute-start | bytes 393224 | tf_op jit(solution)/shard_map/ppermute | solution.py:318
  25.4 7.7 %collective-permute-start.8 = (bf16[2,2,64,256]{3,2,1,0:T(8,128)(2,1)S(1)}, bf16[2,2,64,256]{3,2,1,0:T(8,128)(2,1)S(1)}, u32[]{:S(2)}, u32[]{:S(2)}) collective-permute-start(bf16[2,2,64,256]{3,2,1,0:T(8,128)(2,1)S(1)} %get-tuple-element.40), channel_id=1, source_target_pairs={{0,2},{1,3},{2,0},{3,1},{4,6},{5,7},{6,4},{7,5},{8,10},{9,11},{10,... | collective-permute-start | bytes 393224 | tf_op jit(solution)/shard_map/ppermute | solution.py:318
  33.2 1.8 %collective-permute-start.9 = (bf16[6,2,64,256]{3,2,1,0:T(8,128)(2,1)S(1)}, bf16[6,2,64,256]{3,2,1,0:T(8,128)(2,1)S(1)}, u32[]{:S(2)}, u32[]{:S(2)}) collective-permute-start(bf16[6,2,64,256]{3,2,1,0:T(8,128)(2,1)S(1)} %slice_dynamic-update-slice_fusion), channel_id=1, source_target_pairs={{0,1},{1,0},{2,3},{3,2},{4,5},{5,4},{6,7},{7,6},{8,9},{9,8},{10,11... | collective-permute-start | bytes 1179656 | tf_op jit(solution)/shard_map/ppermute | solution.py:318
  35.0 16.3 %copy-start.1 = (s32[64,512]{1,0:T(8,128)S(1)}, s32[64,512]{1,0:T(8,128)}, u32[]{:S(2)}) copy-start(s32[64,512]{1,0:T(8,128)} %delay_ref.1) | copy-start | bytes 393220

commit v8 on v7

--- a/solution.py
+++ b/solution.py
@@ -13,7 +13,7 @@
 OWNERS = ("wide_high", "wide_low", "sub", "pol")
 ROWS = 16
 LOTS = 4
-PARTS = 4
+PARTS = 8
 COST = pl.CostEstimate(flops=0, bytes_accessed=0, transcendentals=0)
 
 

time: 52.5 us -> 53.2 us (1.013)
  Pallas kernels: 21.6 us -> 22.3 us
    pallas_call x2, Pallas kernels: 12 us -> 12.7 us  [spectra(): pl.pallas_call(functools.partial(dft_kernel, (steps, subs, pols, len(weig...]
where the time goes in v8:
time: 53.2 us; the launch traced here: 53 us
  Pallas kernels  22.3 us (42%)
  starting transfers between devices  13 us (24%)
  blocking collectives  11.8 us (22%)
  waiting for transfers between devices  5.44 us (10%)
    ppermute x10, starting transfers between devices, exchange(): return lax.ppermute(x, names, [(k, k ^ offset) for k in range(count)])  13 us
    pallas_call x2, Pallas kernels, spectra(): pl.pallas_call(functools.partial(dft_kernel, (steps, subs, pols, len(weig...  12.7 us
    all_to_all x1, blocking collectives, local(): power = turn(total.reshape(owners, own, -1))  11.8 us
    ppermute x10, waiting for transfers between devices, exchange(): return lax.ppermute(x, names, [(k, k ^ offset) for k in range(count)])  5.44 us
    pallas_call x1, Pallas kernels, beam_power(): pl.pallas_call(functools.partial(last_kernel, subs, len(kept)), in_specs=...  4.52 us
    pallas_call x1, Pallas kernels, first_beams(): pl.pallas_call(functools.partial(first_kernel, subs), in_specs=[pl.BlockS...  4.13 us
  transfers between devices with their start and end apart: 10, of which 4 were waited for; matrix products, arithmetic and copies ran while one was open for 0% of the time, Pallas kernels for 23%

profile of v8, /device:TPU:0, one launch (start us, length us, event | category | flops | bytes accessed | tf_op | source)
XLA Modules:
  0.0 53.0 jit_solution(14848308041426928981)
XLA Ops:
  0.0 0.1 pad_add_fusion.2.here_ref
  0.1 4.6 %spectra.2 = (bf16[2,2,64,256]{3,2,1,0:T(8,128)(2,1)S(1)}, bf16[2,2,64,256]{3,2,1,0:T(8,128)(2,1)S(1)}, bf16[2,256,2048]{2,1,0:T(8,128)(2,1)S(1)}) custom-call(s32[2]{0:T(128)S(1)} %pad_add_fusion.2.here_ref, bf16[4,512,2048]{2,1,0:T(8,128)(2,1)} %constant.24.clone.table_ref, bf16[1,256,2,2048]{3,2,1,0:T(2,128)(2,1)} %volt_ref.1), custom_call_target="tpu_custom_call" | custom-call | tf_op jit(solution)/shard_map/spectra/pallas_call | solution.py:149
  4.7 5.0 %collective-permute-start.1 = (bf16[2,2,64,256]{3,2,1,0:T(8,128)(2,1)S(1)}, bf16[2,2,64,256]{3,2,1,0:T(8,128)(2,1)S(1)}, u32[]{:S(2)}, u32[]{:S(2)}) collective-permute-start(bf16[2,2,64,256]{3,2,1,0:T(8,128)(2,1)S(1)} %get-tuple-element.29), channel_id=1, source_target_pairs={{0,10},{1,11},{2,8},{3,9},{4,14},{5,15},{6,12},{7,13},{8,2},{9,3},... | collective-permute-start | bytes 393224 | tf_op jit(solution)/shard_map/ppermute | solution.py:318
  9.8 0.3 collective-permute-start
  10.1 0.1 pad_add_fusion.3.here_ref
  10.2 0.0 copy-start
  10.2 0.0 copy-start.2
  10.2 8.0 %spectra.3 = (bf16[2,2,64,256]{3,2,1,0:T(8,128)(2,1)S(1)}, bf16[2,2,64,256]{3,2,1,0:T(8,128)(2,1)S(1)}, bf16[2,2,64,256]{3,2,1,0:T(8,128)(2,1)S(1)}, bf16[2,2,64...) custom-call(s32[4]{0:T(128)S(1)} %pad_add_fusion.3.here_ref, ...), custom_call_target="tpu_custom_call" | custom-call | tf_op jit(solution)/shard_map/spectra/pallas_call | solution.py:149
  18.2 1.6 %collective-permute-start.4 = (bf16[2,2,64,256]{3,2,1,0:T(8,128)(2,1)S(1)}, bf16[2,2,64,256]{3,2,1,0:T(8,128)(2,1)S(1)}, u32[]{:S(2)}, u32[]{:S(2)}) collective-permute-start(bf16[2,2,64,256]{3,2,1,0:T(8,128)(2,1)S(1)} %get-tuple-element.36), channel_id=1, source_target_pairs={{0,6},{1,7},{2,4},{3,5},{4,2},{5,3},{6,0},{7,1},{8,14},{9,15},{10,... | collective-permute-start | bytes 393224 | tf_op jit(solution)/shard_map/ppermute | solution.py:318
  19.8 3.4 %collective-permute-start.6 = (bf16[2,2,64,256]{3,2,1,0:T(8,128)(2,1)S(1)}, bf16[2,2,64,256]{3,2,1,0:T(8,128)(2,1)S(1)}, u32[]{:S(2)}, u32[]{:S(2)}) collective-permute-start(bf16[2,2,64,256]{3,2,1,0:T(8,128)(2,1)S(1)} %get-tuple-element.37), channel_id=1, source_target_pairs={{0,14},{1,15},{2,12},{3,13},{4,10},{5,11},{6,8},{7,9},{8,6},{9,7},... | collective-permute-start | bytes 393224 | tf_op jit(solution)/shard_map/ppermute | solution.py:318
  23.2 1.3 %collective-permute-start.5 = (bf16[2,2,64,256]{3,2,1,0:T(8,128)(2,1)S(1)}, bf16[2,2,64,256]{3,2,1,0:T(8,128)(2,1)S(1)}, u32[]{:S(2)}, u32[]{:S(2)}) collective-permute-start(bf16[2,2,64,256]{3,2,1,0:T(8,128)(2,1)S(1)} %get-tuple-element.31), channel_id=1, source_target_pairs={{0,12},{1,13},{2,14},{3,15},{4,8},{5,9},{6,10},{7,11},{8,4},{9,5},... | collective-permute-start | bytes 393224 | tf_op jit(solution)/shard_map/ppermute | solution.py:318
  24.6 0.0 collective-permute-done.1.refs_1_
  24.6 0.0 collective-permute-done.refs_0_
  24.6 0.1 collective-permute-start.3
  24.7 0.5 collective-permute-start.2
  25.2 0.1 pad_add_fusion.1.place_ref
  25.3 0.7 %collective-permute-done.3.refs_3_ = bf16[1,2,64,256]{3,2,1,0:T(8,128)(2,1)S(1)} collective-permute-done((bf16[1,2,64,256]{3,2,1,0:T(8,128)(2,1)S(1)}, bf16[1,2,64,256]{3,2,1,0:T(8,128)(2,1)S(1)}, u32[]{:S(2)}, u32[]{:S(2)}) %collective-permute-start.3) | collective-permute-done | bytes 65568 | tf_op jit(solution)/shard_map/ppermute | solution.py:318
  25.9 0.0 collective-permute-start.7
  25.9 0.2 collective-permute-done.2.refs_2_
  26.1 0.6 %collective-permute-start.8 = (bf16[2,2,64,256]{3,2,1,0:T(8,128)(2,1)S(1)}, bf16[2,2,64,256]{3,2,1,0:T(8,128)(2,1)S(1)}, u32[]{:S(2)}, u32[]{:S(2)}) collective-permute-start(bf16[2,2,64,256]{3,2,1,0:T(8,128)(2,1)S(1)} %get-tuple-element.40), channel_id=1, source_target_pairs={{0,2},{1,3},{2,0},{3,1},{4,6},{5,7},{6,4},{7,5},{8,10},{9,11},{10,... | collective-permute-start | bytes 393224 | tf_op jit(solution)/shard_map/ppermute | solution.py:318
  26.6 0.0 copy-done
  26.6 0.0 copy-done.2
  26.6 4.1 %first_beams.1 = (f32[32,16,256]{2,1,0:T(8,128)S(1)}, bf16[1,32,256,256]{3,2,1,0:T(8,128)(2,1)S(1)}) custom-call(s32[2]{0:T(128)S(1)} %pad_add_fusion.1.place_ref, bf16[128,128]{1,0:T(8,128)(2,1)S(1)} %copy-done.2, bf16[32,1024,256]{2,1,0:T(8,128)(2,1)} %re_ref.1, bf16[32,4,256,256]{3,2,1,0:T(8,128)(2,1)S(1)} %bitcast.9, ...), custom_call_target="tpu_custom_call" | custom-call | flops 40000000000 | bytes 400000000 | tf_op jit(solution)/shard_map/first_beams/pallas_call | solution.py:274
  30.8 0.0 collective-permute-done.4.refs_7_
  30.8 0.0 collective-permute-done.6.refs_5_
  30.8 3.0 %collective-permute-done.7.refs_6_ = bf16[2,2,64,256]{3,2,1,0:T(8,128)(2,1)S(1)} collective-permute-done((bf16[2,2,64,256]{3,2,1,0:T(8,128)(2,1)S(1)}, bf16[2,2,64,256]{3,2,1,0:T(8,128)(2,1)S(1)}, u32[]{:S(2)}, u32[]{:S(2)}) %collective-permute-start.7) | collective-permute-done | bytes 131104 | tf_op jit(solution)/shard_map/ppermute | solution.py:318
  33.8 0.0 collective-permute-done.8.refs_9_
  33.8 0.0 collective-permute-done.5.refs_4_
  33.9 0.1 collective-permute-start.9
  34.0 0.1 pad_add_fusion.place_ref
  34.1 1.6 %collective-permute-done.9.refs_10_ = bf16[6,2,64,256]{3,2,1,0:T(8,128)(2,1)S(1)} collective-permute-done((bf16[6,2,64,256]{3,2,1,0:T(8,128)(2,1)S(1)}, bf16[6,2,64,256]{3,2,1,0:T(8,128)(2,1)S(1)}, u32[]{:S(2)}, u32[]{:S(2)}) %collective-permute-start.9) | collective-permute-done | bytes 393248 | tf_op jit(solution)/shard_map/ppermute | solution.py:318
  35.7 0.0 copy-start.1
  35.7 4.5 %beam_power.1 = bf16[8,2,32,128]{3,2,1,0:T(8,128)(2,1)S(1)} custom-call(s32[4]{0:T(128)S(1)} %pad_add_fusion.place_ref, bf16[128,128]{1,0:T(8,128)(2,1)S(1)} %copy-done.2, bf16[1,32,256,256]{3,2,1,0:T(8,128)(2,1)S(1)} %get-tuple-element.34.refs_0_, bf16[2,32,256,256]{3,2,1,0:T(8,128)(2,1)S(1)} %get-tuple-element.35.refs_1_, ...), custom_call_target="tpu_custom_call" | custom-call | tf_op jit(solution)/shard_map/beam_power/pallas_call | solution.py:298
  40.2 11.8 %all_to_all.5 = bf16[16,32,128]{2,1,0:T(8,128)(2,1)S(1)} all-to-all(bf16[16,32,128]{2,1,0:T(8,128)(2,1)S(1)} %bitcast.11), channel_id=1, replica_groups=mesh['group'=2,'wide_high'=2,'wide_low'=2,'sub'=2,'pol'=2] {'wide_high',..., dimensions={0} | all-to-all | bytes 262144 | tf_op jit(solution)/shard_map/all_to_all | solution.py:468
  52.0 0.0 copy-done.1
  52.0 1.0 %shift_and_add.1 = f32[32,4,64]{2,1,0:T(4,128)} custom-call(bf16[512,128]{1,0:T(8,128)(2,1)S(1)} %bitcast.12, s32[64,512]{1,0:T(8,128)S(1)} %copy-done.1), custom_call_target="tpu_custom_call" | custom-call | tf_op jit(solution)/shard_map/shift_and_add/pallas_call | solution.py:353
  (8 shorter events, 0.1 us)
Async XLA Ops:
  4.7 19.9 %collective-permute-start.1 = (bf16[2,2,64,256]{3,2,1,0:T(8,128)(2,1)S(1)}, bf16[2,2,64,256]{3,2,1,0:T(8,128)(2,1)S(1)}, u32[]{:S(2)}, u32[]{:S(2)}) collective-permute-start(bf16[2,2,64,256]{3,2,1,0:T(8,128)(2,1)S(1)} %get-tuple-element.29), channel_id=1, source_target_pairs={{0,10},{1,11},{2,8},{3,9},{4,14},{5,15},{6,12},{7,13},{8,2},{9,3},... | collective-permute-start | bytes 393224 | tf_op jit(solution)/shard_map/ppermute | solution.py:318
  9.8 14.8 %collective-permute-start = (bf16[2,2,64,256]{3,2,1,0:T(8,128)(2,1)S(1)}, bf16[2,2,64,256]{3,2,1,0:T(8,128)(2,1)S(1)}, u32[]{:S(2)}, u32[]{:S(2)}) collective-permute-start(bf16[2,2,64,256]{3,2,1,0:T(8,128)(2,1)S(1)} %get-tuple-element.27), channel_id=1, source_target_pairs={{0,8},{1,9},{2,10},{3,11},{4,12},{5,13},{6,14},{7,15},{8,0},{9,1},... | collective-permute-start | bytes 393224 | tf_op jit(solution)/shard_map/ppermute | solution.py:318
  10.2 16.5 %copy-start = (bf16[32,1024,256]{2,1,0:T(8,128)(2,1)S(1)}, bf16[32,1024,256]{2,1,0:T(8,128)(2,1)}, u32[]{:S(2)}) copy-start(bf16[32,1024,256]{2,1,0:T(8,128)(2,1)} %param.9) | copy-start | bytes 50331652
  10.2 16.5 %copy-start.2 = (bf16[128,128]{1,0:T(8,128)(2,1)S(1)}, bf16[128,128]{1,0:T(8,128)(2,1)}, u32[]{:S(2)}) copy-start(bf16[128,128]{1,0:T(8,128)(2,1)} %constant.25.clone.order_ref) | copy-start | bytes 98308
  18.2 12.6 %collective-permute-start.4 = (bf16[2,2,64,256]{3,2,1,0:T(8,128)(2,1)S(1)}, bf16[2,2,64,256]{3,2,1,0:T(8,128)(2,1)S(1)}, u32[]{:S(2)}, u32[]{:S(2)}) collective-permute-start(bf16[2,2,64,256]{3,2,1,0:T(8,128)(2,1)S(1)} %get-tuple-element.36), channel_id=1, source_target_pairs={{0,6},{1,7},{2,4},{3,5},{4,2},{5,3},{6,0},{7,1},{8,14},{9,15},{10,... | collective-permute-start | bytes 393224 | tf_op jit(solution)/shard_map/ppermute | solution.py:318
  19.8 11.0 %collective-permute-start.6 = (bf16[2,2,64,256]{3,2,1,0:T(8,128)(2,1)S(1)}, bf16[2,2,64,256]{3,2,1,0:T(8,128)(2,1)S(1)}, u32[]{:S(2)}, u32[]{:S(2)}) collective-permute-start(bf16[2,2,64,256]{3,2,1,0:T(8,128)(2,1)S(1)} %get-tuple-element.37), channel_id=1, source_target_pairs={{0,14},{1,15},{2,12},{3,13},{4,10},{5,11},{6,8},{7,9},{8,6},{9,7},... | collective-permute-start | bytes 393224 | tf_op jit(solution)/shard_map/ppermute | solution.py:318
  23.2 10.6 %collective-permute-start.5 = (bf16[2,2,64,256]{3,2,1,0:T(8,128)(2,1)S(1)}, bf16[2,2,64,256]{3,2,1,0:T(8,128)(2,1)S(1)}, u32[]{:S(2)}, u32[]{:S(2)}) collective-permute-start(bf16[2,2,64,256]{3,2,1,0:T(8,128)(2,1)S(1)} %get-tuple-element.31), channel_id=1, source_target_pairs={{0,12},{1,13},{2,14},{3,15},{4,8},{5,9},{6,10},{7,11},{8,4},{9,5},... | collective-permute-start | bytes 393224 | tf_op jit(solution)/shard_map/ppermute | solution.py:318
  24.6 1.3 %collective-permute-start.3 = (bf16[1,2,64,256]{3,2,1,0:T(8,128)(2,1)S(1)}, bf16[1,2,64,256]{3,2,1,0:T(8,128)(2,1)S(1)}, u32[]{:S(2)}, u32[]{:S(2)}) collective-permute-start(bf16[1,2,64,256]{3,2,1,0:T(8,128)(2,1)S(1)} %slice.25), channel_id=1, source_target_pairs={{0,1},{1,0},{2,3},{3,2},{4,5},{5,4},{6,7},{7,6},{8,9},{9,8},{10,11... | collective-permute-start | bytes 196616 | tf_op jit(solution)/shard_map/ppermute | solution.py:318
  24.7 1.4 %collective-permute-start.2 = (bf16[1,2,64,256]{3,2,1,0:T(8,128)(2,1)S(1)}, bf16[1,2,64,256]{3,2,1,0:T(8,128)(2,1)S(1)}, u32[]{:S(2)}, u32[]{:S(2)}) collective-permute-start(bf16[1,2,64,256]{3,2,1,0:T(8,128)(2,1)S(1)} %slice.24), channel_id=1, source_target_pairs={{0,1},{1,0},{2,3},{3,2},{4,5},{5,4},{6,7},{7,6},{8,9},{9,8},{10,11... | collective-permute-start | bytes 196616 | tf_op jit(solution)/shard_map/ppermute | solution.py:318
  25.9 7.9 %collective-permute-start.7 = (bf16[2,2,64,256]{3,2,1,0:T(8,128)(2,1)S(1)}, bf16[2,2,64,256]{3,2,1,0:T(8,128)(2,1)S(1)}, u32[]{:S(2)}, u32[]{:S(2)}) collective-permute-start(bf16[2,2,64,256]{3,2,1,0:T(8,128)(2,1)S(1)} %get-tuple-element.38), channel_id=1, source_target_pairs={{0,4},{1,5},{2,6},{3,7},{4,0},{5,1},{6,2},{7,3},{8,12},{9,13},{10,... | collective-permute-start | bytes 393224 | tf_op jit(solution)/shard_map/ppermute | solution.py:318
  26.1 7.7 %collective-permute-start.8 = (bf16[2,2,64,256]{3,2,1,0:T(8,128)(2,1)S(1)}, bf16[2,2,64,256]{3,2,1,0:T(8,128)(2,1)S(1)}, u32[]{:S(2)}, u32[]{:S(2)}) collective-permute-start(bf16[2,2,64,256]{3,2,1,0:T(8,128)(2,1)S(1)} %get-tuple-element.40), channel_id=1, source_target_pairs={{0,2},{1,3},{2,0},{3,1},{4,6},{5,7},{6,4},{7,5},{8,10},{9,11},{10,... | collective-permute-start | bytes 393224 | tf_op jit(solution)/shard_map/ppermute | solution.py:318
  33.9 1.8 %collective-permute-start.9 = (bf16[6,2,64,256]{3,2,1,0:T(8,128)(2,1)S(1)}, bf16[6,2,64,256]{3,2,1,0:T(8,128)(2,1)S(1)}, u32[]{:S(2)}, u32[]{:S(2)}) collective-permute-start(bf16[6,2,64,256]{3,2,1,0:T(8,128)(2,1)S(1)} %slice_dynamic-update-slice_fusion), channel_id=1, source_target_pairs={{0,1},{1,0},{2,3},{3,2},{4,5},{5,4},{6,7},{7,6},{8,9},{9,8},{10,11... | collective-permute-start | bytes 1179656 | tf_op jit(solution)/shard_map/ppermute | solution.py:318
  35.7 16.3 %copy-start.1 = (s32[64,512]{1,0:T(8,128)S(1)}, s32[64,512]{1,0:T(8,128)}, u32[]{:S(2)}) copy-start(s32[64,512]{1,0:T(8,128)} %delay_ref.1) | copy-start | bytes 393220
